TPU v7x, 256 devices: a whole 4x4x8 slice. The times are simulated.
256 devices in a mesh: expert: 16 (over z, y_hi), hrow: 8 (over x, core), hcol: 2 (over y_lo).
Axes of the slice: x: 4, y: 4 (y_hi: 2, y_lo: 2; y = y_hi * 2 + y_lo), z: 8, core: 2. Of those that a mesh axis runs over, the one named last changes fastest.
Arguments:
- tokens: bfloat16 [2048, 7168], P(('expert', 'hrow'), 'hcol')
- expert_ids: int32 [2048, 8], P(('expert', 'hrow')), may hold values from 0 to 127, all different within a row; in each aligned block of 16 rows (0 to 15, 16 to 31, ...) at most 2 rows name the same one
- weight: bfloat16 [128, 256, 7168], P(('expert', 'hrow'), None, 'hcol'), may hold values from -6 to 6
- mask_bits: int32 [256, 224], P(None, 'hcol'), may hold values from -2147483648 to 2147483646, as said below
- damping: float32 [128, 7168], P(('expert', 'hrow'), 'hcol'), may hold values from 0.5 to 2
Outputs:
- new_weight: bfloat16 [128, 256, 7168], P(('expert', 'hrow'), None, 'hcol')
Inputs may be any that keep to these rules, and one draw needn't show every extreme that they name: `expert_ids`: each token names 8 different experts; among the 16 rows of one device (aligned blocks of rows) no expert is named more than 2 times, a bound that some block reaches. `mask_bits`: every bit of every word is a keep flag (1 keeps the entry, 0 prunes it).
All inputs are finite; a program needn't handle non-finite values.
Results may differ from a plain program's by a relative error of at most 0.0044.
Values may be sent and summed in bfloat16 or wider, within the bound.
No kernel may reach another device: no remote copies, remote signals or barrier semaphores. Data moves between devices by JAX's collectives and lax.ppermute only.
A program may use at most 64 MiB of HBM per device.

v0:
```python
import jax
import jax.numpy as jnp
from jax import lax
from jax.sharding import PartitionSpec as P

ROWS_E = 128


ETA = 0.5


def unpack_bits(bits):
    bit_shifts = jnp.arange(32, dtype=jnp.int32)
    bit_flags = jnp.bitwise_and(jnp.right_shift(bits[:, :, None], bit_shifts[None, None, :]), 1)
    return bit_flags.reshape(bits.shape[0], bits.shape[1] * 32)


def route_rows(tokens, expert_ids, group_count, local_count):
    tok_count, top_count = expert_ids.shape
    expert_count = group_count * local_count
    capacity = 2 * tok_count * top_count // expert_count
    flat_ids = expert_ids.reshape(-1)
    one_hot = (flat_ids[:, None] == jnp.arange(expert_count, dtype=jnp.int32)[None, :]).astype(
        jnp.int32
    )
    prior_count = jnp.cumsum(one_hot, axis=0) - one_hot
    slot_index = jnp.sum(prior_count * one_hot, axis=1)
    group_of = flat_ids // local_count
    local_of = flat_ids % local_count
    target_slot = ((local_of * group_count + group_of) * capacity + slot_index).reshape(
        tok_count, top_count
    )
    slot_ids = jnp.arange(expert_count * capacity, dtype=jnp.int32)
    selector = jnp.any(slot_ids[:, None, None] == target_slot[None, :, :], axis=2).astype(
        jnp.bfloat16
    )
    packed = jnp.dot(selector, tokens, preferred_element_type=jnp.float32).astype(jnp.bfloat16)
    return packed.reshape(local_count, group_count, 1, capacity, tokens.shape[1])


def local(tokens, expert_ids, weight, mask_bits, damping):
    group_count = lax.axis_size(("expert", "hrow"))
    local_experts = weight.shape[0]
    feat_width = tokens.shape[1]
    slab_rows = weight.shape[1]
    packed = route_rows(tokens, expert_ids, group_count, local_experts)
    keep_flags = unpack_bits(mask_bits)
    keep_mask = keep_flags[None, :, :] == 1
    pruned = jnp.where(keep_mask, jnp.zeros_like(weight), weight)
    block = lax.all_to_all(packed, ("expert", "hrow"), split_axis=1, concat_axis=2, tiled=True)
    partials = jnp.einsum("esf,exgcf->exgcs", pruned, block, preferred_element_type=jnp.float32)
    slot_count = block.shape[1] * block.shape[2] * block.shape[3]
    routed = block.reshape(local_experts, slot_count, feat_width)
    partials = partials.reshape(local_experts, slot_count, slab_rows)
    projected = lax.psum(partials, "hcol").astype(jnp.bfloat16)
    comp_term = (
        jnp.einsum("ers,erf->esf", projected, routed, preferred_element_type=jnp.float32) / ROWS_E
    )
    diag_scale = (
        jnp.einsum("erf,erf->ef", routed, routed, preferred_element_type=jnp.float32) / ROWS_E
        + damping
    )
    updated = weight.astype(jnp.float32) + ETA * comp_term / diag_scale[:, None, :]
    return jnp.where(keep_mask, updated, jnp.float32(0.0)).astype(jnp.bfloat16)


def solution(mesh):
    in_specs = (
        P(("expert", "hrow"), "hcol"),
        P(("expert", "hrow"), None),
        P(("expert", "hrow"), None, "hcol"),
        P(None, "hcol"),
        P(("expert", "hrow"), "hcol"),
    )
    out_specs = P(("expert", "hrow"), None, "hcol")
    return jax.shard_map(local, mesh=mesh, in_specs=in_specs, out_specs=out_specs, check_vma=False)
```

profile of v0, /device:TPU:8, one launch (start us, length us, event | category | flops | bytes accessed | tf_op | source)
XLA Modules:
  0.0 87.6 jit_solution(13085517939095235751)
XLA Ops:
  0.0 0.0 copy-start
  0.0 0.8 copy.17
  0.8 0.1 eq.44
  0.9 0.1 fusion.16
  1.0 0.2 reduce_window_sum.11
  1.2 0.2 select_reduce_fusion
  1.3 0.1 reduce_sum.12
  1.4 0.1 fusion.15
  1.6 0.0 copy-done
  1.6 0.7 convolution_convert_fusion
  2.3 1.6 %reshape.94 = bf16[1,128,1,2,3584]{4,3,1,2,0:T(2,128)(2,1)} reshape(bf16[256,3584]{1,0:T(8,128)(2,1)S(1)} %convolution_convert_fusion) | data formatting | bytes 3670016 | tf_op jit(solution)/shard_map/reshape | solution.py:38
  3.9 15.0 %all-to-all-start = ((bf16[1,128,1,2,3584]{4,3,2,0,1:T(2,128)(2,1)}), bf16[1,128,1,2,3584]{4,3,2,0,1:T(2,128)(2,1)S(1)}, u32[]{:S(2)}, u32[]{:S(2)}) async-start(bf16[1,128,1,2,3584]{4,3,2,0,1:T(2,128)(2,1)} %bitcast.30), calls=%async_computation | async-start | bytes 3670016 | tf_op jit(solution)/shard_map/all_to_all | solution.py:50
  18.9 0.0 copy-done.2
  18.9 2.1 %shift_right_arithmetic.27 = s32[256,112,32]{0,2,1:T(8,128)} broadcast(s32[256,112]{0,1:T(8,128)S(1)} %copy-done.2), dimensions={0,1} | broadcast | bytes 3784704 | tf_op jit(solution)/shard_map/shift_right_arithmetic | solution.py:14
  21.0 5.2 %copy.16 = s32[1,256,3584]{2,1,0:T(8,128)} copy(s32[1,256,3584]{1,2,0:T(8,128)} %bitcast.29) | data formatting | bytes 7340032 | tf_op jit(solution)/shard_map/shift_right_arithmetic | solution.py:14
  26.2 0.1 shift_right_arithmetic.30
  26.3 2.8 %and_compare_fusion = pred[1,256,3584]{2,1,0:T(32,128)(4,1)S(1)} fusion(s32[1,256,3584]{2,1,0:T(8,128)} %copy.16, s32[3584]{0:T(1024)S(1)} %shift_right_arithmetic.30), kind=kLoop, calls=%fused_computation.9 | loop fusion | flops 2752512 | bytes 4601856 | tf_op jit(solution)/shard_map/eq | solution.py:48
  29.0 36.5 %all-to-all-done = bf16[1,128,1,2,3584]{4,3,2,0,1:T(2,128)(2,1)S(1)} async-done(((bf16[1,128,1,2,3584]{4,3,2,0,1:T(2,128)(2,1)}), bf16[1,128,1,2,3584]{4,3,2,0,1:T(2,128)(2,1)S(1)}, u32[]{:S(2)}, u32[]{:S(2)}) %all-to-all-start) | async-done | bytes 1835040 | tf_op jit(solution)/shard_map/all_to_all | solution.py:50
  65.5 1.6 %reshape.95 = bf16[256,3584]{1,0:T(8,128)(2,1)} reshape(bf16[1,128,1,2,3584]{4,3,2,0,1:T(2,128)(2,1)S(1)} %all-to-all-done) | data formatting | bytes 3670016 | tf_op jit(solution)/shard_map/reshape.40
  67.2 2.0 %fusion.5 = f32[3584]{0:T(1024)S(1)} fusion(bf16[256,3584]{1,0:T(8,128)(2,1)} %reshape.95), kind=kLoop, calls=%fused_computation.8 | loop fusion | flops 2748928 | bytes 1849344 | tf_op jit(solution)/shard_map/erf,erf->ef/dot_general | solution.py:60
  69.2 0.0 copy-done.1
  69.2 2.2 %fusion.9 = f32[1,256,256]{2,1,0:T(8,128)S(1)} fusion(bf16[256,3584]{1,0:T(8,128)(2,1)S(1)} %copy-done.1, pred[1,256,3584]{2,1,0:T(32,128)(4,1)S(1)} %and_compare_fusion, bf16[1,256,3584]{2,1,0:T(8,128)(2,1)} %param.7), kind=kOutput, calls=%fused_computation.13 | convolution fusion | flops 470679552 | bytes 4849664 | tf_op jit(solution)/shard_map/esf,exgcf->exgcs/dot_general | solution.py:51
  71.4 12.2 %all-reduce.1 = bf16[1,256,256]{2,1,0:T(8,128)(2,1)S(1)} all-reduce(f32[1,256,256]{2,1,0:T(8,128)S(1)} %fusion.9), channel_id=1, replica_groups=mesh['expert'=16,'hrow'=8,'hcol'=2] {'hcol'}, use_global_device_ids=true, to_apply=%region_3.4 | all-reduce | flops 65536 | bytes 393216 | tf_op jit(solution)/shard_map/psum | solution.py:55
  83.7 3.9 %fusion.4 = bf16[1,256,3584]{2,1,0:T(8,128)(2,1)} fusion(pred[1,256,3584]{2,1,0:T(32,128)(4,1)S(1)} %and_compare_fusion, bf16[256,3584]{1,0:T(8,128)(2,1)S(1)} %copy-done.1, bf16[1,256,3584]{2,1,0:T(8,128)(2,1)} %param.7, f32[3584]{0:T(1024)S(1)} %add_reduce_fusion, bf16[1,256,256]{2,1,0:T(8,128)(2,1)S(1)} %all-reduce.1), kind=kOutput, calls=%fused_computation.6 | convolution fusion | flops 475267072 | bytes 6567936 | tf_op jit(solution)/shard_map/ers,erf->esf/dot_general | solution.py:57
  (8 shorter events, 0.1 us)
Async XLA Ops:
  0.0 1.6 %copy-start = (bf16[16,3584]{1,0:T(8,128)(2,1)S(1)}, bf16[16,3584]{1,0:T(8,128)(2,1)}, u32[]{:S(2)}) copy-start(bf16[16,3584]{1,0:T(8,128)(2,1)} %param.5) | copy-start | bytes 344068
  3.9 15.0 %copy-start.2 = (s32[256,112]{0,1:T(8,128)S(1)}, s32[256,112]{0,1:T(8,128)}, u32[]{:S(2)}) copy-start(s32[256,112]{0,1:T(8,128)} %param.8) | copy-start | bytes 344068
  3.9 61.6 %all-to-all-start = ((bf16[1,128,1,2,3584]{4,3,2,0,1:T(2,128)(2,1)}), bf16[1,128,1,2,3584]{4,3,2,0,1:T(2,128)(2,1)S(1)}, u32[]{:S(2)}, u32[]{:S(2)}) async-start(bf16[1,128,1,2,3584]{4,3,2,0,1:T(2,128)(2,1)} %bitcast.30), calls=%async_computation | async-start | bytes 3670016 | tf_op jit(solution)/shard_map/all_to_all | solution.py:50
  67.2 2.1 %copy-start.1 = (bf16[256,3584]{1,0:T(8,128)(2,1)S(1)}, bf16[256,3584]{1,0:T(8,128)(2,1)}, u32[]{:S(2)}) copy-start(bf16[256,3584]{1,0:T(8,128)(2,1)} %reshape.95) | copy-start | bytes 5505028
  69.2 14.5 %copy-start.3 = (f32[1,3584]{1,0:T(1,128)S(1)}, f32[1,3584]{1,0:T(1,128)}, u32[]{:S(2)}) copy-start(f32[1,3584]{1,0:T(1,128)} %param.9) | copy-start | bytes 43012
where the time goes:
time: 88.3 us; the launch traced here: 87.6 us
  waiting for transfers between devices  36.5 us (41%)
  starting transfers between devices  15 us (17%)
  blocking collectives  12.2 us (14%)
  local copies, waits for them, and re-layouts  11.6 us (13%)
  matrix products  6.77 us (8%)
  other arithmetic  5.39 us (6%)
    all_to_all x1, waiting for transfers between devices, local(): lax.all_to_all(packed, ('expert', 'hrow'), split_axis=1, concat_axis=2, t...  36.5 us
    all_to_all x1, starting transfers between devices, local(): lax.all_to_all(packed, ('expert', 'hrow'), split_axis=1, concat_axis=2, t...  15 us
    psum x1, blocking collectives, local(): projected = lax.psum(partials, 'hcol').astype(jnp.bfloat16)  12.2 us
    shift_right_arithmetic x4, local copies, waits for them, and re-layouts, unpack_bits(): jnp.right_shift(bits[:, :, None], bit_shifts[None, None, :])  7.34 us
    dot_general x1, matrix products, local(): jnp.einsum('ers,erf->esf', projected, routed, preferred_element_type=jnp....  3.9 us
    eq x1, other arithmetic, local(): keep_mask = keep_flags[None, :, :] == 1  2.75 us
    dot_general x1, matrix products, local(): jnp.einsum('esf,exgcf->exgcs', pruned, block, preferred_element_type=jnp....  2.2 us
    dot_general x1, other arithmetic, local(): jnp.einsum('erf,erf->ef', routed, routed, preferred_element_type=jnp.floa...  2.01 us
  transfers between devices with their start and end apart: 1, of which 1 were waited for; matrix products, arithmetic and copies ran while one was open for 12% of the time, Pallas kernels for 0%

commit v1 on v0

v1 whole, which is shorter than its diff:
```python
import functools

import jax
import jax.numpy as jnp
from jax import lax
from jax.experimental import pallas as pl
from jax.experimental.pallas import tpu as pltpu
from jax.sharding import Mesh, PartitionSpec as P

ROWS_E = 128
ETA = 0.5
CAP = 2
LANES = 128
F32 = jnp.float32
BF16 = jnp.bfloat16


def call(body, out_shape, operands, flops, scratch=(), name=None):
    size = sum(o.size * o.dtype.itemsize for o in operands)
    outs = jax.tree.leaves(out_shape)
    size += sum(o.size * o.dtype.itemsize for o in outs)
    return pl.pallas_call(
        body,
        out_shape=out_shape,
        in_specs=[pl.BlockSpec(memory_space=pltpu.VMEM)] * len(operands),
        out_specs=jax.tree.map(lambda _: pl.BlockSpec(memory_space=pltpu.VMEM), out_shape),
        scratch_shapes=list(scratch),
        cost_estimate=pl.CostEstimate(flops=flops, bytes_accessed=size, transcendentals=0),
        compiler_params=pltpu.CompilerParams(vmem_limit_bytes=40 * 2**20),
        name=name,
    )(*operands)


def tag_body(tokens_ref, ids_ref, out_ref):
    rows, feats = tokens_ref.shape
    top = ids_ref.shape[0]
    out_ref[:, :feats] = tokens_ref[...]
    spread = (
        lax.broadcasted_iota(jnp.int32, (top, LANES), 0)
        == lax.broadcasted_iota(jnp.int32, (top, LANES), 1)
    ).astype(BF16)
    ids = ids_ref[...].astype(F32).astype(BF16)
    out_ref[:, feats:] = lax.dot_general(
        ids, spread, (((0,), (0,)), ((), ())), preferred_element_type=F32
    ).astype(BF16)


def pack_body(tok_rows, top, first_ref, *refs):
    *block_refs, out_ref, held = refs
    feats = out_ref.shape[-1]
    at = 0
    for ref in block_refs:
        held[at : at + ref.shape[0], :] = ref[...]
        at += ref.shape[0]
    tokens = at
    dests, per_dest = out_ref.shape[0], out_ref.shape[1]
    rows = dests * per_dest
    pick = (
        lax.broadcasted_iota(jnp.int32, (top, LANES), 0)
        == lax.broadcasted_iota(jnp.int32, (top, LANES), 1)
    ).astype(BF16)
    ids = lax.dot_general(
        pick, held[:, feats:], (((1,), (1,)), ((), ())), preferred_element_type=F32
    )
    row = lax.broadcasted_iota(jnp.int32, (rows, 1), 0)
    expert = (first_ref[0] + 2 * (row // per_dest)).astype(F32)
    block = (row % per_dest) // CAP
    slot = (row % CAP).astype(F32)
    tok = lax.broadcasted_iota(jnp.int32, (1, tokens), 1)
    named = ids[0:1, :] == expert
    for k in range(1, top):
        named = named | (ids[k : k + 1, :] == expert)
    named = named & (tok // tok_rows == block)
    member = jnp.where(named, 1.0, 0.0)
    before = (
        lax.broadcasted_iota(jnp.int32, (tokens, tokens), 0)
        < lax.broadcasted_iota(jnp.int32, (tokens, tokens), 1)
    ).astype(BF16)
    rank = jnp.dot(member.astype(BF16), before, preferred_element_type=F32)
    select = jnp.where(rank == slot, member, 0.0).astype(BF16)
    width = 512
    for lo in range(0, feats, width):
        out_ref[:, :, lo : lo + width] = (
            jnp.dot(select, held[:, lo : lo + width], preferred_element_type=F32)
            .astype(BF16)
            .reshape(dests, per_dest, width)
        )


def prune_body(weight_ref, bits_ref, pruned_ref, keep_ref):
    rows, words = bits_ref.shape
    feats = weight_ref.shape[1]
    lane = lax.broadcasted_iota(jnp.int32, (rows, LANES), 1)
    bits = jnp.concatenate([bits_ref[...], jnp.zeros((rows, LANES - words), jnp.int32)], axis=1)
    for j in range(feats // LANES):
        word = jnp.take_along_axis(bits, lane // 32 + 4 * j, axis=1, mode="promise_in_bounds")
        keep = jnp.bitwise_and(jnp.right_shift(word, lane % 32), 1).astype(F32)
        cols = slice(j * LANES, (j + 1) * LANES)
        slab = weight_ref[:, cols].astype(F32)
        pruned_ref[:, cols] = jnp.where(keep > 0.5, 0.0, slab).astype(BF16)
        keep_ref[:, cols] = keep.astype(BF16)


def project_body(routed_ref, pruned_ref, part_ref, low_ref):
    part = lax.dot_general(
        routed_ref[...], pruned_ref[...], (((1,), (1,)), ((), ())), preferred_element_type=F32
    )
    part_ref[...] = part
    low_ref[...] = part.astype(BF16)


def scale_body(routed_ref, damping_ref, scale_ref):
    feats = routed_ref.shape[1]
    width = 512
    for lo in range(0, feats, width):
        cols = slice(lo, lo + width)
        rows = routed_ref[:, cols].astype(F32)
        diag = jnp.sum(rows * rows, axis=0, keepdims=True) * (1.0 / ROWS_E) + damping_ref[:, cols]
        scale_ref[:, cols] = (ETA / ROWS_E) / diag


def update_body(part_ref, other_ref, routed_ref, scale_ref, weight_ref, keep_ref, out_ref):
    feats = routed_ref.shape[1]
    projected = (part_ref[...] + other_ref[...].astype(F32)).astype(BF16)
    width = 512
    for lo in range(0, feats, width):
        cols = slice(lo, lo + width)
        comp = lax.dot_general(
            projected, routed_ref[:, cols], (((0,), (0,)), ((), ())), preferred_element_type=F32
        )
        updated = weight_ref[:, cols].astype(F32) + comp * scale_ref[:, cols]
        out_ref[:, cols] = jnp.where(keep_ref[:, cols].astype(F32) > 0.5, updated, 0.0).astype(BF16)


def shape(*dims, dtype=BF16):
    return jax.ShapeDtypeStruct(dims, dtype)


def shift(x, axis, step):
    n = lax.axis_size(axis)
    return lax.ppermute(x, axis, [(i, (i + step) % n) for i in range(n)])


def local(tokens, expert_ids, weight, mask_bits, damping):
    tok_rows, feats = tokens.shape
    top = expert_ids.shape[1]
    slab = weight.shape[1]
    weight = weight.reshape(slab, feats)
    me_z, me_core = lax.axis_index("z"), lax.axis_index("core")
    plane = lax.axis_size("yh") * lax.axis_size("x")
    first = (me_z * plane * 2 + me_core).astype(jnp.int32).reshape(1)

    with jax.named_scope("tag"):
        own = call(tag_body, shape(tok_rows, feats + LANES), (tokens, expert_ids.T), 1 << 16)
    with jax.named_scope("gather_z"):
        m1, p1 = shift(own, "z", 1), shift(own, "z", -1)
        m2, p2 = shift(m1, "z", 1), shift(p1, "z", -1)
        m3, p3 = shift(m1, "z", 2), shift(p1, "z", -2)
        far = shift(m3, "z", 1)
    groups = ((own, m1, p1), (m2, p2, m3, p3), (far,))
    with jax.named_scope("swap_core"):
        swapped = tuple(shift(jnp.concatenate(g), "core", 1) for g in groups)
    blocks = tuple(b for g in groups for b in g) + swapped
    n_tok = sum(b.shape[0] for b in blocks)
    per_dest = n_tok // tok_rows * CAP
    with jax.named_scope("pack"):
        packed = pl.pallas_call(
            functools.partial(pack_body, tok_rows, top),
            out_shape=shape(plane, per_dest, feats),
            in_specs=[pl.BlockSpec(memory_space=pltpu.SMEM)]
            + [pl.BlockSpec(memory_space=pltpu.VMEM)] * len(blocks),
            out_specs=pl.BlockSpec(memory_space=pltpu.VMEM),
            scratch_shapes=[pltpu.VMEM((n_tok, feats + LANES), BF16)],
            cost_estimate=pl.CostEstimate(
                flops=2 * plane * per_dest * n_tok * feats, bytes_accessed=4 << 20, transcendentals=0
            ),
            compiler_params=pltpu.CompilerParams(vmem_limit_bytes=40 * 2**20),
        )(first, *blocks)
    with jax.named_scope("prune"):
        pruned, keep = call(
            prune_body, (shape(slab, feats), shape(slab, feats)), (weight, mask_bits), 1 << 22
        )
    with jax.named_scope("route"):
        block = lax.all_to_all(packed, ("yh", "x"), split_axis=0, concat_axis=0, tiled=True)
    routed = block.reshape(plane * per_dest, feats)
    rows = routed.shape[0]
    with jax.named_scope("project"):
        part, low = call(
            project_body,
            (shape(rows, slab, dtype=F32), shape(rows, slab)),
            (routed, pruned),
            2 * rows * slab * feats,
        )
    with jax.named_scope("swap_features"):
        other = shift(low, "yl", 1)
    with jax.named_scope("scale"):
        scale = call(scale_body, shape(1, feats, dtype=F32), (routed, damping), 2 * rows * feats)
    with jax.named_scope("update"):
        out = call(
            update_body,
            shape(slab, feats),
            (part, other, routed, scale, weight, keep),
            2 * rows * slab * feats,
        )
    return out.reshape(1, slab, feats)


def solution(mesh):
    n_hrow, n_hcol = mesh.shape["hrow"], mesh.shape["hcol"]
    n_expert = mesh.shape["expert"]
    fine = Mesh(
        mesh.devices.reshape(n_expert // 2, 2, n_hrow // 2, 2, n_hcol),
        ("z", "yh", "x", "core", "yl"),
    )
    own = ("z", "yh", "x", "core")
    in_specs = (P(own, "yl"), P(own, None), P(own, None, "yl"), P(None, "yl"), P(own, "yl"))
    return jax.shard_map(
        local, mesh=fine, in_specs=in_specs, out_specs=P(own, None, "yl"), check_vma=False
    )
```

time: 88.3 us -> 78 us (0.88)
  blocking collectives: 12.2 us -> 0 us
  matrix products: 6.77 us -> 0 us
  waiting for transfers between devices: 36.5 us -> 42.7 us
  Pallas kernels: 0 us -> 5.46 us
  starting transfers between devices: 15 us -> 20.3 us
  other arithmetic: 5.39 us -> 0.09 us
  local copies, waits for them, and re-layouts: 11.6 us -> 8.39 us
    ppermute x0 -> x11, waiting for transfers between devices: none -> 21.9 us  [shift(): return lax.ppermute(x, axis, [(i, (i + step) % n) for i in range(n)])]
    all_to_all x1, waiting for transfers between devices: 36.5 us -> 20.7 us  [local(): lax.all_to_all(packed, ('yh', 'x'), split_axis=0, concat_axis=0, tiled=True)]
    ppermute x0 -> x11, starting transfers between devices: none -> 14.1 us  [shift(): return lax.ppermute(x, axis, [(i, (i + step) % n) for i in range(n)])]
    psum x1 -> x0, blocking collectives: 12.2 us -> none  [local(): projected = lax.psum(partials, 'hcol').astype(jnp.bfloat16)]
    all_to_all x1, starting transfers between devices: 15 us -> 6.16 us  [local(): lax.all_to_all(packed, ('yh', 'x'), split_axis=0, concat_axis=0, tiled=True)]
    unnamed x9 -> x23, local copies, waits for them, and re-layouts: 0.82 us -> 8.39 us
    shift_right_arithmetic x4 -> x0, local copies, waits for them, and re-layouts: 7.34 us -> none  [unpack_bits(): jnp.right_shift(bits[:, :, None], bit_shifts[None, None, :])]
    dot_general x3 -> x0, matrix products: 6.77 us -> none  [the longest x1 3.9 us: local(): jnp.einsum('ers,erf->esf', projected, routed, preferred_element_type=jnp....]
  transfers between devices with their start and end apart: 1 -> 12, of which waited for: 1 -> 7; matrix products, arithmetic and copies ran while one was open for 12% -> 0% of each run, Pallas kernels for 0% -> 2%
where the time goes in v1:
time: 78 us; the launch traced here: 77 us
  waiting for transfers between devices  42.7 us (55%)
  starting transfers between devices  20.3 us (26%)
  local copies, waits for them, and re-layouts  8.39 us (11%)
  Pallas kernels  5.46 us (7%)
    ppermute x11, waiting for transfers between devices, shift(): return lax.ppermute(x, axis, [(i, (i + step) % n) for i in range(n)])  21.9 us
    all_to_all x1, waiting for transfers between devices, local(): lax.all_to_all(packed, ('yh', 'x'), split_axis=0, concat_axis=0, tiled=True)  20.7 us
    ppermute x11, starting transfers between devices, shift(): return lax.ppermute(x, axis, [(i, (i + step) % n) for i in range(n)])  14.1 us
    unnamed x23, local copies, waits for them, and re-layouts  8.39 us
    all_to_all x1, starting transfers between devices, local(): lax.all_to_all(packed, ('yh', 'x'), split_axis=0, concat_axis=0, tiled=True)  6.16 us
    pallas_call x5, Pallas kernels, call(): pl.pallas_call(body, out_shape=out_shape, in_specs=[pl.BlockSpec(memory_s...  4.34 us
  transfers between devices with their start and end apart: 12, of which 7 were waited for; matrix products, arithmetic and copies ran while one was open for 0% of the time, Pallas kernels for 2%

profile of v1, /device:TPU:8, one launch (start us, length us, event | category | flops | bytes accessed | tf_op | source)
XLA Modules:
  0.0 77.0 jit_solution(12568645699846610347)
XLA Ops:
  0.0 0.9 %copy-done.7 = bf16[16,3584]{1,0:T(8,128)(2,1)S(1)} copy-done((bf16[16,3584]{1,0:T(8,128)(2,1)S(1)}, bf16[16,3584]{1,0:T(8,128)(2,1)}, u32[]{:S(2)}) %copy-start.7) | copy-done | bytes 114712
  0.9 0.7 copy-done.9
  1.8 1.9 %collective-permute-start = (bf16[16,3712]{1,0:T(8,128)(2,1)S(1)}, bf16[16,3712]{1,0:T(8,128)(2,1)S(1)}, u32[]{:S(2)}, u32[]{:S(2)}) collective-permute-start(bf16[16,3712]{1,0:T(8,128)(2,1)S(1)} %tag.1.refs_0_), channel_id=1, source_target_pairs={{0,32},{32,64},{64,96},{96,128},{128,160},{160,192},{192,224},{224... | collective-permute-start | bytes 356360 | tf_op jit(solution)/shard_map/gather_z/ppermute | solution.py:141
  3.7 3.9 %collective-permute-start.1 = (bf16[16,3712]{1,0:T(8,128)(2,1)S(1)}, bf16[16,3712]{1,0:T(8,128)(2,1)S(1)}, u32[]{:S(2)}, u32[]{:S(2)}) collective-permute-start(bf16[16,3712]{1,0:T(8,128)(2,1)S(1)} %tag.1.refs_0_), channel_id=1, source_target_pairs={{0,224},{32,0},{64,32},{96,64},{128,96},{160,128},{192,160},{224,1... | collective-permute-start | bytes 356360 | tf_op jit(solution)/shard_map/gather_z/ppermute | solution.py:141
  7.6 3.2 %collective-permute-done.refs_1_ = bf16[16,3712]{1,0:T(8,128)(2,1)S(1)} collective-permute-done((bf16[16,3712]{1,0:T(8,128)(2,1)S(1)}, bf16[16,3712]{1,0:T(8,128)(2,1)S(1)}, u32[]{:S(2)}, u32[]{:S(2)}) %collective-permute-start) | collective-permute-done | bytes 118816 | tf_op jit(solution)/shard_map/gather_z/ppermute | solution.py:141
  10.9 1.7 %collective-permute-start.2 = (bf16[16,3712]{1,0:T(8,128)(2,1)S(1)}, bf16[16,3712]{1,0:T(8,128)(2,1)S(1)}, u32[]{:S(2)}, u32[]{:S(2)}) collective-permute-start(bf16[16,3712]{1,0:T(8,128)(2,1)S(1)} %collective-permute-done.refs_1_), channel_id=1, source_target_pairs={{0,32},{32,64},{64,96},{96,128},{128,160},{160,192},{192,224},{224... | collective-permute-start | bytes 356360 | tf_op jit(solution)/shard_map/gather_z/ppermute | solution.py:141
  12.6 1.5 %collective-permute-start.3 = (bf16[16,3712]{1,0:T(8,128)(2,1)S(1)}, bf16[16,3712]{1,0:T(8,128)(2,1)S(1)}, u32[]{:S(2)}, u32[]{:S(2)}) collective-permute-start(bf16[16,3712]{1,0:T(8,128)(2,1)S(1)} %collective-permute-done.1.refs_2_), channel_id=1, source_target_pairs={{0,224},{32,0},{64,32},{96,64},{128,96},{160,128},{192,160},{224,1... | collective-permute-start | bytes 356360 | tf_op jit(solution)/shard_map/gather_z/ppermute | solution.py:141
  14.1 2.9 %collective-permute-start.5 = (bf16[16,3712]{1,0:T(8,128)(2,1)S(1)}, bf16[16,3712]{1,0:T(8,128)(2,1)S(1)}, u32[]{:S(2)}, u32[]{:S(2)}) collective-permute-start(bf16[16,3712]{1,0:T(8,128)(2,1)S(1)} %collective-permute-done.1.refs_2_), channel_id=1, source_target_pairs={{0,192},{32,224},{64,0},{96,32},{128,64},{160,96},{192,128},{224,1... | collective-permute-start | bytes 356360 | tf_op jit(solution)/shard_map/gather_z/ppermute | solution.py:141
  17.0 3.9 %collective-permute-done.4.refs_5_ = bf16[16,3712]{1,0:T(8,128)(2,1)S(1)} collective-permute-done((bf16[16,3712]{1,0:T(8,128)(2,1)S(1)}, bf16[16,3712]{1,0:T(8,128)(2,1)S(1)}, u32[]{:S(2)}, u32[]{:S(2)}) %collective-permute-start.4) | collective-permute-done | bytes 118816 | tf_op jit(solution)/shard_map/gather_z/ppermute | solution.py:141
  20.9 3.4 %collective-permute-done.5.refs_6_ = bf16[16,3712]{1,0:T(8,128)(2,1)S(1)} collective-permute-done((bf16[16,3712]{1,0:T(8,128)(2,1)S(1)}, bf16[16,3712]{1,0:T(8,128)(2,1)S(1)}, u32[]{:S(2)}, u32[]{:S(2)}) %collective-permute-start.5) | collective-permute-done | bytes 118816 | tf_op jit(solution)/shard_map/gather_z/ppermute | solution.py:141
  25.1 6.4 %collective-permute-done.6.refs_7_ = bf16[16,3712]{1,0:T(8,128)(2,1)S(1)} collective-permute-done((bf16[16,3712]{1,0:T(8,128)(2,1)S(1)}, bf16[16,3712]{1,0:T(8,128)(2,1)S(1)}, u32[]{:S(2)}, u32[]{:S(2)}) %collective-permute-start.6) | collective-permute-done | bytes 118816 | tf_op jit(solution)/shard_map/gather_z/ppermute | solution.py:141
  31.6 1.3 %collective-permute-done.9.refs_10_ = bf16[16,3712]{1,0:T(8,128)(2,1)S(1)} collective-permute-done((bf16[16,3712]{1,0:T(8,128)(2,1)S(1)}, bf16[16,3712]{1,0:T(8,128)(2,1)S(1)}, u32[]{:S(2)}, u32[]{:S(2)}) %collective-permute-start.9) | collective-permute-done | bytes 118816 | tf_op jit(solution)/shard_map/swap_core/ppermute | solution.py:141
  32.9 1.1 %pack.1 = bf16[8,32,3584]{2,1,0:T(8,128)(2,1)S(1)} custom-call(s32[1]{0:T(128)} %bitcast.first_ref, bf16[16,3712]{1,0:T(8,128)(2,1)S(1)} %tag.1.refs_0_, bf16[16,3712]{1,0:T(8,128)(2,1)S(1)} %collective-permute-done.refs_1_, bf16[16,3712]{1,0:T(8,128)(2,1)S(1)} %collective-permute-done.1.refs_2_, bf16[16,3712]{1,0:T(8,128)(2,1)S(1)} %collective-permute-done.2.refs_3_, ...), custom_call_target="tpu_custom_call" | custom-call | flops 469762048 | bytes 4194304 | tf_op jit(solution)/shard_map/pack/pallas_call | solution.py:167
  34.0 1.2 %copy-done = bf16[8,32,3584]{2,1,0:T(8,128)(2,1)} copy-done((bf16[8,32,3584]{2,1,0:T(8,128)(2,1)}, bf16[8,32,3584]{2,1,0:T(8,128)(2,1)S(1)}, u32[]{:S(2)}) %copy-start) | copy-done | bytes 1835032
  35.2 6.2 %all-to-all-start = ((bf16[8,32,3584]{2,1,0:T(8,128)(2,1)}), bf16[8,32,3584]{2,1,0:T(8,128)(2,1)S(1)}, u32[]{:S(2)}, u32[]{:S(2)}) async-start(bf16[8,32,3584]{2,1,0:T(8,128)(2,1)} %copy-done), calls=%async_computation | async-start | bytes 3670016 | tf_op jit(solution)/shard_map/route/all_to_all | solution.py:184
  41.5 1.5 %copy-done.1 = bf16[1,256,3584]{2,1,0:T(8,128)(2,1)S(1)} copy-done((bf16[1,256,3584]{2,1,0:T(8,128)(2,1)S(1)}, bf16[1,256,3584]{2,1,0:T(8,128)(2,1)}, u32[]{:S(2)}) %copy-start.1) | copy-done | bytes 1835032
  43.0 1.1 %prune.1 = (bf16[256,3584]{1,0:T(8,128)(2,1)S(1)}, bf16[256,3584]{1,0:T(8,128)(2,1)S(1)}) custom-call(bf16[256,3584]{1,0:T(8,128)(2,1)S(1)} %bitcast.8, s32[256,112]{1,0:T(8,128)S(1)} %copy.6.bits_ref), custom_call_target="tpu_custom_call" | custom-call | flops 4194304 | bytes 5619712 | tf_op jit(solution)/shard_map/prune/pallas_call | solution.py:22
  44.1 1.3 %copy-done.3 = bf16[256,3584]{1,0:T(8,128)(2,1)} copy-done((bf16[256,3584]{1,0:T(8,128)(2,1)}, bf16[256,3584]{1,0:T(8,128)(2,1)S(1)}, u32[]{:S(2)}) %copy-start.3) | copy-done | bytes 1835032
  45.4 1.2 %copy-done.5 = bf16[256,3584]{1,0:T(8,128)(2,1)} copy-done((bf16[256,3584]{1,0:T(8,128)(2,1)}, bf16[256,3584]{1,0:T(8,128)(2,1)S(1)}, u32[]{:S(2)}) %copy-start.5) | copy-done | bytes 1835032
  46.6 20.7 %all-to-all-done = bf16[8,32,3584]{2,1,0:T(8,128)(2,1)S(1)} async-done(((bf16[8,32,3584]{2,1,0:T(8,128)(2,1)}), bf16[8,32,3584]{2,1,0:T(8,128)(2,1)S(1)}, u32[]{:S(2)}, u32[]{:S(2)}) %all-to-all-start) | async-done | bytes 1835040 | tf_op jit(solution)/shard_map/route/all_to_all | solution.py:184
  67.3 1.5 %copy-done.4 = bf16[256,3584]{1,0:T(8,128)(2,1)S(1)} copy-done((bf16[256,3584]{1,0:T(8,128)(2,1)S(1)}, bf16[256,3584]{1,0:T(8,128)(2,1)}, u32[]{:S(2)}) %copy-start.4) | copy-done | bytes 1835032
  69.5 1.4 %collective-permute-start.10 = (bf16[256,256]{1,0:T(8,128)(2,1)S(1)}, bf16[256,256]{1,0:T(8,128)(2,1)S(1)}, u32[]{:S(2)}, u32[]{:S(2)}) collective-permute-start(bf16[256,256]{1,0:T(8,128)(2,1)S(1)} %get-tuple-element.11), channel_id=1, source_target_pairs={{0,1},{1,0},{2,3},{3,2},{4,5},{5,4},{6,7},{7,6},{8,9},{9,8},{10,11... | collective-permute-start | bytes 393224 | tf_op jit(solution)/shard_map/swap_features/ppermute | solution.py:141
  71.1 3.6 %collective-permute-done.10.other_ref = bf16[256,256]{1,0:T(8,128)(2,1)S(1)} collective-permute-done((bf16[256,256]{1,0:T(8,128)(2,1)S(1)}, bf16[256,256]{1,0:T(8,128)(2,1)S(1)}, u32[]{:S(2)}, u32[]{:S(2)}) %collective-permute-start.10) | collective-permute-done | bytes 131104 | tf_op jit(solution)/shard_map/swap_features/ppermute | solution.py:141
  74.7 2.3 %update.1 = bf16[256,3584]{1,0:T(8,128)(2,1)} custom-call(f32[256,256]{1,0:T(8,128)S(1)} %get-tuple-element.10.part_ref, bf16[256,256]{1,0:T(8,128)(2,1)S(1)} %collective-permute-done.10.other_ref, bf16[256,3584]{1,0:T(8,128)(2,1)S(1)} %bitcast.7, f32[1,3584]{1,0:T(1,128)S(1)} %scale.1.scale_ref, bf16[256,3584]{1,0:T(8,128)(2,1)S(1)} %bitcast.9, ...), custom_call_target="tpu_custom_call" | custom-call | flops 469762048 | bytes 7747584 | tf_op jit(solution)/shard_map/update/pallas_call | solution.py:22
  (31 shorter events, 1.9 us)
Async XLA Ops:
  0.0 0.9 %copy-start.7 = (bf16[16,3584]{1,0:T(8,128)(2,1)S(1)}, bf16[16,3584]{1,0:T(8,128)(2,1)}, u32[]{:S(2)}) copy-start(bf16[16,3584]{1,0:T(8,128)(2,1)} %tokens_ref.1) | copy-start | bytes 344068
  0.9 0.7 copy-start.9
  1.8 9.1 %collective-permute-start = (bf16[16,3712]{1,0:T(8,128)(2,1)S(1)}, bf16[16,3712]{1,0:T(8,128)(2,1)S(1)}, u32[]{:S(2)}, u32[]{:S(2)}) collective-permute-start(bf16[16,3712]{1,0:T(8,128)(2,1)S(1)} %tag.1.refs_0_), channel_id=1, source_target_pairs={{0,32},{32,64},{64,96},{96,128},{128,160},{160,192},{192,224},{224... | collective-permute-start | bytes 356360 | tf_op jit(solution)/shard_map/gather_z/ppermute | solution.py:141
  3.7 8.9 %collective-permute-start.1 = (bf16[16,3712]{1,0:T(8,128)(2,1)S(1)}, bf16[16,3712]{1,0:T(8,128)(2,1)S(1)}, u32[]{:S(2)}, u32[]{:S(2)}) collective-permute-start(bf16[16,3712]{1,0:T(8,128)(2,1)S(1)} %tag.1.refs_0_), channel_id=1, source_target_pairs={{0,224},{32,0},{64,32},{96,64},{128,96},{160,128},{192,160},{224,1... | collective-permute-start | bytes 356360 | tf_op jit(solution)/shard_map/gather_z/ppermute | solution.py:141
  10.8 10.0 %collective-permute-start.4 = (bf16[16,3712]{1,0:T(8,128)(2,1)S(1)}, bf16[16,3712]{1,0:T(8,128)(2,1)S(1)}, u32[]{:S(2)}, u32[]{:S(2)}) collective-permute-start(bf16[16,3712]{1,0:T(8,128)(2,1)S(1)} %collective-permute-done.refs_1_), channel_id=1, source_target_pairs={{0,64},{32,96},{64,128},{96,160},{128,192},{160,224},{192,0},{224,... | collective-permute-start | bytes 356360 | tf_op jit(solution)/shard_map/gather_z/ppermute | solution.py:141
  10.9 10.0 %collective-permute-start.2 = (bf16[16,3712]{1,0:T(8,128)(2,1)S(1)}, bf16[16,3712]{1,0:T(8,128)(2,1)S(1)}, u32[]{:S(2)}, u32[]{:S(2)}) collective-permute-start(bf16[16,3712]{1,0:T(8,128)(2,1)S(1)} %collective-permute-done.refs_1_), channel_id=1, source_target_pairs={{0,32},{32,64},{64,96},{96,128},{128,160},{160,192},{192,224},{224... | collective-permute-start | bytes 356360 | tf_op jit(solution)/shard_map/gather_z/ppermute | solution.py:141
  12.6 8.3 %collective-permute-start.3 = (bf16[16,3712]{1,0:T(8,128)(2,1)S(1)}, bf16[16,3712]{1,0:T(8,128)(2,1)S(1)}, u32[]{:S(2)}, u32[]{:S(2)}) collective-permute-start(bf16[16,3712]{1,0:T(8,128)(2,1)S(1)} %collective-permute-done.1.refs_2_), channel_id=1, source_target_pairs={{0,224},{32,0},{64,32},{96,64},{128,96},{160,128},{192,160},{224,1... | collective-permute-start | bytes 356360 | tf_op jit(solution)/shard_map/gather_z/ppermute | solution.py:141
  14.1 10.2 %collective-permute-start.5 = (bf16[16,3712]{1,0:T(8,128)(2,1)S(1)}, bf16[16,3712]{1,0:T(8,128)(2,1)S(1)}, u32[]{:S(2)}, u32[]{:S(2)}) collective-permute-start(bf16[16,3712]{1,0:T(8,128)(2,1)S(1)} %collective-permute-done.1.refs_2_), channel_id=1, source_target_pairs={{0,192},{32,224},{64,0},{96,32},{128,64},{160,96},{192,128},{224,1... | collective-permute-start | bytes 356360 | tf_op jit(solution)/shard_map/gather_z/ppermute | solution.py:141
  24.4 8.5 %collective-permute-start.8 = (bf16[64,3712]{1,0:T(8,128)(2,1)S(1)}, bf16[64,3712]{1,0:T(8,128)(2,1)S(1)}, u32[]{:S(2)}, u32[]{:S(2)}) collective-permute-start(bf16[64,3712]{1,0:T(8,128)(2,1)S(1)} %pad_maximum_fusion), channel_id=1, source_target_pairs={{0,2},{2,0},{1,3},{3,1},{4,6},{6,4},{5,7},{7,5},{8,10},{10,8},{9,1... | collective-permute-start | bytes 1425416 | tf_op jit(solution)/shard_map/swap_core/ppermute | solution.py:141
  24.5 7.0 %collective-permute-start.7 = (bf16[48,3712]{1,0:T(8,128)(2,1)S(1)}, bf16[48,3712]{1,0:T(8,128)(2,1)S(1)}, u32[]{:S(2)}, u32[]{:S(2)}) collective-permute-start(bf16[48,3712]{1,0:T(8,128)(2,1)S(1)} %pad_maximum_fusion.1), channel_id=1, source_target_pairs={{0,2},{2,0},{1,3},{3,1},{4,6},{6,4},{5,7},{7,5},{8,10},{10,8},{9,1... | collective-permute-start | bytes 1069064 | tf_op jit(solution)/shard_map/swap_core/ppermute | solution.py:141
  25.1 6.4 %collective-permute-start.6 = (bf16[16,3712]{1,0:T(8,128)(2,1)S(1)}, bf16[16,3712]{1,0:T(8,128)(2,1)S(1)}, u32[]{:S(2)}, u32[]{:S(2)}) collective-permute-start(bf16[16,3712]{1,0:T(8,128)(2,1)S(1)} %collective-permute-done.4.refs_5_), channel_id=1, source_target_pairs={{0,32},{32,64},{64,96},{96,128},{128,160},{160,192},{192,224},{224... | collective-permute-start | bytes 356360 | tf_op jit(solution)/shard_map/gather_z/ppermute | solution.py:141
  31.5 1.3 %collective-permute-start.9 = (bf16[16,3712]{1,0:T(8,128)(2,1)S(1)}, bf16[16,3712]{1,0:T(8,128)(2,1)S(1)}, u32[]{:S(2)}, u32[]{:S(2)}) collective-permute-start(bf16[16,3712]{1,0:T(8,128)(2,1)S(1)} %collective-permute-done.6.refs_7_), channel_id=1, source_target_pairs={{0,2},{2,0},{1,3},{3,1},{4,6},{6,4},{5,7},{7,5},{8,10},{10,8},{9,1... | collective-permute-start | bytes 356360 | tf_op jit(solution)/shard_map/swap_core/ppermute | solution.py:141
  34.0 1.2 %copy-start = (bf16[8,32,3584]{2,1,0:T(8,128)(2,1)}, bf16[8,32,3584]{2,1,0:T(8,128)(2,1)S(1)}, u32[]{:S(2)}) copy-start(bf16[8,32,3584]{2,1,0:T(8,128)(2,1)S(1)} %pack.1) | copy-start | bytes 5505028
  35.2 6.2 %copy-start.10 = (s32[256,112]{0,1:T(8,128)S(1)}, s32[256,112]{0,1:T(8,128)}, u32[]{:S(2)}) copy-start(s32[256,112]{0,1:T(8,128)} %param.8) | copy-start | bytes 344068
  35.2 32.1 %all-to-all-start = ((bf16[8,32,3584]{2,1,0:T(8,128)(2,1)}), bf16[8,32,3584]{2,1,0:T(8,128)(2,1)S(1)}, u32[]{:S(2)}, u32[]{:S(2)}) async-start(bf16[8,32,3584]{2,1,0:T(8,128)(2,1)} %copy-done), calls=%async_computation | async-start | bytes 3670016 | tf_op jit(solution)/shard_map/route/all_to_all | solution.py:184
  41.5 1.5 %copy-start.1 = (bf16[1,256,3584]{2,1,0:T(8,128)(2,1)S(1)}, bf16[1,256,3584]{2,1,0:T(8,128)(2,1)}, u32[]{:S(2)}) copy-start(bf16[1,256,3584]{2,1,0:T(8,128)(2,1)} %param.7) | copy-start | bytes 5505028
  44.1 1.3 %copy-start.3 = (bf16[256,3584]{1,0:T(8,128)(2,1)}, bf16[256,3584]{1,0:T(8,128)(2,1)S(1)}, u32[]{:S(2)}) copy-start(bf16[256,3584]{1,0:T(8,128)(2,1)S(1)} %get-tuple-element.9.pruned_ref) | copy-start | bytes 5505028
  45.4 1.2 %copy-start.5 = (bf16[256,3584]{1,0:T(8,128)(2,1)}, bf16[256,3584]{1,0:T(8,128)(2,1)S(1)}, u32[]{:S(2)}) copy-start(bf16[256,3584]{1,0:T(8,128)(2,1)S(1)} %get-tuple-element.12.keep_ref) | copy-start | bytes 5505028
  67.3 1.5 %copy-start.4 = (bf16[256,3584]{1,0:T(8,128)(2,1)S(1)}, bf16[256,3584]{1,0:T(8,128)(2,1)}, u32[]{:S(2)}) copy-start(bf16[256,3584]{1,0:T(8,128)(2,1)} %copy-done.3) | copy-start | bytes 5505028
  68.8 2.1 %copy-start.8 = (f32[1,3584]{1,0:T(1,128)S(1)}, f32[1,3584]{1,0:T(1,128)}, u32[]{:S(2)}) copy-start(f32[1,3584]{1,0:T(1,128)} %damping_ref.1) | copy-start | bytes 43012
  68.8 5.9 %copy-start.6 = (bf16[256,3584]{1,0:T(8,128)(2,1)S(1)}, bf16[256,3584]{1,0:T(8,128)(2,1)}, u32[]{:S(2)}) copy-start(bf16[256,3584]{1,0:T(8,128)(2,1)} %copy-done.5) | copy-start | bytes 5505028
  69.5 5.2 %copy-start.2 = (bf16[1,256,3584]{2,1,0:T(8,128)(2,1)S(1)}, bf16[1,256,3584]{2,1,0:T(8,128)(2,1)}, u32[]{:S(2)}) copy-start(bf16[1,256,3584]{2,1,0:T(8,128)(2,1)} %param.7) | copy-start | bytes 5505028
  69.5 5.2 %collective-permute-start.10 = (bf16[256,256]{1,0:T(8,128)(2,1)S(1)}, bf16[256,256]{1,0:T(8,128)(2,1)S(1)}, u32[]{:S(2)}, u32[]{:S(2)}) collective-permute-start(bf16[256,256]{1,0:T(8,128)(2,1)S(1)} %get-tuple-element.11), channel_id=1, source_target_pairs={{0,1},{1,0},{2,3},{3,2},{4,5},{5,4},{6,7},{7,6},{8,9},{9,8},{10,11... | collective-permute-start | bytes 393224 | tf_op jit(solution)/shard_map/swap_features/ppermute | solution.py:141

commit v2 on v1

v2 whole, which is shorter than its diff:
```python
import functools

import jax
import jax.numpy as jnp
from jax import lax
from jax.experimental import pallas as pl
from jax.experimental.pallas import tpu as pltpu
from jax.sharding import Mesh, PartitionSpec as P

ROWS_E = 128
ETA = 0.5
CAP = 2
LANES = 128
WIDTH = 896
VMEM = 16 * 2**20
F32 = jnp.float32
BF16 = jnp.bfloat16


def call(body, out_shape, operands, flops, scratch=(), name=None):
    size = sum(o.size * o.dtype.itemsize for o in operands)
    outs = jax.tree.leaves(out_shape)
    size += sum(o.size * o.dtype.itemsize for o in outs)
    return pl.pallas_call(
        body,
        out_shape=out_shape,
        in_specs=[pl.BlockSpec(memory_space=pltpu.VMEM)] * len(operands),
        out_specs=jax.tree.map(lambda _: pl.BlockSpec(memory_space=pltpu.VMEM), out_shape),
        scratch_shapes=list(scratch),
        cost_estimate=pl.CostEstimate(flops=flops, bytes_accessed=size, transcendentals=0),
        compiler_params=pltpu.CompilerParams(vmem_limit_bytes=VMEM),
        name=name,
    )(*operands)


def tag_body(tokens_hbm, ids_hbm, out_ref, ids_ref, sems):
    feats = tokens_hbm.shape[1]
    top = ids_ref.shape[0]
    get_ids = pltpu.make_async_copy(ids_hbm, ids_ref, sems.at[0])
    get_tokens = pltpu.make_async_copy(tokens_hbm, out_ref.at[:, pl.ds(0, feats)], sems.at[1])
    get_ids.start()
    get_tokens.start()
    spread = (
        lax.broadcasted_iota(jnp.int32, (top, LANES), 0)
        == lax.broadcasted_iota(jnp.int32, (top, LANES), 1)
    ).astype(BF16)
    get_ids.wait()
    ids = ids_ref[...].astype(F32).astype(BF16)
    out_ref[:, feats:] = lax.dot_general(
        ids, spread, (((0,), (0,)), ((), ())), preferred_element_type=F32
    ).astype(BF16)
    get_tokens.wait()


def pack_body(tok_rows, top, first_ref, *refs):
    *block_refs, out_hbm, held, out_ref, sems = refs
    feats = out_ref.shape[-1]
    at = 0
    for ref in block_refs:
        held[at : at + ref.shape[0], :] = ref[...]
        at += ref.shape[0]
    tokens = at
    dests, per_dest = out_ref.shape[0], out_ref.shape[1]
    rows = dests * per_dest
    pick = (
        lax.broadcasted_iota(jnp.int32, (top, LANES), 0)
        == lax.broadcasted_iota(jnp.int32, (top, LANES), 1)
    ).astype(BF16)
    ids = lax.dot_general(
        pick, held[:, feats:], (((1,), (1,)), ((), ())), preferred_element_type=F32
    )
    row = lax.broadcasted_iota(jnp.int32, (rows, 1), 0)
    expert = (first_ref[0] + 2 * (row // per_dest)).astype(F32)
    block = (row % per_dest) // CAP
    slot = (row % CAP).astype(F32)
    tok = lax.broadcasted_iota(jnp.int32, (1, tokens), 1)
    named = ids[0:1, :] == expert
    for k in range(1, top):
        named = named | (ids[k : k + 1, :] == expert)
    named = named & (tok // tok_rows == block)
    member = jnp.where(named, 1.0, 0.0)
    before = (
        lax.broadcasted_iota(jnp.int32, (tokens, tokens), 0)
        < lax.broadcasted_iota(jnp.int32, (tokens, tokens), 1)
    ).astype(BF16)
    rank = jnp.dot(member.astype(BF16), before, preferred_element_type=F32)
    select = jnp.where(rank == slot, member, 0.0).astype(BF16)
    copies = []
    for i, lo in enumerate(range(0, feats, WIDTH)):
        out_ref[:, :, lo : lo + WIDTH] = (
            jnp.dot(select, held[:, lo : lo + WIDTH], preferred_element_type=F32)
            .astype(BF16)
            .reshape(dests, per_dest, WIDTH)
        )
        cols = (slice(None), slice(None), pl.ds(lo, WIDTH))
        copies.append(pltpu.make_async_copy(out_ref.at[cols], out_hbm.at[cols], sems.at[i]))
        copies[-1].start()
    for copy in copies:
        copy.wait()


def prune_body(weight_ref, bits_ref, pruned_ref, kept_ref, keep_ref):
    rows, words = bits_ref.shape
    feats = weight_ref.shape[1]
    lane = lax.broadcasted_iota(jnp.int32, (rows, LANES), 1)
    bits = jnp.concatenate([bits_ref[...], jnp.zeros((rows, LANES - words), jnp.int32)], axis=1)
    for j in range(feats // LANES):
        word = jnp.take_along_axis(bits, lane // 32 + 4 * j, axis=1, mode="promise_in_bounds")
        keep = jnp.bitwise_and(jnp.right_shift(word, lane % 32), 1).astype(F32)
        cols = slice(j * LANES, (j + 1) * LANES)
        slab = weight_ref[:, cols].astype(F32)
        pruned_ref[:, cols] = jnp.where(keep > 0.5, 0.0, slab).astype(BF16)
        kept_ref[:, cols] = jnp.where(keep > 0.5, slab, 0.0).astype(BF16)
        keep_ref[:, cols] = keep.astype(BF16)


def project_body(routed_ref, pruned_ref, part_ref, low_ref, routed_hbm=None, sem=None):
    if sem is not None:
        away = pltpu.make_async_copy(routed_ref, routed_hbm, sem)
        away.start()
    part = lax.dot_general(
        pruned_ref[...], routed_ref[...], (((1,), (1,)), ((), ())), preferred_element_type=F32
    )
    part_ref[...] = part
    low_ref[...] = part.astype(BF16)
    if sem is not None:
        away.wait()


def scale_body(*refs):
    *routed_refs, damping_ref, scale_ref = refs
    feats = damping_ref.shape[1]
    for lo in range(0, feats, WIDTH):
        cols = slice(lo, lo + WIDTH)
        diag = damping_ref[:, cols]
        for ref in routed_refs:
            rows = ref[:, cols].astype(F32)
            diag = diag + jnp.sum(rows * rows, axis=0, keepdims=True) * (1.0 / ROWS_E)
        scale_ref[:, cols] = (ETA / ROWS_E) / diag


def update_body(n, *refs):
    parts, others, routed_refs = refs[:n], refs[n : 2 * n], refs[2 * n : 3 * n]
    scale_ref, kept_ref, keep_ref, out_hbm, out_ref, sems = refs[3 * n :]
    feats = kept_ref.shape[1]
    projected = [(p[...] + o[...].astype(F32)).astype(BF16) for p, o in zip(parts, others)]
    copies = []
    for i, lo in enumerate(range(0, feats, WIDTH)):
        cols = slice(lo, lo + WIDTH)
        comp = jnp.dot(projected[0], routed_refs[0][:, cols], preferred_element_type=F32)
        for p, r in zip(projected[1:], routed_refs[1:]):
            comp = comp + jnp.dot(p, r[:, cols], preferred_element_type=F32)
        gain = keep_ref[:, cols].astype(F32) * (comp * scale_ref[:, cols])
        out_ref[:, cols] = (kept_ref[:, cols].astype(F32) + gain).astype(BF16)
        cols = (slice(None), pl.ds(lo, WIDTH))
        copies.append(pltpu.make_async_copy(out_ref.at[cols], out_hbm.at[cols], sems.at[i]))
        copies[-1].start()
    for copy in copies:
        copy.wait()


def shape(*dims, dtype=BF16):
    return jax.ShapeDtypeStruct(dims, dtype)


def shift(x, axis, step):
    n = lax.axis_size(axis)
    return lax.ppermute(x, axis, [(i, (i + step) % n) for i in range(n)])


def pack(first, blocks, tok_rows, top, feats, plane):
    n_tok = sum(b.shape[0] for b in blocks)
    per_dest = n_tok // tok_rows * CAP
    return pl.pallas_call(
        functools.partial(pack_body, tok_rows, top),
        out_shape=shape(plane, per_dest, feats),
        in_specs=[pl.BlockSpec(memory_space=pltpu.SMEM)]
        + [pl.BlockSpec(memory_space=pltpu.VMEM)] * len(blocks),
        out_specs=pl.BlockSpec(memory_space=pltpu.HBM),
        scratch_shapes=[
            pltpu.VMEM((n_tok, feats + LANES), BF16),
            pltpu.VMEM((plane, per_dest, feats), BF16),
            pltpu.SemaphoreType.DMA((feats // WIDTH,)),
        ],
        cost_estimate=pl.CostEstimate(
            flops=1, bytes_accessed=1, transcendentals=0
        ),
        compiler_params=pltpu.CompilerParams(vmem_limit_bytes=VMEM),
    )(first, *blocks)


def local(tokens, expert_ids, weight, mask_bits, damping):
    tok_rows, feats = tokens.shape
    top = expert_ids.shape[1]
    slab = weight.shape[1]
    weight = weight.reshape(slab, feats)
    me_z, me_core = lax.axis_index("z"), lax.axis_index("core")
    plane = lax.axis_size("yh") * lax.axis_size("x")
    first = (me_z * plane * 2 + me_core).astype(jnp.int32).reshape(1)
    hbm, vmem = pl.BlockSpec(memory_space=pltpu.HBM), pl.BlockSpec(memory_space=pltpu.VMEM)

    with jax.named_scope("tag"):
        own = pl.pallas_call(
            tag_body,
            out_shape=shape(tok_rows, feats + LANES),
            in_specs=[hbm, hbm],
            out_specs=vmem,
            scratch_shapes=[
                pltpu.VMEM((top, tok_rows), jnp.int32),
                pltpu.SemaphoreType.DMA((2,)),
            ],
            compiler_params=pltpu.CompilerParams(vmem_limit_bytes=VMEM),
        )(tokens, expert_ids.T)

    def packed(blocks):
        with jax.named_scope("pack"):
            return pack(first, blocks, tok_rows, top, feats, plane)

    def route(rows):
        with jax.named_scope("route"):
            block = lax.all_to_all(rows, ("yh", "x"), split_axis=0, concat_axis=0, tiled=True)
        return block.reshape(-1, feats)

    with jax.named_scope("gather_near"):
        m1, p1, m2 = shift(own, "z", 1), shift(own, "z", -1), shift(own, "z", 2)
    with jax.named_scope("gather_far"):
        p23 = shift(jnp.concatenate((own, p1)), "z", -2)
        m34 = shift(jnp.concatenate((m1, m2)), "z", 2)

    def swap(group):
        with jax.named_scope("swap_core"):
            return (*group, shift(jnp.concatenate(group), "core", 1))

    routed1 = route(packed(swap((own, m1, p1, m2))))
    routed2 = route(packed(swap((p23, m34))))
    with jax.named_scope("prune"):
        pruned, kept, keep = call(
            prune_body, (shape(slab, feats),) * 3, (weight, mask_bits), 1 << 22
        )

    def project(routed, away):
        rows = routed.shape[0]
        with jax.named_scope("project"):
            return pl.pallas_call(
                project_body,
                out_shape=(shape(slab, rows, dtype=F32), shape(slab, rows))
                + ((shape(rows, feats),) if away else ()),
                in_specs=[vmem, vmem],
                out_specs=(vmem, vmem) + ((hbm,) if away else ()),
                scratch_shapes=[pltpu.SemaphoreType.DMA] if away else [],
                cost_estimate=pl.CostEstimate(
                    flops=2 * rows * slab * feats, bytes_accessed=1 << 21, transcendentals=0
                ),
                compiler_params=pltpu.CompilerParams(vmem_limit_bytes=VMEM),
            )(routed, pruned)

    part1, low1, routed1 = project(routed1, True)
    with jax.named_scope("swap_features"):
        other1 = shift(low1, "yl", 1)
    part2, low2 = project(routed2, False)
    with jax.named_scope("swap_features"):
        other2 = shift(low2, "yl", 1)
    with jax.named_scope("scale"):
        scale = call(
            scale_body, shape(1, feats, dtype=F32), (routed1, routed2, damping), 4 * slab * feats
        )
    with jax.named_scope("update"):
        operands = (part1, part2, other1, other2, routed1, routed2, scale, kept, keep)
        out = pl.pallas_call(
            functools.partial(update_body, 2),
            out_shape=shape(slab, feats),
            in_specs=[vmem] * len(operands),
            out_specs=hbm,
            scratch_shapes=[
                pltpu.VMEM((slab, feats), BF16),
                pltpu.SemaphoreType.DMA((feats // WIDTH,)),
            ],
            compiler_params=pltpu.CompilerParams(vmem_limit_bytes=VMEM),
        )(*operands)
    return out.reshape(1, slab, feats)


def solution(mesh):
    n_hrow, n_hcol = mesh.shape["hrow"], mesh.shape["hcol"]
    n_expert = mesh.shape["expert"]
    fine = Mesh(
        mesh.devices.reshape(n_expert // 2, 2, n_hrow // 2, 2, n_hcol),
        ("z", "yh", "x", "core", "yl"),
    )
    own = ("z", "yh", "x", "core")
    in_specs = (P(own, "yl"), P(own, None), P(own, None, "yl"), P(None, "yl"), P(own, "yl"))
    return jax.shard_map(
        local, mesh=fine, in_specs=in_specs, out_specs=P(own, None, "yl"), check_vma=False
    )
```

time: 78 us -> 71.6 us (0.918)
  waiting for transfers between devices: 42.7 us -> 34.2 us
  Pallas kernels: 5.46 us -> 8.33 us
  local copies, waits for them, and re-layouts: 8.39 us -> 6.37 us
  starting transfers between devices: 20.3 us -> 21.6 us
    all_to_all x1 -> x2, waiting for transfers between devices: 20.7 us -> 14.9 us  [route(): lax.all_to_all(rows, ('yh', 'x'), split_axis=0, concat_axis=0, tiled=True)]
    pallas_call x1 -> x6, Pallas kernels: 1.12 us -> 6.79 us  [the longest x2 3.01 us: pack(): pl.pallas_call(functools.partial(pack_body, tok_rows, top), out_shape=sha...]
    all_to_all x1 -> x2, starting transfers between devices: 6.16 us -> 9.6 us  [route(): lax.all_to_all(rows, ('yh', 'x'), split_axis=0, concat_axis=0, tiled=True)]
    pallas_call x5 -> x2, Pallas kernels: 4.34 us -> 1.54 us  [call(): pl.pallas_call(body, out_shape=out_shape, in_specs=[pl.BlockSpec(memory_s...]
    ppermute x11 -> x9, waiting for transfers between devices: 21.9 us -> 19.3 us  [shift(): return lax.ppermute(x, axis, [(i, (i + step) % n) for i in range(n)])]
    ppermute x11 -> x9, starting transfers between devices: 14.1 us -> 12 us  [shift(): return lax.ppermute(x, axis, [(i, (i + step) % n) for i in range(n)])]
    unnamed x23 -> x27, local copies, waits for them, and re-layouts: 8.39 us -> 6.37 us
  transfers between devices with their start and end apart: 12 -> 11, of which waited for: 7 -> 8; matrix products, arithmetic and copies ran while one was open for 0% -> 0% of each run, Pallas kernels for 2% -> 9%
where the time goes in v2:
time: 71.6 us; the launch traced here: 70.9 us
  waiting for transfers between devices  34.2 us (48%)
  starting transfers between devices  21.6 us (30%)
  Pallas kernels  8.33 us (12%)
  local copies, waits for them, and re-layouts  6.37 us (9%)
    ppermute x9, waiting for transfers between devices, shift(): return lax.ppermute(x, axis, [(i, (i + step) % n) for i in range(n)])  19.3 us
    all_to_all x2, waiting for transfers between devices, route(): lax.all_to_all(rows, ('yh', 'x'), split_axis=0, concat_axis=0, tiled=True)  14.9 us
    ppermute x9, starting transfers between devices, shift(): return lax.ppermute(x, axis, [(i, (i + step) % n) for i in range(n)])  12 us
    all_to_all x2, starting transfers between devices, route(): lax.all_to_all(rows, ('yh', 'x'), split_axis=0, concat_axis=0, tiled=True)  9.6 us
    unnamed x27, local copies, waits for them, and re-layouts  6.37 us
    pallas_call x2, Pallas kernels, pack(): pl.pallas_call(functools.partial(pack_body, tok_rows, top), out_shape=sha...  3.01 us
    pallas_call x1, Pallas kernels, local(): pl.pallas_call(functools.partial(update_body, 2), out_shape=shape(slab, f...  2.05 us
    pallas_call x2, Pallas kernels, call(): pl.pallas_call(body, out_shape=out_shape, in_specs=[pl.BlockSpec(memory_s...  1.54 us
  transfers between devices with their start and end apart: 11, of which 8 were waited for; matrix products, arithmetic and copies ran while one was open for 0% of the time, Pallas kernels for 9%

profile of v2, /device:TPU:8, one launch (start us, length us, event | category | flops | bytes accessed | tf_op | source)
XLA Modules:
  0.0 70.9 jit_solution(6122622048296980460)
XLA Ops:
  0.0 0.9 %copy-done.9 = bf16[16,3584]{1,0:T(8,128)(2,1)S(1)} copy-done((bf16[16,3584]{1,0:T(8,128)(2,1)S(1)}, bf16[16,3584]{1,0:T(8,128)(2,1)}, u32[]{:S(2)}) %copy-start.9) | copy-done | bytes 114712
  1.8 5.9 %collective-permute-start.1 = (bf16[16,3712]{1,0:T(8,128)(2,1)S(1)}, bf16[16,3712]{1,0:T(8,128)(2,1)S(1)}, u32[]{:S(2)}, u32[]{:S(2)}) collective-permute-start(bf16[16,3712]{1,0:T(8,128)(2,1)S(1)} %tag.1.refs_0_), channel_id=1, source_target_pairs={{0,224},{32,0},{64,32},{96,64},{128,96},{160,128},{192,160},{224,1... | collective-permute-start | bytes 356360 | tf_op jit(solution)/shard_map/gather_near/ppermute | solution.py:168
  7.8 2.5 %collective-permute-done.1.refs_2_ = bf16[16,3712]{1,0:T(8,128)(2,1)S(1)} collective-permute-done((bf16[16,3712]{1,0:T(8,128)(2,1)S(1)}, bf16[16,3712]{1,0:T(8,128)(2,1)S(1)}, u32[]{:S(2)}, u32[]{:S(2)}) %collective-permute-start.1) | collective-permute-done | bytes 118816 | tf_op jit(solution)/shard_map/gather_near/ppermute | solution.py:168
  10.3 3.0 %collective-permute-start.4 = (bf16[32,3712]{1,0:T(8,128)(2,1)S(1)}, bf16[32,3712]{1,0:T(8,128)(2,1)S(1)}, u32[]{:S(2)}, u32[]{:S(2)}) collective-permute-start(bf16[32,3712]{1,0:T(8,128)(2,1)S(1)} %pad_maximum_fusion.2), channel_id=1, source_target_pairs={{0,192},{32,224},{64,0},{96,32},{128,64},{160,96},{192,128},{224,1... | collective-permute-start | bytes 712712 | tf_op jit(solution)/shard_map/gather_far/ppermute | solution.py:168
  13.3 4.5 %collective-permute-done.2.refs_3_ = bf16[16,3712]{1,0:T(8,128)(2,1)S(1)} collective-permute-done((bf16[16,3712]{1,0:T(8,128)(2,1)S(1)}, bf16[16,3712]{1,0:T(8,128)(2,1)S(1)}, u32[]{:S(2)}, u32[]{:S(2)}) %collective-permute-start.2) | collective-permute-done | bytes 118816 | tf_op jit(solution)/shard_map/gather_near/ppermute | solution.py:168
  18.1 1.7 %collective-permute-done.3.refs_4_ = bf16[64,3712]{1,0:T(8,128)(2,1)S(1)} collective-permute-done((bf16[64,3712]{1,0:T(8,128)(2,1)S(1)}, bf16[64,3712]{1,0:T(8,128)(2,1)S(1)}, u32[]{:S(2)}, u32[]{:S(2)}) %collective-permute-start.3) | collective-permute-done | bytes 475168 | tf_op jit(solution)/shard_map/swap_core/ppermute | solution.py:168
  19.8 1.5 %pack.2 = bf16[8,16,3584]{2,1,0:T(8,128)(2,1)} custom-call(s32[1]{0:T(128)} %bitcast.first_ref, bf16[16,3712]{1,0:T(8,128)(2,1)S(1)} %tag.1.refs_0_, bf16[16,3712]{1,0:T(8,128)(2,1)S(1)} %collective-permute-done.refs_1_, bf16[16,3712]{1,0:T(8,128)(2,1)S(1)} %collective-permute-done.1.refs_2_, bf16[16,3712]{1,0:T(8,128)(2,1)S(1)} %collective-permute-done.2.refs_3_, ...), custom_call_target="tpu_custom_call" | custom-call | flops 1 | bytes 1 | tf_op jit(solution)/shard_map/pack/pallas_call | solution.py:174
  21.3 6.0 %all-to-all-start = ((bf16[8,16,3584]{2,1,0:T(8,128)(2,1)}), bf16[8,16,3584]{2,1,0:T(8,128)(2,1)S(1)}, u32[]{:S(2)}, u32[]{:S(2)}) async-start(bf16[8,16,3584]{2,1,0:T(8,128)(2,1)} %pack.2), calls=%async_computation | async-start | bytes 1835008 | tf_op jit(solution)/shard_map/route/all_to_all | solution.py:221
  27.3 6.1 %collective-permute-done.5.refs_1_ = bf16[32,3712]{1,0:T(8,128)(2,1)S(1)} collective-permute-done((bf16[32,3712]{1,0:T(8,128)(2,1)S(1)}, bf16[32,3712]{1,0:T(8,128)(2,1)S(1)}, u32[]{:S(2)}, u32[]{:S(2)}) %collective-permute-start.5) | collective-permute-done | bytes 237600 | tf_op jit(solution)/shard_map/gather_far/ppermute | solution.py:168
  33.6 1.8 %collective-permute-done.6.refs_2_ = bf16[64,3712]{1,0:T(8,128)(2,1)S(1)} collective-permute-done((bf16[64,3712]{1,0:T(8,128)(2,1)S(1)}, bf16[64,3712]{1,0:T(8,128)(2,1)S(1)}, u32[]{:S(2)}, u32[]{:S(2)}) %collective-permute-start.6) | collective-permute-done | bytes 475168 | tf_op jit(solution)/shard_map/swap_core/ppermute | solution.py:168
  35.4 1.5 %pack.3 = bf16[8,16,3584]{2,1,0:T(8,128)(2,1)} custom-call(s32[1]{0:T(128)} %bitcast.first_ref, bf16[32,3712]{1,0:T(8,128)(2,1)S(1)} %collective-permute-done.4.refs_0_, bf16[32,3712]{1,0:T(8,128)(2,1)S(1)} %collective-permute-done.5.refs_1_, bf16[64,3712]{1,0:T(8,128)(2,1)S(1)} %collective-permute-done.6.refs_2_), custom_call_target="tpu_custom_call" | custom-call | flops 1 | bytes 1 | tf_op jit(solution)/shard_map/pack/pallas_call | solution.py:174
  36.9 6.5 %all-to-all-done = bf16[8,16,3584]{2,1,0:T(8,128)(2,1)S(1)} async-done(((bf16[8,16,3584]{2,1,0:T(8,128)(2,1)}), bf16[8,16,3584]{2,1,0:T(8,128)(2,1)S(1)}, u32[]{:S(2)}, u32[]{:S(2)}) %all-to-all-start) | async-done | bytes 917536 | tf_op jit(solution)/shard_map/route/all_to_all | solution.py:221
  43.4 0.9 %copy-done.2 = bf16[8,16,3584]{2,1,0:T(8,128)(2,1)} copy-done((bf16[8,16,3584]{2,1,0:T(8,128)(2,1)}, bf16[8,16,3584]{2,1,0:T(8,128)(2,1)S(1)}, u32[]{:S(2)}) %copy-start.2) | copy-done | bytes 917528
  44.4 3.6 %all-to-all-start.1 = ((bf16[8,16,3584]{2,1,0:T(8,128)(2,1)}), bf16[8,16,3584]{2,1,0:T(8,128)(2,1)S(1)}, u32[]{:S(2)}, u32[]{:S(2)}) async-start(bf16[8,16,3584]{2,1,0:T(8,128)(2,1)} %pack.3), calls=%async_computation.1 | async-start | bytes 1835008 | tf_op jit(solution)/shard_map/route/all_to_all | solution.py:221
  48.1 1.6 %copy-done.4 = bf16[1,256,3584]{2,1,0:T(8,128)(2,1)S(1)} copy-done((bf16[1,256,3584]{2,1,0:T(8,128)(2,1)S(1)}, bf16[1,256,3584]{2,1,0:T(8,128)(2,1)}, u32[]{:S(2)}) %copy-start.4) | copy-done | bytes 1835032
  49.6 1.3 %prune.1 = (bf16[256,3584]{1,0:T(8,128)(2,1)S(1)}, bf16[256,3584]{1,0:T(8,128)(2,1)S(1)}, bf16[256,3584]{1,0:T(8,128)(2,1)S(1)}) custom-call(bf16[256,3584]{1,0:T(8,128)(2,1)S(1)} %bitcast.10, s32[256,112]{1,0:T(8,128)S(1)} %copy.6.bits_ref), custom_call_target="tpu_custom_call" | custom-call | flops 4194304 | bytes 7454720 | tf_op jit(solution)/shard_map/prune/pallas_call | solution.py:24
  51.0 1.2 %copy-done.5 = bf16[256,3584]{1,0:T(8,128)(2,1)} copy-done((bf16[256,3584]{1,0:T(8,128)(2,1)}, bf16[256,3584]{1,0:T(8,128)(2,1)S(1)}, u32[]{:S(2)}) %copy-start.5) | copy-done | bytes 1835032
  52.2 0.9 %project.2 = (f32[256,128]{1,0:T(8,128)S(1)}, bf16[256,128]{1,0:T(8,128)(2,1)S(1)}, bf16[128,3584]{1,0:T(8,128)(2,1)S(1)}) custom-call(bf16[128,3584]{1,0:T(8,128)(2,1)S(1)} %bitcast.9, bf16[256,3584]{1,0:T(8,128)(2,1)S(1)} %get-tuple-element.13.pruned_ref), custom_call_target="tpu_custom_call" | custom-call | flops 234881024 | bytes 2097152 | tf_op jit(solution)/shard_map/project/pallas_call | solution.py:244
  53.1 0.9 %copy-done = bf16[128,3584]{1,0:T(8,128)(2,1)} copy-done((bf16[128,3584]{1,0:T(8,128)(2,1)}, bf16[128,3584]{1,0:T(8,128)(2,1)S(1)}, u32[]{:S(2)}) %copy-start) | copy-done | bytes 917528
  54.0 1.4 %collective-permute-start.7 = (bf16[256,128]{1,0:T(8,128)(2,1)S(1)}, bf16[256,128]{1,0:T(8,128)(2,1)S(1)}, u32[]{:S(2)}, u32[]{:S(2)}) collective-permute-start(bf16[256,128]{1,0:T(8,128)(2,1)S(1)} %get-tuple-element.16), channel_id=1, source_target_pairs={{0,1},{1,0},{2,3},{3,2},{4,5},{5,4},{6,7},{7,6},{8,9},{9,8},{10,11... | collective-permute-start | bytes 196616 | tf_op jit(solution)/shard_map/swap_features/ppermute | solution.py:168
  55.4 8.4 %all-to-all-done.1 = bf16[8,16,3584]{2,1,0:T(8,128)(2,1)S(1)} async-done(((bf16[8,16,3584]{2,1,0:T(8,128)(2,1)}), bf16[8,16,3584]{2,1,0:T(8,128)(2,1)S(1)}, u32[]{:S(2)}, u32[]{:S(2)}) %all-to-all-start.1) | async-done | bytes 917536 | tf_op jit(solution)/shard_map/route/all_to_all | solution.py:221
  64.5 1.4 %collective-permute-start.8 = (bf16[256,128]{1,0:T(8,128)(2,1)S(1)}, bf16[256,128]{1,0:T(8,128)(2,1)S(1)}, u32[]{:S(2)}, u32[]{:S(2)}) collective-permute-start(bf16[256,128]{1,0:T(8,128)(2,1)S(1)} %get-tuple-element.17), channel_id=1, source_target_pairs={{0,1},{1,0},{2,3},{3,2},{4,5},{5,4},{6,7},{7,6},{8,9},{9,8},{10,11... | collective-permute-start | bytes 196616 | tf_op jit(solution)/shard_map/swap_features/ppermute | solution.py:168
  66.1 2.7 %collective-permute-done.8.refs_3_ = bf16[256,128]{1,0:T(8,128)(2,1)S(1)} collective-permute-done((bf16[256,128]{1,0:T(8,128)(2,1)S(1)}, bf16[256,128]{1,0:T(8,128)(2,1)S(1)}, u32[]{:S(2)}, u32[]{:S(2)}) %collective-permute-start.8) | collective-permute-done | bytes 65568 | tf_op jit(solution)/shard_map/swap_features/ppermute | solution.py:168
  68.8 2.1 %update.1 = bf16[256,3584]{1,0:T(8,128)(2,1)} custom-call(f32[256,128]{1,0:T(8,128)S(1)} %get-tuple-element.14.refs_0_, f32[256,128]{1,0:T(8,128)S(1)} %get-tuple-element.15.refs_1_, bf16[256,128]{1,0:T(8,128)(2,1)S(1)} %collective-permute-done.7.refs_2_, bf16[256,128]{1,0:T(8,128)(2,1)S(1)} %collective-permute-done.8.refs_3_, ...), custom_call_target="tpu_custom_call" | custom-call | tf_op jit(solution)/shard_map/update/pallas_call | solution.py:269
  (37 shorter events, 2.3 us)
Async XLA Ops:
  0.0 0.9 %copy-start.9 = (bf16[16,3584]{1,0:T(8,128)(2,1)S(1)}, bf16[16,3584]{1,0:T(8,128)(2,1)}, u32[]{:S(2)}) copy-start(bf16[16,3584]{1,0:T(8,128)(2,1)} %tokens_hbm.1) | copy-start | bytes 344068
  0.9 0.7 copy-start.11
  1.8 8.4 %collective-permute-start.1 = (bf16[16,3712]{1,0:T(8,128)(2,1)S(1)}, bf16[16,3712]{1,0:T(8,128)(2,1)S(1)}, u32[]{:S(2)}, u32[]{:S(2)}) collective-permute-start(bf16[16,3712]{1,0:T(8,128)(2,1)S(1)} %tag.1.refs_0_), channel_id=1, source_target_pairs={{0,224},{32,0},{64,32},{96,64},{128,96},{160,128},{192,160},{224,1... | collective-permute-start | bytes 356360 | tf_op jit(solution)/shard_map/gather_near/ppermute | solution.py:168
  7.8 10.0 %collective-permute-start.2 = (bf16[16,3712]{1,0:T(8,128)(2,1)S(1)}, bf16[16,3712]{1,0:T(8,128)(2,1)S(1)}, u32[]{:S(2)}, u32[]{:S(2)}) collective-permute-start(bf16[16,3712]{1,0:T(8,128)(2,1)S(1)} %tag.1.refs_0_), channel_id=1, source_target_pairs={{0,64},{32,96},{64,128},{96,160},{128,192},{160,224},{192,0},{224,... | collective-permute-start | bytes 356360 | tf_op jit(solution)/shard_map/gather_near/ppermute | solution.py:168
  7.8 10.0 %collective-permute-start = (bf16[16,3712]{1,0:T(8,128)(2,1)S(1)}, bf16[16,3712]{1,0:T(8,128)(2,1)S(1)}, u32[]{:S(2)}, u32[]{:S(2)}) collective-permute-start(bf16[16,3712]{1,0:T(8,128)(2,1)S(1)} %tag.1.refs_0_), channel_id=1, source_target_pairs={{0,32},{32,64},{64,96},{96,128},{128,160},{160,192},{192,224},{224... | collective-permute-start | bytes 356360 | tf_op jit(solution)/shard_map/gather_near/ppermute | solution.py:168
  10.3 17.0 %collective-permute-start.4 = (bf16[32,3712]{1,0:T(8,128)(2,1)S(1)}, bf16[32,3712]{1,0:T(8,128)(2,1)S(1)}, u32[]{:S(2)}, u32[]{:S(2)}) collective-permute-start(bf16[32,3712]{1,0:T(8,128)(2,1)S(1)} %pad_maximum_fusion.2), channel_id=1, source_target_pairs={{0,192},{32,224},{64,0},{96,32},{128,64},{160,96},{192,128},{224,1... | collective-permute-start | bytes 712712 | tf_op jit(solution)/shard_map/gather_far/ppermute | solution.py:168
  17.9 1.9 %collective-permute-start.3 = (bf16[64,3712]{1,0:T(8,128)(2,1)S(1)}, bf16[64,3712]{1,0:T(8,128)(2,1)S(1)}, u32[]{:S(2)}, u32[]{:S(2)}) collective-permute-start(bf16[64,3712]{1,0:T(8,128)(2,1)S(1)} %pad_maximum_fusion), channel_id=1, source_target_pairs={{0,2},{2,0},{1,3},{3,1},{4,6},{6,4},{5,7},{7,5},{8,10},{10,8},{9,1... | collective-permute-start | bytes 1425416 | tf_op jit(solution)/shard_map/swap_core/ppermute | solution.py:168
  18.0 15.4 %collective-permute-start.5 = (bf16[32,3712]{1,0:T(8,128)(2,1)S(1)}, bf16[32,3712]{1,0:T(8,128)(2,1)S(1)}, u32[]{:S(2)}, u32[]{:S(2)}) collective-permute-start(bf16[32,3712]{1,0:T(8,128)(2,1)S(1)} %pad_maximum_fusion.3), channel_id=1, source_target_pairs={{0,64},{32,96},{64,128},{96,160},{128,192},{160,224},{192,0},{224,... | collective-permute-start | bytes 712712 | tf_op jit(solution)/shard_map/gather_far/ppermute | solution.py:168
  21.3 22.1 %all-to-all-start = ((bf16[8,16,3584]{2,1,0:T(8,128)(2,1)}), bf16[8,16,3584]{2,1,0:T(8,128)(2,1)S(1)}, u32[]{:S(2)}, u32[]{:S(2)}) async-start(bf16[8,16,3584]{2,1,0:T(8,128)(2,1)} %pack.2), calls=%async_computation | async-start | bytes 1835008 | tf_op jit(solution)/shard_map/route/all_to_all | solution.py:221
  33.5 14.5 %copy-start.12 = (s32[256,112]{0,1:T(8,128)S(1)}, s32[256,112]{0,1:T(8,128)}, u32[]{:S(2)}) copy-start(s32[256,112]{0,1:T(8,128)} %param.8) | copy-start | bytes 344068
  33.5 1.9 %collective-permute-start.6 = (bf16[64,3712]{1,0:T(8,128)(2,1)S(1)}, bf16[64,3712]{1,0:T(8,128)(2,1)S(1)}, u32[]{:S(2)}, u32[]{:S(2)}) collective-permute-start(bf16[64,3712]{1,0:T(8,128)(2,1)S(1)} %pad_maximum_fusion.1), channel_id=1, source_target_pairs={{0,2},{2,0},{1,3},{3,1},{4,6},{6,4},{5,7},{7,5},{8,10},{10,8},{9,1... | collective-permute-start | bytes 1425416 | tf_op jit(solution)/shard_map/swap_core/ppermute | solution.py:168
  43.4 0.9 %copy-start.2 = (bf16[8,16,3584]{2,1,0:T(8,128)(2,1)}, bf16[8,16,3584]{2,1,0:T(8,128)(2,1)S(1)}, u32[]{:S(2)}) copy-start(bf16[8,16,3584]{2,1,0:T(8,128)(2,1)S(1)} %all-to-all-done) | copy-start | bytes 2752516
  44.4 19.4 %all-to-all-start.1 = ((bf16[8,16,3584]{2,1,0:T(8,128)(2,1)}), bf16[8,16,3584]{2,1,0:T(8,128)(2,1)S(1)}, u32[]{:S(2)}, u32[]{:S(2)}) async-start(bf16[8,16,3584]{2,1,0:T(8,128)(2,1)} %pack.3), calls=%async_computation.1 | async-start | bytes 1835008 | tf_op jit(solution)/shard_map/route/all_to_all | solution.py:221
  48.0 4.2 %copy-start.3 = (bf16[8,16,3584]{2,1,0:T(8,128)(2,1)S(1)}, bf16[8,16,3584]{2,1,0:T(8,128)(2,1)}, u32[]{:S(2)}) copy-start(bf16[8,16,3584]{2,1,0:T(8,128)(2,1)} %copy-done.2) | copy-start | bytes 2752516
  48.0 1.6 %copy-start.4 = (bf16[1,256,3584]{2,1,0:T(8,128)(2,1)S(1)}, bf16[1,256,3584]{2,1,0:T(8,128)(2,1)}, u32[]{:S(2)}) copy-start(bf16[1,256,3584]{2,1,0:T(8,128)(2,1)} %param.7) | copy-start | bytes 5505028
  51.0 1.2 %copy-start.5 = (bf16[256,3584]{1,0:T(8,128)(2,1)}, bf16[256,3584]{1,0:T(8,128)(2,1)S(1)}, u32[]{:S(2)}) copy-start(bf16[256,3584]{1,0:T(8,128)(2,1)S(1)} %get-tuple-element.19.refs_7_) | copy-start | bytes 5505028
  52.2 1.8 %copy-start.7 = (bf16[256,3584]{1,0:T(8,128)(2,1)}, bf16[256,3584]{1,0:T(8,128)(2,1)S(1)}, u32[]{:S(2)}) copy-start(bf16[256,3584]{1,0:T(8,128)(2,1)S(1)} %get-tuple-element.20.refs_8_) | copy-start | bytes 5505028
  53.1 0.9 %copy-start = (bf16[128,3584]{1,0:T(8,128)(2,1)}, bf16[128,3584]{1,0:T(8,128)(2,1)S(1)}, u32[]{:S(2)}) copy-start(bf16[128,3584]{1,0:T(8,128)(2,1)S(1)} %get-tuple-element.18.refs_0_.refs_4_) | copy-start | bytes 2752516
  54.0 11.9 %copy-start.10 = (f32[1,3584]{1,0:T(1,128)S(1)}, f32[1,3584]{1,0:T(1,128)}, u32[]{:S(2)}) copy-start(f32[1,3584]{1,0:T(1,128)} %refs_2_.1) | copy-start | bytes 43012
  54.0 12.1 %collective-permute-start.7 = (bf16[256,128]{1,0:T(8,128)(2,1)S(1)}, bf16[256,128]{1,0:T(8,128)(2,1)S(1)}, u32[]{:S(2)}, u32[]{:S(2)}) collective-permute-start(bf16[256,128]{1,0:T(8,128)(2,1)S(1)} %get-tuple-element.16), channel_id=1, source_target_pairs={{0,1},{1,0},{2,3},{3,2},{4,5},{5,4},{6,7},{7,6},{8,9},{9,8},{10,11... | collective-permute-start | bytes 196616 | tf_op jit(solution)/shard_map/swap_features/ppermute | solution.py:168
  63.8 2.1 %copy-start.1 = (bf16[128,3584]{1,0:T(8,128)(2,1)S(1)}, bf16[128,3584]{1,0:T(8,128)(2,1)}, u32[]{:S(2)}) copy-start(bf16[128,3584]{1,0:T(8,128)(2,1)} %copy-done) | copy-start | bytes 2752516
  63.8 5.0 %copy-start.6 = (bf16[256,3584]{1,0:T(8,128)(2,1)S(1)}, bf16[256,3584]{1,0:T(8,128)(2,1)}, u32[]{:S(2)}) copy-start(bf16[256,3584]{1,0:T(8,128)(2,1)} %copy-done.5) | copy-start | bytes 5505028
  63.8 5.0 %copy-start.8 = (bf16[256,3584]{1,0:T(8,128)(2,1)S(1)}, bf16[256,3584]{1,0:T(8,128)(2,1)}, u32[]{:S(2)}) copy-start(bf16[256,3584]{1,0:T(8,128)(2,1)} %copy-done.7) | copy-start | bytes 5505028
  64.5 4.4 %collective-permute-start.8 = (bf16[256,128]{1,0:T(8,128)(2,1)S(1)}, bf16[256,128]{1,0:T(8,128)(2,1)S(1)}, u32[]{:S(2)}, u32[]{:S(2)}) collective-permute-start(bf16[256,128]{1,0:T(8,128)(2,1)S(1)} %get-tuple-element.17), channel_id=1, source_target_pairs={{0,1},{1,0},{2,3},{3,2},{4,5},{5,4},{6,7},{7,6},{8,9},{9,8},{10,11... | collective-permute-start | bytes 196616 | tf_op jit(solution)/shard_map/swap_features/ppermute | solution.py:168

commit v3 on v2

--- a/solution.py
+++ b/solution.py
@@ -13,6 +13,7 @@
 LANES = 128
 WIDTH = 896
 VMEM = 16 * 2**20
+GATE = 4
 F32 = jnp.float32
 BF16 = jnp.bfloat16
 
@@ -52,15 +53,15 @@
     get_tokens.wait()
 
 
-def pack_body(tok_rows, top, first_ref, *refs):
-    *block_refs, out_hbm, held, out_ref, sems = refs
-    feats = out_ref.shape[-1]
+def pack_body(tok_rows, top, n_in, experts_ref, *refs):
+    block_refs, out_refs, held = refs[:n_in], refs[n_in:-1], refs[-1]
+    feats = out_refs[0].shape[-1]
     at = 0
     for ref in block_refs:
         held[at : at + ref.shape[0], :] = ref[...]
         at += ref.shape[0]
     tokens = at
-    dests, per_dest = out_ref.shape[0], out_ref.shape[1]
+    dests, per_dest = len(out_refs), out_refs[0].shape[0]
     rows = dests * per_dest
     pick = (
         lax.broadcasted_iota(jnp.int32, (top, LANES), 0)
@@ -70,7 +71,10 @@
         pick, held[:, feats:], (((1,), (1,)), ((), ())), preferred_element_type=F32
     )
     row = lax.broadcasted_iota(jnp.int32, (rows, 1), 0)
-    expert = (first_ref[0] + 2 * (row // per_dest)).astype(F32)
+    expert = jnp.zeros((rows, 1), jnp.int32)
+    for j in range(dests):
+        expert = jnp.where(row // per_dest == j, experts_ref[j], expert)
+    expert = expert.astype(F32)
     block = (row % per_dest) // CAP
     slot = (row % CAP).astype(F32)
     tok = lax.broadcasted_iota(jnp.int32, (1, tokens), 1)
@@ -85,18 +89,11 @@
     ).astype(BF16)
     rank = jnp.dot(member.astype(BF16), before, preferred_element_type=F32)
     select = jnp.where(rank == slot, member, 0.0).astype(BF16)
-    copies = []
-    for i, lo in enumerate(range(0, feats, WIDTH)):
-        out_ref[:, :, lo : lo + WIDTH] = (
-            jnp.dot(select, held[:, lo : lo + WIDTH], preferred_element_type=F32)
-            .astype(BF16)
-            .reshape(dests, per_dest, WIDTH)
-        )
-        cols = (slice(None), slice(None), pl.ds(lo, WIDTH))
-        copies.append(pltpu.make_async_copy(out_ref.at[cols], out_hbm.at[cols], sems.at[i]))
-        copies[-1].start()
-    for copy in copies:
-        copy.wait()
+    for lo in range(0, feats, WIDTH):
+        cols = slice(lo, lo + WIDTH)
+        picked = jnp.dot(select, held[:, cols], preferred_element_type=F32).astype(BF16)
+        for j, ref in enumerate(out_refs):
+            ref[:, cols] = picked[j * per_dest : (j + 1) * per_dest]
 
 
 def prune_body(weight_ref, bits_ref, pruned_ref, kept_ref, keep_ref):
@@ -114,17 +111,17 @@
         keep_ref[:, cols] = keep.astype(BF16)
 
 
-def project_body(routed_ref, pruned_ref, part_ref, low_ref, routed_hbm=None, sem=None):
-    if sem is not None:
-        away = pltpu.make_async_copy(routed_ref, routed_hbm, sem)
-        away.start()
+def project_body(n_in, *refs):
+    blocks, pruned_ref, part_ref, low_ref, routed_ref = refs[:n_in], *refs[n_in:]
+    at = 0
+    for ref in blocks:
+        routed_ref[at : at + ref.shape[0], :] = ref[...]
+        at += ref.shape[0]
     part = lax.dot_general(
         pruned_ref[...], routed_ref[...], (((1,), (1,)), ((), ())), preferred_element_type=F32
     )
     part_ref[...] = part
     low_ref[...] = part.astype(BF16)
-    if sem is not None:
-        away.wait()
 
 
 def scale_body(*refs):
@@ -168,25 +165,23 @@
     return lax.ppermute(x, axis, [(i, (i + step) % n) for i in range(n)])
 
 
-def pack(first, blocks, tok_rows, top, feats, plane):
+def pack(experts, blocks, tok_rows, top, feats, dests):
     n_tok = sum(b.shape[0] for b in blocks)
     per_dest = n_tok // tok_rows * CAP
+    vmem = pl.BlockSpec(memory_space=pltpu.VMEM)
     return pl.pallas_call(
-        functools.partial(pack_body, tok_rows, top),
-        out_shape=shape(plane, per_dest, feats),
-        in_specs=[pl.BlockSpec(memory_space=pltpu.SMEM)]
-        + [pl.BlockSpec(memory_space=pltpu.VMEM)] * len(blocks),
-        out_specs=pl.BlockSpec(memory_space=pltpu.HBM),
-        scratch_shapes=[
-            pltpu.VMEM((n_tok, feats + LANES), BF16),
-            pltpu.VMEM((plane, per_dest, feats), BF16),
-            pltpu.SemaphoreType.DMA((feats // WIDTH,)),
-        ],
-        cost_estimate=pl.CostEstimate(
-            flops=1, bytes_accessed=1, transcendentals=0
-        ),
+        functools.partial(pack_body, tok_rows, top, len(blocks)),
+        out_shape=(shape(per_dest, feats),) * dests,
+        in_specs=[pl.BlockSpec(memory_space=pltpu.SMEM)] + [vmem] * len(blocks),
+        out_specs=(vmem,) * dests,
+        scratch_shapes=[pltpu.VMEM((n_tok, feats + LANES), BF16)],
+        cost_estimate=pl.CostEstimate(flops=1, bytes_accessed=1, transcendentals=0),
         compiler_params=pltpu.CompilerParams(vmem_limit_bytes=VMEM),
-    )(first, *blocks)
+    )(experts, *blocks)
+
+
+def after(x, *others):
+    return lax.optimization_barrier((x, *others))[0]
 
 
 def local(tokens, expert_ids, weight, mask_bits, damping):
@@ -194,9 +189,29 @@
     top = expert_ids.shape[1]
     slab = weight.shape[1]
     weight = weight.reshape(slab, feats)
-    me_z, me_core = lax.axis_index("z"), lax.axis_index("core")
-    plane = lax.axis_size("yh") * lax.axis_size("x")
-    first = (me_z * plane * 2 + me_core).astype(jnp.int32).reshape(1)
+    n_yh, n_x = lax.axis_size("yh"), lax.axis_size("x")
+    z, yh, x, core = (lax.axis_index(a) for a in ("z", "yh", "x", "core"))
+    steps = sorted(
+        ((dy, dx) for dy in range(n_yh) for dx in range(n_x)),
+        key=lambda s: (s[0] + min(s[1], n_x - s[1]), s),
+    )
+    experts = jnp.stack(
+        [
+            ((z * n_yh + (yh + dy) % n_yh) * n_x + (x + dx) % n_x) * lax.axis_size("core") + core
+            for dy, dx in steps
+        ]
+    ).astype(jnp.int32)
+
+    def send(rows, step):
+        dy, dx = step
+        pairs = [
+            (a * n_x + b, (a + dy) % n_yh * n_x + (b + dx) % n_x)
+            for a in range(n_yh)
+            for b in range(n_x)
+        ]
+        with jax.named_scope("route"):
+            return lax.ppermute(rows, ("yh", "x"), pairs)
+
     hbm, vmem = pl.BlockSpec(memory_space=pltpu.HBM), pl.BlockSpec(memory_space=pltpu.VMEM)
 
     with jax.named_scope("tag"):
@@ -214,50 +229,49 @@
 
     def packed(blocks):
         with jax.named_scope("pack"):
-            return pack(first, blocks, tok_rows, top, feats, plane)
-
-    def route(rows):
-        with jax.named_scope("route"):
-            block = lax.all_to_all(rows, ("yh", "x"), split_axis=0, concat_axis=0, tiled=True)
-        return block.reshape(-1, feats)
+            return pack(experts, blocks, tok_rows, top, feats, len(steps))
+
+    def swap(group):
+        with jax.named_scope("swap_core"):
+            return shift(group, "core", 1)
 
     with jax.named_scope("gather_near"):
         m1, p1, m2 = shift(own, "z", 1), shift(own, "z", -1), shift(own, "z", 2)
     with jax.named_scope("gather_far"):
-        p23 = shift(jnp.concatenate((own, p1)), "z", -2)
+        p23 = shift(after(jnp.concatenate((own, p1)), m1, m2), "z", -2)
         m34 = shift(jnp.concatenate((m1, m2)), "z", 2)
-
-    def swap(group):
-        with jax.named_scope("swap_core"):
-            return (*group, shift(jnp.concatenate(group), "core", 1))
-
-    routed1 = route(packed(swap((own, m1, p1, m2))))
-    routed2 = route(packed(swap((p23, m34))))
+    near = (own, m1, p1, m2)
+    rows1 = packed((*near, swap(jnp.concatenate(near))))
+    got1 = [rows1[0]] + [send(r, s) for r, s in zip(rows1[1:], steps[1:])]
+    far = after(jnp.concatenate((p23, m34)), *got1[1:GATE])
+    rows2 = packed((p23, m34, swap(far)))
+    got2 = [rows2[0]]
+    for k, (r, s) in enumerate(zip(rows2[1:], steps[1:])):
+        late = got1[GATE + k : GATE + k + 1]
+        got2.append(send(after(r, *late) if late else r, s))
     with jax.named_scope("prune"):
         pruned, kept, keep = call(
             prune_body, (shape(slab, feats),) * 3, (weight, mask_bits), 1 << 22
         )
 
-    def project(routed, away):
-        rows = routed.shape[0]
+    def project(blocks):
+        rows = sum(b.shape[0] for b in blocks)
         with jax.named_scope("project"):
             return pl.pallas_call(
-                project_body,
-                out_shape=(shape(slab, rows, dtype=F32), shape(slab, rows))
-                + ((shape(rows, feats),) if away else ()),
-                in_specs=[vmem, vmem],
-                out_specs=(vmem, vmem) + ((hbm,) if away else ()),
-                scratch_shapes=[pltpu.SemaphoreType.DMA] if away else [],
+                functools.partial(project_body, len(blocks)),
+                out_shape=(shape(slab, rows, dtype=F32), shape(slab, rows), shape(rows, feats)),
+                in_specs=[vmem] * (len(blocks) + 1),
+                out_specs=(vmem,) * 3,
                 cost_estimate=pl.CostEstimate(
                     flops=2 * rows * slab * feats, bytes_accessed=1 << 21, transcendentals=0
                 ),
                 compiler_params=pltpu.CompilerParams(vmem_limit_bytes=VMEM),
-            )(routed, pruned)
-
-    part1, low1, routed1 = project(routed1, True)
+            )(*blocks, pruned)
+
+    part1, low1, routed1 = project(got1)
     with jax.named_scope("swap_features"):
         other1 = shift(low1, "yl", 1)
-    part2, low2 = project(routed2, False)
+    part2, low2, routed2 = project(got2)
     with jax.named_scope("swap_features"):
         other2 = shift(low2, "yl", 1)
     with jax.named_scope("scale"):

time: 71.6 us -> 81.7 us (1.14)
  the two profiles are of different devices: /device:TPU:8 before, /device:TPU:32 now
where the time goes in v3:
time: 81.7 us; the launch traced here: 81.5 us
  starting transfers between devices  40.6 us (50%)
  waiting for transfers between devices  25.6 us (31%)
  Pallas kernels  9.36 us (11%)
  local copies, waits for them, and re-layouts  3.31 us (4%)
  other arithmetic  2.3 us (3%)
    ppermute x14, starting transfers between devices, send(): return lax.ppermute(rows, ('yh', 'x'), pairs)  29.2 us
    ppermute x9, waiting for transfers between devices, shift(): return lax.ppermute(x, axis, [(i, (i + step) % n) for i in range(n)])  18.2 us
    ppermute x9, starting transfers between devices, shift(): return lax.ppermute(x, axis, [(i, (i + step) % n) for i in range(n)])  11.4 us
    ppermute x14, waiting for transfers between devices, send(): return lax.ppermute(rows, ('yh', 'x'), pairs)  7.46 us
    pallas_call x2, Pallas kernels, pack(): pl.pallas_call(functools.partial(pack_body, tok_rows, top, len(blocks)),...  3.24 us
    unnamed x13, local copies, waits for them, and re-layouts  3.23 us
    pallas_call x2, Pallas kernels, project(): pl.pallas_call(functools.partial(project_body, len(blocks)), out_shape=(s...  2.27 us
    pallas_call x1, Pallas kernels, local(): pl.pallas_call(functools.partial(update_body, 2), out_shape=shape(slab, f...  2.05 us
  transfers between devices with their start and end apart: 23, of which 7 were waited for; matrix products, arithmetic and copies ran while one was open for 4% of the time, Pallas kernels for 9%

profile of v3, /device:TPU:32, one launch (start us, length us, event | category | flops | bytes accessed | tf_op | source)
XLA Modules:
  0.0 81.5 jit_solution(14470952638985824059)
XLA Ops:
  1.8 1.9 %collective-permute-start.1 = (bf16[16,3712]{1,0:T(8,128)(2,1)S(1)}, bf16[16,3712]{1,0:T(8,128)(2,1)S(1)}, u32[]{:S(2)}, u32[]{:S(2)}) collective-permute-start(bf16[16,3712]{1,0:T(8,128)(2,1)S(1)} %tag.1.refs_0_), channel_id=1, source_target_pairs={{0,224},{32,0},{64,32},{96,64},{128,96},{160,128},{192,160},{224,1... | collective-permute-start | bytes 356360 | tf_op jit(solution)/shard_map/gather_near/ppermute | solution.py:165
  3.8 1.5 %collective-permute-start.2 = (bf16[16,3712]{1,0:T(8,128)(2,1)S(1)}, bf16[16,3712]{1,0:T(8,128)(2,1)S(1)}, u32[]{:S(2)}, u32[]{:S(2)}) collective-permute-start(bf16[16,3712]{1,0:T(8,128)(2,1)S(1)} %tag.1.refs_0_), channel_id=1, source_target_pairs={{0,64},{32,96},{64,128},{96,160},{128,192},{160,224},{192,0},{224,... | collective-permute-start | bytes 356360 | tf_op jit(solution)/shard_map/gather_near/ppermute | solution.py:165
  5.3 3.1 %collective-permute-start = (bf16[16,3712]{1,0:T(8,128)(2,1)S(1)}, bf16[16,3712]{1,0:T(8,128)(2,1)S(1)}, u32[]{:S(2)}, u32[]{:S(2)}) collective-permute-start(bf16[16,3712]{1,0:T(8,128)(2,1)S(1)} %tag.1.refs_0_), channel_id=1, source_target_pairs={{0,32},{32,64},{64,96},{96,128},{128,160},{160,192},{192,224},{224... | collective-permute-start | bytes 356360 | tf_op jit(solution)/shard_map/gather_near/ppermute | solution.py:165
  9.1 3.9 %collective-permute-done.2.refs_3_ = bf16[16,3712]{1,0:T(8,128)(2,1)S(1)} collective-permute-done((bf16[16,3712]{1,0:T(8,128)(2,1)S(1)}, bf16[16,3712]{1,0:T(8,128)(2,1)S(1)}, u32[]{:S(2)}, u32[]{:S(2)}) %collective-permute-start.2) | collective-permute-done | bytes 118816 | tf_op jit(solution)/shard_map/gather_near/ppermute | solution.py:165
  13.1 2.9 %collective-permute-done.refs_1_ = bf16[16,3712]{1,0:T(8,128)(2,1)S(1)} collective-permute-done((bf16[16,3712]{1,0:T(8,128)(2,1)S(1)}, bf16[16,3712]{1,0:T(8,128)(2,1)S(1)}, u32[]{:S(2)}, u32[]{:S(2)}) %collective-permute-start) | collective-permute-done | bytes 118816 | tf_op jit(solution)/shard_map/gather_near/ppermute | solution.py:165
  15.9 3.4 %collective-permute-start.11 = (bf16[32,3712]{1,0:T(8,128)(2,1)}, bf16[32,3712]{1,0:T(8,128)(2,1)S(1)}, u32[]{:S(2)}, u32[]{:S(2)}) collective-permute-start(bf16[32,3712]{1,0:T(8,128)(2,1)} %pad_maximum_fusion.2), channel_id=1, source_target_pairs={{0,192},{32,224},{64,0},{96,32},{128,64},{160,96},{192,128},{224,1... | collective-permute-start | bytes 712712 | tf_op jit(solution)/shard_map/gather_far/ppermute | solution.py:165
  22.2 1.2 %pack.2 = (bf16[16,3584]{1,0:T(8,128)(2,1)S(1)}, bf16[16,3584]{1,0:T(8,128)(2,1)S(1)}, bf16[16,3584]{1,0:T(8,128)(2,1)S(1)}, bf16[16,3584]{1,0:T(8,128)(2,1)S(1)...) custom-call(s32[8]{0:T(128)S(1)} %stack.35.experts_ref, ...), custom_call_target="tpu_custom_call" | custom-call | flops 1 | bytes 1 | tf_op jit(solution)/shard_map/pack/pallas_call | solution.py:172
  23.4 1.6 %collective-permute-start.4 = (bf16[16,3584]{1,0:T(8,128)(2,1)S(1)}, bf16[16,3584]{1,0:T(8,128)(2,1)S(1)}, u32[]{:S(2)}, u32[]{:S(2)}) collective-permute-start(bf16[16,3584]{1,0:T(8,128)(2,1)S(1)} %get-tuple-element.37), channel_id=1, source_target_pairs={{0,4},{4,8},{8,12},{12,0},{16,20},{20,24},{24,28},{28,16},{1,5},{5... | collective-permute-start | bytes 344072 | tf_op jit(solution)/shard_map/route/ppermute | solution.py:213
  24.9 1.8 %collective-permute-start.5 = (bf16[16,3584]{1,0:T(8,128)(2,1)S(1)}, bf16[16,3584]{1,0:T(8,128)(2,1)S(1)}, u32[]{:S(2)}, u32[]{:S(2)}) collective-permute-start(bf16[16,3584]{1,0:T(8,128)(2,1)S(1)} %get-tuple-element.38), channel_id=1, source_target_pairs={{0,12},{4,0},{8,4},{12,8},{16,28},{20,16},{24,20},{28,24},{1,13},{... | collective-permute-start | bytes 344072 | tf_op jit(solution)/shard_map/route/ppermute | solution.py:213
  26.7 3.2 %collective-permute-start.6 = (bf16[16,3584]{1,0:T(8,128)(2,1)S(1)}, bf16[16,3584]{1,0:T(8,128)(2,1)S(1)}, u32[]{:S(2)}, u32[]{:S(2)}) collective-permute-start(bf16[16,3584]{1,0:T(8,128)(2,1)S(1)} %get-tuple-element.39), channel_id=1, source_target_pairs={{0,16},{4,20},{8,24},{12,28},{16,0},{20,4},{24,8},{28,12},{1,17},{... | collective-permute-start | bytes 344072 | tf_op jit(solution)/shard_map/route/ppermute | solution.py:213
  29.9 6.5 %collective-permute-done.12.refs_1_ = bf16[32,3712]{1,0:T(8,128)(2,1)S(1)} collective-permute-done((bf16[32,3712]{1,0:T(8,128)(2,1)}, bf16[32,3712]{1,0:T(8,128)(2,1)S(1)}, u32[]{:S(2)}, u32[]{:S(2)}) %collective-permute-start.12) | collective-permute-done | bytes 237600 | tf_op jit(solution)/shard_map/gather_far/ppermute | solution.py:165
  36.6 5.7 %collective-permute-start.10 = (bf16[16,3584]{1,0:T(8,128)(2,1)S(1)}, bf16[16,3584]{1,0:T(8,128)(2,1)S(1)}, u32[]{:S(2)}, u32[]{:S(2)}) collective-permute-start(bf16[16,3584]{1,0:T(8,128)(2,1)S(1)} %get-tuple-element.43), channel_id=1, source_target_pairs={{0,24},{4,28},{8,16},{12,20},{16,8},{20,12},{24,0},{28,4},{1,25},{... | collective-permute-start | bytes 344072 | tf_op jit(solution)/shard_map/route/ppermute | solution.py:213
  43.3 1.5 %collective-permute-start.7 = (bf16[16,3584]{1,0:T(8,128)(2,1)S(1)}, bf16[16,3584]{1,0:T(8,128)(2,1)S(1)}, u32[]{:S(2)}, u32[]{:S(2)}) collective-permute-start(bf16[16,3584]{1,0:T(8,128)(2,1)S(1)} %get-tuple-element.40), channel_id=1, source_target_pairs={{0,8},{4,12},{8,0},{12,4},{16,24},{20,28},{24,16},{28,20},{1,9},{5... | collective-permute-start | bytes 344072 | tf_op jit(solution)/shard_map/route/ppermute | solution.py:213
  44.8 2.0 %collective-permute-start.8 = (bf16[16,3584]{1,0:T(8,128)(2,1)S(1)}, bf16[16,3584]{1,0:T(8,128)(2,1)S(1)}, u32[]{:S(2)}, u32[]{:S(2)}) collective-permute-start(bf16[16,3584]{1,0:T(8,128)(2,1)S(1)} %get-tuple-element.41), channel_id=1, source_target_pairs={{0,20},{4,24},{8,28},{12,16},{16,4},{20,8},{24,12},{28,0},{1,21},{... | collective-permute-start | bytes 344072 | tf_op jit(solution)/shard_map/route/ppermute | solution.py:213
  46.8 2.0 %pack.3 = (bf16[16,3584]{1,0:T(8,128)(2,1)S(1)}, bf16[16,3584]{1,0:T(8,128)(2,1)}, bf16[16,3584]{1,0:T(8,128)(2,1)}, bf16[16,3584]{1,0:T(8,128)(2,1)S(1)}, bf16[...) custom-call(s32[8]{0:T(128)S(1)} %stack.35.experts_ref, ...), custom_call_target="tpu_custom_call" | custom-call | flops 1 | bytes 1 | tf_op jit(solution)/shard_map/pack/pallas_call | solution.py:172
  48.8 4.1 %collective-permute-start.17 = (bf16[16,3584]{1,0:T(8,128)(2,1)S(1)}, bf16[16,3584]{1,0:T(8,128)(2,1)S(1)}, u32[]{:S(2)}, u32[]{:S(2)}) collective-permute-start(bf16[16,3584]{1,0:T(8,128)(2,1)S(1)} %get-tuple-element.56), channel_id=1, source_target_pairs={{0,8},{4,12},{8,0},{12,4},{16,24},{20,28},{24,16},{28,20},{1,9},{5... | collective-permute-start | bytes 344072 | tf_op jit(solution)/shard_map/route/ppermute | solution.py:213
  53.6 2.3 %collective-permute-done.8.refs_5_ = bf16[16,3584]{1,0:T(8,128)(2,1)S(1)} collective-permute-done((bf16[16,3584]{1,0:T(8,128)(2,1)S(1)}, bf16[16,3584]{1,0:T(8,128)(2,1)S(1)}, u32[]{:S(2)}, u32[]{:S(2)}) %collective-permute-start.8) | collective-permute-done | bytes 114720 | tf_op jit(solution)/shard_map/route/ppermute | solution.py:213
  57.1 1.5 %collective-permute-start.14 = (bf16[16,3584]{1,0:T(8,128)(2,1)}, bf16[16,3584]{1,0:T(8,128)(2,1)S(1)}, u32[]{:S(2)}, u32[]{:S(2)}) collective-permute-start(bf16[16,3584]{1,0:T(8,128)(2,1)} %get-tuple-element.50), channel_id=1, source_target_pairs={{0,4},{4,8},{8,12},{12,0},{16,20},{20,24},{24,28},{28,16},{1,5},{5... | collective-permute-start | bytes 344072 | tf_op jit(solution)/shard_map/route/ppermute | solution.py:213
  59.2 5.0 %collective-permute-start.19 = (bf16[16,3584]{1,0:T(8,128)(2,1)}, bf16[16,3584]{1,0:T(8,128)(2,1)}, u32[]{:S(2)}, u32[]{:S(2)}) collective-permute-start(bf16[16,3584]{1,0:T(8,128)(2,1)} %get-tuple-element.58), channel_id=1, source_target_pairs={{0,28},{4,16},{8,20},{12,24},{16,12},{20,0},{24,4},{28,8},{1,29},{... | collective-permute-start | bytes 344072 | tf_op jit(solution)/shard_map/route/ppermute | solution.py:213
  65.3 1.3 %prune.1 = (bf16[256,3584]{1,0:T(8,128)(2,1)S(1)}, bf16[256,3584]{1,0:T(8,128)(2,1)S(1)}, bf16[256,3584]{1,0:T(8,128)(2,1)S(1)}) custom-call(bf16[256,3584]{1,0:T(8,128)(2,1)S(1)} %bitcast.11, s32[256,112]{1,0:T(8,128)S(1)} %copy.6.bits_ref), custom_call_target="tpu_custom_call" | custom-call | flops 4194304 | bytes 7454720 | tf_op jit(solution)/shard_map/prune/pallas_call | solution.py:25
  68.2 5.1 %collective-permute-done.20.refs_7_ = bf16[16,3584]{1,0:T(8,128)(2,1)} collective-permute-done((bf16[16,3584]{1,0:T(8,128)(2,1)}, bf16[16,3584]{1,0:T(8,128)(2,1)}, u32[]{:S(2)}, u32[]{:S(2)}) %collective-permute-start.20) | collective-permute-done | bytes 114720 | tf_op jit(solution)/shard_map/route/ppermute | solution.py:213
  73.3 1.6 %project.3 = (f32[256,128]{1,0:T(8,128)S(1)}, bf16[256,128]{1,0:T(8,128)(2,1)S(1)}, bf16[128,3584]{1,0:T(8,128)(2,1)S(1)}) custom-call(bf16[16,3584]{1,0:T(8,128)(2,1)S(1)} %get-tuple-element.48.refs_0_, bf16[16,3584]{1,0:T(8,128)(2,1)S(1)} %collective-permute-done.14.refs_1_, bf16[16,3584]{1,0:T(8,128)(2,1)S(1)} %collective-permute-done.15.refs_2_, ...), custom_call_target="tpu_custom_call" | custom-call | flops 234881024 | bytes 2097152 | tf_op jit(solution)/shard_map/project/pallas_call | solution.py:260
  75.7 3.6 %collective-permute-done.22.refs_3_ = bf16[256,128]{1,0:T(8,128)(2,1)S(1)} collective-permute-done((bf16[256,128]{1,0:T(8,128)(2,1)S(1)}, bf16[256,128]{1,0:T(8,128)(2,1)S(1)}, u32[]{:S(2)}, u32[]{:S(2)}) %collective-permute-start.22) | collective-permute-done | bytes 65568 | tf_op jit(solution)/shard_map/swap_features/ppermute | solution.py:165
  79.3 2.1 %update.1 = bf16[256,3584]{1,0:T(8,128)(2,1)} custom-call(f32[256,128]{1,0:T(8,128)S(1)} %get-tuple-element.45.refs_0_, f32[256,128]{1,0:T(8,128)S(1)} %get-tuple-element.60.refs_1_, bf16[256,128]{1,0:T(8,128)(2,1)S(1)} %collective-permute-done.21.refs_2_, bf16[256,128]{1,0:T(8,128)(2,1)S(1)} %collective-permute-done.22.refs_3_, ...), custom_call_target="tpu_custom_call" | custom-call | tf_op jit(solution)/shard_map/update/pallas_call | solution.py:283
  (48 shorter events, 12.3 us)
Async XLA Ops:
  1.8 6.6 %collective-permute-start.1 = (bf16[16,3712]{1,0:T(8,128)(2,1)S(1)}, bf16[16,3712]{1,0:T(8,128)(2,1)S(1)}, u32[]{:S(2)}, u32[]{:S(2)}) collective-permute-start(bf16[16,3712]{1,0:T(8,128)(2,1)S(1)} %tag.1.refs_0_), channel_id=1, source_target_pairs={{0,224},{32,0},{64,32},{96,64},{128,96},{160,128},{192,160},{224,1... | collective-permute-start | bytes 356360 | tf_op jit(solution)/shard_map/gather_near/ppermute | solution.py:165
  3.8 9.3 %collective-permute-start.2 = (bf16[16,3712]{1,0:T(8,128)(2,1)S(1)}, bf16[16,3712]{1,0:T(8,128)(2,1)S(1)}, u32[]{:S(2)}, u32[]{:S(2)}) collective-permute-start(bf16[16,3712]{1,0:T(8,128)(2,1)S(1)} %tag.1.refs_0_), channel_id=1, source_target_pairs={{0,64},{32,96},{64,128},{96,160},{128,192},{160,224},{192,0},{224,... | collective-permute-start | bytes 356360 | tf_op jit(solution)/shard_map/gather_near/ppermute | solution.py:165
  5.3 10.6 %collective-permute-start = (bf16[16,3712]{1,0:T(8,128)(2,1)S(1)}, bf16[16,3712]{1,0:T(8,128)(2,1)S(1)}, u32[]{:S(2)}, u32[]{:S(2)}) collective-permute-start(bf16[16,3712]{1,0:T(8,128)(2,1)S(1)} %tag.1.refs_0_), channel_id=1, source_target_pairs={{0,32},{32,64},{64,96},{96,128},{128,160},{160,192},{192,224},{224... | collective-permute-start | bytes 356360 | tf_op jit(solution)/shard_map/gather_near/ppermute | solution.py:165
  15.9 14.0 %collective-permute-start.11 = (bf16[32,3712]{1,0:T(8,128)(2,1)}, bf16[32,3712]{1,0:T(8,128)(2,1)S(1)}, u32[]{:S(2)}, u32[]{:S(2)}) collective-permute-start(bf16[32,3712]{1,0:T(8,128)(2,1)} %pad_maximum_fusion.2), channel_id=1, source_target_pairs={{0,192},{32,224},{64,0},{96,32},{128,64},{160,96},{192,128},{224,1... | collective-permute-start | bytes 712712 | tf_op jit(solution)/shard_map/gather_far/ppermute | solution.py:165
  20.1 45.2 %copy-start = (bf16[1,256,3584]{2,1,0:T(8,128)(2,1)S(1)}, bf16[1,256,3584]{2,1,0:T(8,128)(2,1)}, u32[]{:S(2)}) copy-start(bf16[1,256,3584]{2,1,0:T(8,128)(2,1)} %param.7) | copy-start | bytes 5505028
  20.1 2.1 %collective-permute-start.3 = (bf16[64,3712]{1,0:T(8,128)(2,1)}, bf16[64,3712]{1,0:T(8,128)(2,1)S(1)}, u32[]{:S(2)}, u32[]{:S(2)}) collective-permute-start(bf16[64,3712]{1,0:T(8,128)(2,1)} %pad_maximum_fusion), channel_id=1, source_target_pairs={{0,2},{2,0},{1,3},{3,1},{4,6},{6,4},{5,7},{7,5},{8,10},{10,8},{9,1... | collective-permute-start | bytes 1425416 | tf_op jit(solution)/shard_map/swap_core/ppermute | solution.py:165
  20.8 15.6 %collective-permute-start.12 = (bf16[32,3712]{1,0:T(8,128)(2,1)}, bf16[32,3712]{1,0:T(8,128)(2,1)S(1)}, u32[]{:S(2)}, u32[]{:S(2)}) collective-permute-start(bf16[32,3712]{1,0:T(8,128)(2,1)} %pad_maximum_fusion.3), channel_id=1, source_target_pairs={{0,64},{32,96},{64,128},{96,160},{128,192},{160,224},{192,0},{224,... | collective-permute-start | bytes 712712 | tf_op jit(solution)/shard_map/gather_far/ppermute | solution.py:165
  23.4 13.1 %collective-permute-start.4 = (bf16[16,3584]{1,0:T(8,128)(2,1)S(1)}, bf16[16,3584]{1,0:T(8,128)(2,1)S(1)}, u32[]{:S(2)}, u32[]{:S(2)}) collective-permute-start(bf16[16,3584]{1,0:T(8,128)(2,1)S(1)} %get-tuple-element.37), channel_id=1, source_target_pairs={{0,4},{4,8},{8,12},{12,0},{16,20},{20,24},{24,28},{28,16},{1,5},{5... | collective-permute-start | bytes 344072 | tf_op jit(solution)/shard_map/route/ppermute | solution.py:213
  24.9 11.5 %collective-permute-start.5 = (bf16[16,3584]{1,0:T(8,128)(2,1)S(1)}, bf16[16,3584]{1,0:T(8,128)(2,1)S(1)}, u32[]{:S(2)}, u32[]{:S(2)}) collective-permute-start(bf16[16,3584]{1,0:T(8,128)(2,1)S(1)} %get-tuple-element.38), channel_id=1, source_target_pairs={{0,12},{4,0},{8,4},{12,8},{16,28},{20,16},{24,20},{28,24},{1,13},{... | collective-permute-start | bytes 344072 | tf_op jit(solution)/shard_map/route/ppermute | solution.py:213
  26.7 9.8 %collective-permute-start.6 = (bf16[16,3584]{1,0:T(8,128)(2,1)S(1)}, bf16[16,3584]{1,0:T(8,128)(2,1)S(1)}, u32[]{:S(2)}, u32[]{:S(2)}) collective-permute-start(bf16[16,3584]{1,0:T(8,128)(2,1)S(1)} %get-tuple-element.39), channel_id=1, source_target_pairs={{0,16},{4,20},{8,24},{12,28},{16,0},{20,4},{24,8},{28,12},{1,17},{... | collective-permute-start | bytes 344072 | tf_op jit(solution)/shard_map/route/ppermute | solution.py:213
  36.5 10.3 %collective-permute-start.13 = (bf16[64,3712]{1,0:T(8,128)(2,1)S(1)}, bf16[64,3712]{1,0:T(8,128)(2,1)S(1)}, u32[]{:S(2)}, u32[]{:S(2)}) collective-permute-start(bf16[64,3712]{1,0:T(8,128)(2,1)S(1)} %pad_maximum_fusion.1), channel_id=1, source_target_pairs={{0,2},{2,0},{1,3},{3,1},{4,6},{6,4},{5,7},{7,5},{8,10},{10,8},{9,1... | collective-permute-start | bytes 1425416 | tf_op jit(solution)/shard_map/swap_core/ppermute | solution.py:165
  36.6 12.2 %collective-permute-start.10 = (bf16[16,3584]{1,0:T(8,128)(2,1)S(1)}, bf16[16,3584]{1,0:T(8,128)(2,1)S(1)}, u32[]{:S(2)}, u32[]{:S(2)}) collective-permute-start(bf16[16,3584]{1,0:T(8,128)(2,1)S(1)} %get-tuple-element.43), channel_id=1, source_target_pairs={{0,24},{4,28},{8,16},{12,20},{16,8},{20,12},{24,0},{28,4},{1,25},{... | collective-permute-start | bytes 344072 | tf_op jit(solution)/shard_map/route/ppermute | solution.py:213
  42.3 10.6 %collective-permute-start.9 = (bf16[16,3584]{1,0:T(8,128)(2,1)S(1)}, bf16[16,3584]{1,0:T(8,128)(2,1)S(1)}, u32[]{:S(2)}, u32[]{:S(2)}) collective-permute-start(bf16[16,3584]{1,0:T(8,128)(2,1)S(1)} %get-tuple-element.42), channel_id=1, source_target_pairs={{0,28},{4,16},{8,20},{12,24},{16,12},{20,0},{24,4},{28,8},{1,29},{... | collective-permute-start | bytes 344072 | tf_op jit(solution)/shard_map/route/ppermute | solution.py:213
  43.3 10.3 %collective-permute-start.7 = (bf16[16,3584]{1,0:T(8,128)(2,1)S(1)}, bf16[16,3584]{1,0:T(8,128)(2,1)S(1)}, u32[]{:S(2)}, u32[]{:S(2)}) collective-permute-start(bf16[16,3584]{1,0:T(8,128)(2,1)S(1)} %get-tuple-element.40), channel_id=1, source_target_pairs={{0,8},{4,12},{8,0},{12,4},{16,24},{20,28},{24,16},{28,20},{1,9},{5... | collective-permute-start | bytes 344072 | tf_op jit(solution)/shard_map/route/ppermute | solution.py:213
  44.8 11.1 %collective-permute-start.8 = (bf16[16,3584]{1,0:T(8,128)(2,1)S(1)}, bf16[16,3584]{1,0:T(8,128)(2,1)S(1)}, u32[]{:S(2)}, u32[]{:S(2)}) collective-permute-start(bf16[16,3584]{1,0:T(8,128)(2,1)S(1)} %get-tuple-element.41), channel_id=1, source_target_pairs={{0,20},{4,24},{8,28},{12,16},{16,4},{20,8},{24,12},{28,0},{1,21},{... | collective-permute-start | bytes 344072 | tf_op jit(solution)/shard_map/route/ppermute | solution.py:213
  48.8 10.4 %collective-permute-start.17 = (bf16[16,3584]{1,0:T(8,128)(2,1)S(1)}, bf16[16,3584]{1,0:T(8,128)(2,1)S(1)}, u32[]{:S(2)}, u32[]{:S(2)}) collective-permute-start(bf16[16,3584]{1,0:T(8,128)(2,1)S(1)} %get-tuple-element.56), channel_id=1, source_target_pairs={{0,8},{4,12},{8,0},{12,4},{16,24},{20,28},{24,16},{28,20},{1,9},{5... | collective-permute-start | bytes 344072 | tf_op jit(solution)/shard_map/route/ppermute | solution.py:213
  52.9 11.3 %collective-permute-start.16 = (bf16[16,3584]{1,0:T(8,128)(2,1)S(1)}, bf16[16,3584]{1,0:T(8,128)(2,1)S(1)}, u32[]{:S(2)}, u32[]{:S(2)}) collective-permute-start(bf16[16,3584]{1,0:T(8,128)(2,1)S(1)} %get-tuple-element.54), channel_id=1, source_target_pairs={{0,16},{4,20},{8,24},{12,28},{16,0},{20,4},{24,8},{28,12},{1,17},{... | collective-permute-start | bytes 344072 | tf_op jit(solution)/shard_map/route/ppermute | solution.py:213
  56.5 10.8 %collective-permute-start.15 = (bf16[16,3584]{1,0:T(8,128)(2,1)}, bf16[16,3584]{1,0:T(8,128)(2,1)S(1)}, u32[]{:S(2)}, u32[]{:S(2)}) collective-permute-start(bf16[16,3584]{1,0:T(8,128)(2,1)} %get-tuple-element.52), channel_id=1, source_target_pairs={{0,12},{4,0},{8,4},{12,8},{16,28},{20,16},{24,20},{28,24},{1,13},{... | collective-permute-start | bytes 344072 | tf_op jit(solution)/shard_map/route/ppermute | solution.py:213
  57.1 11.1 %collective-permute-start.14 = (bf16[16,3584]{1,0:T(8,128)(2,1)}, bf16[16,3584]{1,0:T(8,128)(2,1)S(1)}, u32[]{:S(2)}, u32[]{:S(2)}) collective-permute-start(bf16[16,3584]{1,0:T(8,128)(2,1)} %get-tuple-element.50), channel_id=1, source_target_pairs={{0,4},{4,8},{8,12},{12,0},{16,20},{20,24},{24,28},{28,16},{1,5},{5... | collective-permute-start | bytes 344072 | tf_op jit(solution)/shard_map/route/ppermute | solution.py:213
  58.6 9.6 %collective-permute-start.18 = (bf16[16,3584]{1,0:T(8,128)(2,1)}, bf16[16,3584]{1,0:T(8,128)(2,1)}, u32[]{:S(2)}, u32[]{:S(2)}) collective-permute-start(bf16[16,3584]{1,0:T(8,128)(2,1)} %get-tuple-element.57), channel_id=1, source_target_pairs={{0,20},{4,24},{8,28},{12,16},{16,4},{20,8},{24,12},{28,0},{1,21},{... | collective-permute-start | bytes 344072 | tf_op jit(solution)/shard_map/route/ppermute | solution.py:213
  59.2 9.0 %collective-permute-start.19 = (bf16[16,3584]{1,0:T(8,128)(2,1)}, bf16[16,3584]{1,0:T(8,128)(2,1)}, u32[]{:S(2)}, u32[]{:S(2)}) collective-permute-start(bf16[16,3584]{1,0:T(8,128)(2,1)} %get-tuple-element.58), channel_id=1, source_target_pairs={{0,28},{4,16},{8,20},{12,24},{16,12},{20,0},{24,4},{28,8},{1,29},{... | collective-permute-start | bytes 344072 | tf_op jit(solution)/shard_map/route/ppermute | solution.py:213
  64.2 9.1 %collective-permute-start.20 = (bf16[16,3584]{1,0:T(8,128)(2,1)}, bf16[16,3584]{1,0:T(8,128)(2,1)}, u32[]{:S(2)}, u32[]{:S(2)}) collective-permute-start(bf16[16,3584]{1,0:T(8,128)(2,1)} %get-tuple-element.59), channel_id=1, source_target_pairs={{0,24},{4,28},{8,16},{12,20},{16,8},{20,12},{24,0},{28,4},{1,25},{... | collective-permute-start | bytes 344072 | tf_op jit(solution)/shard_map/route/ppermute | solution.py:213
  67.3 8.4 %collective-permute-start.21 = (bf16[256,128]{1,0:T(8,128)(2,1)S(1)}, bf16[256,128]{1,0:T(8,128)(2,1)S(1)}, u32[]{:S(2)}, u32[]{:S(2)}) collective-permute-start(bf16[256,128]{1,0:T(8,128)(2,1)S(1)} %get-tuple-element.61), channel_id=1, source_target_pairs={{0,1},{1,0},{2,3},{3,2},{4,5},{5,4},{6,7},{7,6},{8,9},{9,8},{10,11... | collective-permute-start | bytes 196616 | tf_op jit(solution)/shard_map/swap_features/ppermute | solution.py:165
  75.0 4.4 %collective-permute-start.22 = (bf16[256,128]{1,0:T(8,128)(2,1)S(1)}, bf16[256,128]{1,0:T(8,128)(2,1)S(1)}, u32[]{:S(2)}, u32[]{:S(2)}) collective-permute-start(bf16[256,128]{1,0:T(8,128)(2,1)S(1)} %get-tuple-element.62), channel_id=1, source_target_pairs={{0,1},{1,0},{2,3},{3,2},{4,5},{5,4},{6,7},{7,6},{8,9},{9,8},{10,11... | collective-permute-start | bytes 196616 | tf_op jit(solution)/shard_map/swap_features/ppermute | solution.py:165
  (5 other events, 20.5 us)

commit v4 on v2

v4 whole, which is shorter than its diff:
```python
import functools

import jax
import jax.numpy as jnp
from jax import lax
from jax.experimental import pallas as pl
from jax.experimental.pallas import tpu as pltpu
from jax.sharding import Mesh, PartitionSpec as P

ROWS_E = 128
ETA = 0.5
CAP = 2
LANES = 128
WIDTH = 896
VMEM = 16 * 2**20
F32 = jnp.float32
BF16 = jnp.bfloat16


def call(body, out_shape, operands, flops, scratch=(), name=None):
    size = sum(o.size * o.dtype.itemsize for o in operands)
    outs = jax.tree.leaves(out_shape)
    size += sum(o.size * o.dtype.itemsize for o in outs)
    return pl.pallas_call(
        body,
        out_shape=out_shape,
        in_specs=[pl.BlockSpec(memory_space=pltpu.VMEM)] * len(operands),
        out_specs=jax.tree.map(lambda _: pl.BlockSpec(memory_space=pltpu.VMEM), out_shape),
        scratch_shapes=list(scratch),
        cost_estimate=pl.CostEstimate(flops=flops, bytes_accessed=size, transcendentals=0),
        compiler_params=pltpu.CompilerParams(vmem_limit_bytes=VMEM),
        name=name,
    )(*operands)


def tag_body(tokens_hbm, ids_hbm, out_ref, ids_ref, sems):
    feats = tokens_hbm.shape[1]
    top = ids_ref.shape[0]
    get_ids = pltpu.make_async_copy(ids_hbm, ids_ref, sems.at[0])
    get_tokens = pltpu.make_async_copy(tokens_hbm, out_ref.at[:, pl.ds(0, feats)], sems.at[1])
    get_ids.start()
    get_tokens.start()
    spread = (
        lax.broadcasted_iota(jnp.int32, (top, LANES), 0)
        == lax.broadcasted_iota(jnp.int32, (top, LANES), 1)
    ).astype(BF16)
    get_ids.wait()
    ids = ids_ref[...].astype(F32).astype(BF16)
    out_ref[:, feats:] = lax.dot_general(
        ids, spread, (((0,), (0,)), ((), ())), preferred_element_type=F32
    ).astype(BF16)
    get_tokens.wait()


def pack_body(tok_rows, top, first_ref, held, out_hbm, out_ref, sems):
    rows, feats = out_ref.shape
    tokens = held.shape[0]
    per_dest = tokens // tok_rows * CAP
    pick = (
        lax.broadcasted_iota(jnp.int32, (top, LANES), 0)
        == lax.broadcasted_iota(jnp.int32, (top, LANES), 1)
    ).astype(BF16)
    ids = lax.dot_general(
        pick, held[:, feats:], (((1,), (1,)), ((), ())), preferred_element_type=F32
    )
    row = lax.broadcasted_iota(jnp.int32, (rows, 1), 0)
    expert = (first_ref[0] + row // per_dest).astype(F32)
    block = (row % per_dest) // CAP
    slot = (row % CAP).astype(F32)
    tok = lax.broadcasted_iota(jnp.int32, (1, tokens), 1)
    named = ids[0:1, :] == expert
    for k in range(1, top):
        named = named | (ids[k : k + 1, :] == expert)
    named = named & (tok // tok_rows == block)
    member = jnp.where(named, 1.0, 0.0)
    before = (
        lax.broadcasted_iota(jnp.int32, (tokens, tokens), 0)
        < lax.broadcasted_iota(jnp.int32, (tokens, tokens), 1)
    ).astype(BF16)
    rank = jnp.dot(member.astype(BF16), before, preferred_element_type=F32)
    select = jnp.where(rank == slot, member, 0.0).astype(BF16)
    copies = []
    for i, lo in enumerate(range(0, feats, WIDTH)):
        cols = (slice(None), pl.ds(lo, WIDTH))
        out_ref[cols] = jnp.dot(select, held[cols], preferred_element_type=F32).astype(BF16)
        copies.append(pltpu.make_async_copy(out_ref.at[cols], out_hbm.at[cols], sems.at[i]))
        copies[-1].start()
    for copy in copies:
        copy.wait()


def prune_body(weight_ref, bits_ref, *refs):
    *pruned_refs, kept_ref, keep_ref = refs
    rows, words = bits_ref.shape
    feats = weight_ref.shape[1]
    lane = lax.broadcasted_iota(jnp.int32, (rows, LANES), 1)
    bits = jnp.concatenate([bits_ref[...], jnp.zeros((rows, LANES - words), jnp.int32)], axis=1)
    for j in range(feats // LANES):
        word = jnp.take_along_axis(bits, lane // 32 + 4 * j, axis=1, mode="promise_in_bounds")
        keep = jnp.bitwise_and(jnp.right_shift(word, lane % 32), 1).astype(F32)
        cols = slice(j * LANES, (j + 1) * LANES)
        slab = weight_ref[:, cols].astype(F32)
        piece, at = divmod(j * LANES, WIDTH)
        pruned_refs[piece][:, at : at + LANES] = jnp.where(keep > 0.5, 0.0, slab).astype(BF16)
        kept_ref[:, cols] = jnp.where(keep > 0.5, slab, 0.0).astype(BF16)
        keep_ref[:, cols] = keep.astype(BF16)


def project_body(routed_ref, *refs):
    *pruned_refs, part_ref, low_ref = refs
    part = None
    for i, ref in enumerate(pruned_refs):
        term = lax.dot_general(
            ref[...],
            routed_ref[:, i * WIDTH : (i + 1) * WIDTH],
            (((1,), (1,)), ((), ())),
            preferred_element_type=F32,
        )
        part = term if part is None else part + term
    part_ref[...] = part
    low_ref[...] = part.astype(BF16)


def scale_body(*refs):
    *routed_refs, damping_ref, scale_ref = refs
    feats = damping_ref.shape[1]
    for lo in range(0, feats, WIDTH):
        cols = slice(lo, lo + WIDTH)
        diag = damping_ref[:, cols]
        for ref in routed_refs:
            rows = ref[:, cols].astype(F32)
            diag = diag + jnp.sum(rows * rows, axis=0, keepdims=True) * (1.0 / ROWS_E)
        scale_ref[:, cols] = (ETA / ROWS_E) / diag


def update_body(n, *refs):
    parts, others, routed_refs = refs[:n], refs[n : 2 * n], refs[2 * n : 3 * n]
    scale_ref, kept_ref, keep_ref, out_hbm, out_ref, sems = refs[3 * n :]
    feats = kept_ref.shape[1]
    projected = [(p[...] + o[...].astype(F32)).astype(BF16) for p, o in zip(parts, others)]
    copies = []
    for i, lo in enumerate(range(0, feats, WIDTH)):
        cols = slice(lo, lo + WIDTH)
        comp = jnp.dot(projected[0], routed_refs[0][:, cols], preferred_element_type=F32)
        for p, r in zip(projected[1:], routed_refs[1:]):
            comp = comp + jnp.dot(p, r[:, cols], preferred_element_type=F32)
        gain = keep_ref[:, cols].astype(F32) * (comp * scale_ref[:, cols])
        out_ref[:, cols] = (kept_ref[:, cols].astype(F32) + gain).astype(BF16)
        cols = (slice(None), pl.ds(lo, WIDTH))
        copies.append(pltpu.make_async_copy(out_ref.at[cols], out_hbm.at[cols], sems.at[i]))
        copies[-1].start()
    for copy in copies:
        copy.wait()


def shape(*dims, dtype=BF16):
    return jax.ShapeDtypeStruct(dims, dtype)


def shift(x, axis, step):
    n = lax.axis_size(axis)
    return lax.ppermute(x, axis, [(i, (i + step) % n) for i in range(n)])


def local(tokens, expert_ids, weight, mask_bits, damping):
    tok_rows, feats = tokens.shape
    top = expert_ids.shape[1]
    slab = weight.shape[1]
    weight = weight.reshape(slab, feats)
    near = ("zl", "yh", "x", "core")
    dests = lax.axis_size(near)
    n_tok = tok_rows * lax.axis_size("zh")
    rows = dests * lax.axis_size("zh") * CAP
    pieces = feats // WIDTH
    first = (lax.axis_index("zh") * dests).astype(jnp.int32).reshape(1)
    hbm, vmem = pl.BlockSpec(memory_space=pltpu.HBM), pl.BlockSpec(memory_space=pltpu.VMEM)
    params = pltpu.CompilerParams(vmem_limit_bytes=VMEM)

    with jax.named_scope("tag"):
        own = pl.pallas_call(
            tag_body,
            out_shape=shape(tok_rows, feats + LANES),
            in_specs=[hbm, hbm],
            out_specs=vmem,
            scratch_shapes=[
                pltpu.VMEM((top, tok_rows), jnp.int32),
                pltpu.SemaphoreType.DMA((2,)),
            ],
            compiler_params=params,
        )(tokens, expert_ids.T)
    with jax.named_scope("gather"):
        held = lax.all_gather(own, "zh", tiled=True)
    with jax.named_scope("pack"):
        packed = pl.pallas_call(
            functools.partial(pack_body, tok_rows, top),
            out_shape=pltpu.HBM((rows, feats), BF16),
            in_specs=[pl.BlockSpec(memory_space=pltpu.SMEM), vmem],
            out_specs=hbm,
            scratch_shapes=[pltpu.VMEM((rows, feats), BF16), pltpu.SemaphoreType.DMA((pieces,))],
            compiler_params=params,
        )(first, held)
    with jax.named_scope("route"):
        block = lax.all_to_all(
            packed.reshape(dests, -1, feats), near, split_axis=0, concat_axis=0, tiled=True
        )
    routed = block.reshape(rows, feats)
    with jax.named_scope("prune"):
        *pruned, kept, keep = call(
            prune_body,
            (shape(slab, WIDTH),) * pieces + (shape(slab, feats),) * 2,
            (weight, mask_bits),
            1 << 22,
        )
    with jax.named_scope("project"):
        part, low = call(
            project_body,
            (shape(slab, rows, dtype=F32), shape(slab, rows)),
            (routed, *pruned),
            2 * rows * slab * feats,
        )
    with jax.named_scope("swap_features"):
        other = shift(low, "yl", 1)
    with jax.named_scope("scale"):
        scale = call(
            scale_body, shape(1, feats, dtype=F32), (routed, damping), 4 * slab * feats
        )
    with jax.named_scope("update"):
        operands = (part, other, routed, scale, kept, keep)
        out = pl.pallas_call(
            functools.partial(update_body, 1),
            out_shape=shape(slab, feats),
            in_specs=[vmem] * len(operands),
            out_specs=hbm,
            scratch_shapes=[pltpu.VMEM((slab, feats), BF16), pltpu.SemaphoreType.DMA((pieces,))],
            compiler_params=params,
        )(*operands)
    return out.reshape(1, slab, feats)


def solution(mesh):
    n_hrow, n_hcol = mesh.shape["hrow"], mesh.shape["hcol"]
    n_expert = mesh.shape["expert"]
    fine = Mesh(
        mesh.devices.reshape(n_expert // 4, 2, 2, n_hrow // 2, 2, n_hcol),
        ("zh", "zl", "yh", "x", "core", "yl"),
    )
    own = ("zh", "zl", "yh", "x", "core")
    in_specs = (P(own, "yl"), P(own, None), P(own, None, "yl"), P(None, "yl"), P(own, "yl"))
    return jax.shard_map(
        local, mesh=fine, in_specs=in_specs, out_specs=P(own, None, "yl"), check_vma=False
    )
```

time: 71.6 us -> 67.3 us (0.940)
  blocking collectives: 0 us -> 19.7 us
  starting transfers between devices: 21.6 us -> 8.59 us
  waiting for transfers between devices: 34.2 us -> 24.4 us
  Pallas kernels: 8.33 us -> 5.93 us
  local copies, waits for them, and re-layouts: 6.37 us -> 7.49 us
    all_gather x0 -> x1, blocking collectives: none -> 19.7 us  [local(): held = lax.all_gather(own, 'zh', tiled=True)]
    ppermute x9 -> x1, waiting for transfers between devices: 19.3 us -> 3.67 us  [shift(): return lax.ppermute(x, axis, [(i, (i + step) % n) for i in range(n)])]
    ppermute x9 -> x1, starting transfers between devices: 12 us -> 1.44 us  [shift(): return lax.ppermute(x, axis, [(i, (i + step) % n) for i in range(n)])]
    all_to_all x2 -> x1, waiting for transfers between devices: 14.9 us -> 20.7 us  [local(): lax.all_to_all(packed.reshape(dests, -1, feats), near, split_axis=0, conc...]
    pallas_call x5 -> x2, Pallas kernels: 6.54 us -> 3.5 us  [the longest x1 1.82 us: local(): pl.pallas_call(functools.partial(pack_body, tok_rows, top), out_shape=plt...]
    all_to_all x2 -> x1, starting transfers between devices: 9.6 us -> 7.16 us  [local(): lax.all_to_all(packed.reshape(dests, -1, feats), near, split_axis=0, conc...]
    unnamed x27 -> x23, local copies, waits for them, and re-layouts: 6.37 us -> 7.49 us
    pallas_call x2 -> x3, Pallas kernels: 1.54 us -> 2.19 us  [call(): pl.pallas_call(body, out_shape=out_shape, in_specs=[pl.BlockSpec(memory_s...]
  transfers between devices with their start and end apart: 11 -> 2, of which waited for: 8 -> 2; matrix products, arithmetic and copies ran while one was open for 0% -> 0% of each run, Pallas kernels for 9% -> 2%
where the time goes in v4:
time: 67.3 us; the launch traced here: 66.2 us
  waiting for transfers between devices  24.4 us (36%)
  blocking collectives  19.7 us (29%)
  starting transfers between devices  8.59 us (13%)
  local copies, waits for them, and re-layouts  7.49 us (11%)
  Pallas kernels  5.93 us (9%)
    all_to_all x1, waiting for transfers between devices, local(): lax.all_to_all(packed.reshape(dests, -1, feats), near, split_axis=0, conc...  20.7 us
    all_gather x1, blocking collectives, local(): held = lax.all_gather(own, 'zh', tiled=True)  19.7 us
    unnamed x23, local copies, waits for them, and re-layouts  7.49 us
    all_to_all x1, starting transfers between devices, local(): lax.all_to_all(packed.reshape(dests, -1, feats), near, split_axis=0, conc...  7.16 us
    ppermute x1, waiting for transfers between devices, shift(): return lax.ppermute(x, axis, [(i, (i + step) % n) for i in range(n)])  3.67 us
    pallas_call x3, Pallas kernels, call(): pl.pallas_call(body, out_shape=out_shape, in_specs=[pl.BlockSpec(memory_s...  2.19 us
    pallas_call x1, Pallas kernels, local(): pl.pallas_call(functools.partial(pack_body, tok_rows, top), out_shape=plt...  1.82 us
    pallas_call x1, Pallas kernels, local(): pl.pallas_call(functools.partial(update_body, 1), out_shape=shape(slab, f...  1.68 us
  transfers between devices with their start and end apart: 2, of which 2 were waited for; matrix products, arithmetic and copies ran while one was open for 0% of the time, Pallas kernels for 2%

profile of v4, /device:TPU:8, one launch (start us, length us, event | category | flops | bytes accessed | tf_op | source)
XLA Modules:
  0.0 66.2 jit_solution(11638795107833125014)
XLA Ops:
  0.0 0.9 %copy-done.7 = bf16[16,3584]{1,0:T(8,128)(2,1)S(1)} copy-done((bf16[16,3584]{1,0:T(8,128)(2,1)S(1)}, bf16[16,3584]{1,0:T(8,128)(2,1)}, u32[]{:S(2)}) %copy-start.7) | copy-done | bytes 114712
  0.9 0.7 %copy-done.9 = s32[16,8]{0,1:T(8,128)S(1)} copy-done((s32[16,8]{0,1:T(8,128)S(1)}, s32[16,8]{0,1:T(8,128)}, u32[]{:S(2)}) %copy-start.9) | copy-done | bytes 536
  1.6 0.2 tag.1
  1.8 19.7 %all_gather.3.held = bf16[64,3712]{1,0:T(8,128)(2,1)S(1)} all-gather(bf16[16,3712]{1,0:T(8,128)(2,1)S(1)} %tag.1), channel_id=1, replica_groups=mesh['zh'=4,'zl'=2,'yh'=2,'x'=4,'core'=2,'yl'=2] {'zh'}, dimensions={0}, use_global_device_ids=true | all-gather | bytes 593920 | tf_op jit(solution)/shard_map/gather/all_gather | solution.py:192
  21.5 1.8 %pack.1 = bf16[256,3584]{1,0:T(8,128)(2,1)} custom-call(s32[1]{0:T(128)} %bitcast.first_ref, bf16[64,3712]{1,0:T(8,128)(2,1)S(1)} %all_gather.3.held), custom_call_target="tpu_custom_call" | custom-call | tf_op jit(solution)/shard_map/pack/pallas_call | solution.py:194
  23.3 0.0 copy-start.10
  23.3 7.2 %all-to-all-start = ((bf16[32,8,3584]{2,1,0:T(8,128)(2,1)}), bf16[32,8,3584]{2,1,0:T(8,128)(2,1)S(1)}, u32[]{:S(2)}, u32[]{:S(2)}) async-start(bf16[32,8,3584]{2,1,0:T(8,128)(2,1)} %bitcast.11), calls=%async_computation | async-start | bytes 3670016 | tf_op jit(solution)/shard_map/route/all_to_all | solution.py:203
  30.5 0.1 copy.6.bits_ref
  30.6 0.0 copy-start
  30.6 1.5 %copy-done = bf16[1,256,3584]{2,1,0:T(8,128)(2,1)S(1)} copy-done((bf16[1,256,3584]{2,1,0:T(8,128)(2,1)S(1)}, bf16[1,256,3584]{2,1,0:T(8,128)(2,1)}, u32[]{:S(2)}) %copy-start) | copy-done | bytes 1835032
  32.1 1.3 %prune.1 = (bf16[256,896]{1,0:T(8,128)(2,1)S(1)}, bf16[256,896]{1,0:T(8,128)(2,1)S(1)}, bf16[256,896]{1,0:T(8,128)(2,1)S(1)}, bf16[256,896]{1,0:T(8,128)(2,1)S(1...) custom-call(bf16[256,3584]{1,0:T(8,128)(2,1)S(1)} %bitcast.9, s32[256,112]{1,0:T(8,128)S(1)} %copy.6.bits_ref), custom_call_target="tpu_custom_call" | custom-call | flops 4194304 | bytes 7454720 | tf_op jit(solution)/shard_map/prune/pallas_call | solution.py:24
  33.4 1.3 %copy-done.1 = bf16[256,3584]{1,0:T(8,128)(2,1)} copy-done((bf16[256,3584]{1,0:T(8,128)(2,1)}, bf16[256,3584]{1,0:T(8,128)(2,1)S(1)}, u32[]{:S(2)}) %copy-start.1) | copy-done | bytes 1835032
  34.7 1.2 %copy-done.3 = bf16[256,3584]{1,0:T(8,128)(2,1)} copy-done((bf16[256,3584]{1,0:T(8,128)(2,1)}, bf16[256,3584]{1,0:T(8,128)(2,1)S(1)}, u32[]{:S(2)}) %copy-start.3) | copy-done | bytes 1835032
  36.0 0.8 %copy-done.5 = bf16[256,896]{1,0:T(8,128)(2,1)} copy-done((bf16[256,896]{1,0:T(8,128)(2,1)}, bf16[256,896]{1,0:T(8,128)(2,1)S(1)}, u32[]{:S(2)}) %copy-start.5) | copy-done | bytes 458776
  36.7 20.7 %all-to-all-done = bf16[32,8,3584]{2,1,0:T(8,128)(2,1)S(1)} async-done(((bf16[32,8,3584]{2,1,0:T(8,128)(2,1)}), bf16[32,8,3584]{2,1,0:T(8,128)(2,1)S(1)}, u32[]{:S(2)}, u32[]{:S(2)}) %all-to-all-start) | async-done | bytes 1835040 | tf_op jit(solution)/shard_map/route/all_to_all | solution.py:203
  57.5 1.0 %copy-done.6 = bf16[256,896]{1,0:T(8,128)(2,1)S(1)} copy-done((bf16[256,896]{1,0:T(8,128)(2,1)S(1)}, bf16[256,896]{1,0:T(8,128)(2,1)}, u32[]{:S(2)}) %copy-start.6) | copy-done | bytes 458776
  58.5 0.7 %project.1 = (f32[256,256]{1,0:T(8,128)S(1)}, bf16[256,256]{1,0:T(8,128)(2,1)S(1)}) custom-call(bf16[256,3584]{1,0:T(8,128)(2,1)S(1)} %bitcast.6, bf16[256,896]{1,0:T(8,128)(2,1)S(1)} %get-tuple-element.13.refs_0_, bf16[256,896]{1,0:T(8,128)(2,1)S(1)} %get-tuple-element.14.refs_1_, bf16[256,896]{1,0:T(8,128)(2,1)S(1)} %get-tuple-element.15.refs_2_, ...), custom_call_target="tpu_custom_call" | custom-call | flops 469762048 | bytes 4063232 | tf_op jit(solution)/shard_map/project/pallas_call | solution.py:24
  59.2 0.0 copy-start.2
  59.2 1.4 %collective-permute-start = (bf16[256,256]{1,0:T(8,128)(2,1)S(1)}, bf16[256,256]{1,0:T(8,128)(2,1)S(1)}, u32[]{:S(2)}, u32[]{:S(2)}) collective-permute-start(bf16[256,256]{1,0:T(8,128)(2,1)S(1)} %get-tuple-element.18), channel_id=1, source_target_pairs={{0,1},{1,0},{2,3},{3,2},{4,5},{5,4},{6,7},{7,6},{8,9},{9,8},{10,11... | collective-permute-start | bytes 393224 | tf_op jit(solution)/shard_map/swap_features/ppermute | solution.py:162
  60.7 0.0 copy-done.8
  60.7 0.2 scale.1.refs_3_
  60.8 3.7 %collective-permute-done.refs_1_ = bf16[256,256]{1,0:T(8,128)(2,1)S(1)} collective-permute-done((bf16[256,256]{1,0:T(8,128)(2,1)S(1)}, bf16[256,256]{1,0:T(8,128)(2,1)S(1)}, u32[]{:S(2)}, u32[]{:S(2)}) %collective-permute-start) | collective-permute-done | bytes 131104 | tf_op jit(solution)/shard_map/swap_features/ppermute | solution.py:162
  64.5 0.0 copy-done.4
  64.5 1.7 %update.1 = bf16[256,3584]{1,0:T(8,128)(2,1)} custom-call(f32[256,256]{1,0:T(8,128)S(1)} %get-tuple-element.17.refs_0_, bf16[256,256]{1,0:T(8,128)(2,1)S(1)} %collective-permute-done.refs_1_, bf16[256,3584]{1,0:T(8,128)(2,1)S(1)} %bitcast.8, f32[1,3584]{1,0:T(1,128)S(1)} %scale.1.refs_3_, bf16[256,3584]{1,0:T(8,128)(2,1)S(1)} %copy-done.2, ...), custom_call_target="tpu_custom_call" | custom-call | tf_op jit(solution)/shard_map/update/pallas_call | solution.py:229
  (10 shorter events, 0.0 us)
Async XLA Ops:
  0.0 0.9 %copy-start.7 = (bf16[16,3584]{1,0:T(8,128)(2,1)S(1)}, bf16[16,3584]{1,0:T(8,128)(2,1)}, u32[]{:S(2)}) copy-start(bf16[16,3584]{1,0:T(8,128)(2,1)} %tokens_hbm.1) | copy-start | bytes 344068
  0.9 0.7 %copy-start.9 = (s32[16,8]{0,1:T(8,128)S(1)}, s32[16,8]{0,1:T(8,128)}, u32[]{:S(2)}) copy-start(s32[16,8]{0,1:T(8,128)} %param.6) | copy-start | bytes 1540
  23.3 7.2 %copy-start.10 = (s32[256,112]{0,1:T(8,128)S(1)}, s32[256,112]{0,1:T(8,128)}, u32[]{:S(2)}) copy-start(s32[256,112]{0,1:T(8,128)} %param.8) | copy-start | bytes 344068
  23.3 34.1 %all-to-all-start = ((bf16[32,8,3584]{2,1,0:T(8,128)(2,1)}), bf16[32,8,3584]{2,1,0:T(8,128)(2,1)S(1)}, u32[]{:S(2)}, u32[]{:S(2)}) async-start(bf16[32,8,3584]{2,1,0:T(8,128)(2,1)} %bitcast.11), calls=%async_computation | async-start | bytes 3670016 | tf_op jit(solution)/shard_map/route/all_to_all | solution.py:203
  30.6 1.5 %copy-start = (bf16[1,256,3584]{2,1,0:T(8,128)(2,1)S(1)}, bf16[1,256,3584]{2,1,0:T(8,128)(2,1)}, u32[]{:S(2)}) copy-start(bf16[1,256,3584]{2,1,0:T(8,128)(2,1)} %param.7) | copy-start | bytes 5505028
  33.4 1.3 %copy-start.1 = (bf16[256,3584]{1,0:T(8,128)(2,1)}, bf16[256,3584]{1,0:T(8,128)(2,1)S(1)}, u32[]{:S(2)}) copy-start(bf16[256,3584]{1,0:T(8,128)(2,1)S(1)} %get-tuple-element.19.refs_4_) | copy-start | bytes 5505028
  34.7 1.2 %copy-start.3 = (bf16[256,3584]{1,0:T(8,128)(2,1)}, bf16[256,3584]{1,0:T(8,128)(2,1)S(1)}, u32[]{:S(2)}) copy-start(bf16[256,3584]{1,0:T(8,128)(2,1)S(1)} %get-tuple-element.20.refs_5_) | copy-start | bytes 5505028
  36.0 0.8 %copy-start.5 = (bf16[256,896]{1,0:T(8,128)(2,1)}, bf16[256,896]{1,0:T(8,128)(2,1)S(1)}, u32[]{:S(2)}) copy-start(bf16[256,896]{1,0:T(8,128)(2,1)S(1)} %get-tuple-element.16.refs_3_) | copy-start | bytes 1376260
  57.5 1.0 %copy-start.6 = (bf16[256,896]{1,0:T(8,128)(2,1)S(1)}, bf16[256,896]{1,0:T(8,128)(2,1)}, u32[]{:S(2)}) copy-start(bf16[256,896]{1,0:T(8,128)(2,1)} %copy-done.5) | copy-start | bytes 1376260
  58.5 2.2 %copy-start.8 = (f32[1,3584]{1,0:T(1,128)S(1)}, f32[1,3584]{1,0:T(1,128)}, u32[]{:S(2)}) copy-start(f32[1,3584]{1,0:T(1,128)} %refs_1_.1) | copy-start | bytes 43012
  58.5 6.0 %copy-start.4 = (bf16[256,3584]{1,0:T(8,128)(2,1)S(1)}, bf16[256,3584]{1,0:T(8,128)(2,1)}, u32[]{:S(2)}) copy-start(bf16[256,3584]{1,0:T(8,128)(2,1)} %copy-done.3) | copy-start | bytes 5505028
  59.2 5.3 %copy-start.2 = (bf16[256,3584]{1,0:T(8,128)(2,1)S(1)}, bf16[256,3584]{1,0:T(8,128)(2,1)}, u32[]{:S(2)}) copy-start(bf16[256,3584]{1,0:T(8,128)(2,1)} %copy-done.1) | copy-start | bytes 5505028
  59.2 5.3 %collective-permute-start = (bf16[256,256]{1,0:T(8,128)(2,1)S(1)}, bf16[256,256]{1,0:T(8,128)(2,1)S(1)}, u32[]{:S(2)}, u32[]{:S(2)}) collective-permute-start(bf16[256,256]{1,0:T(8,128)(2,1)S(1)} %get-tuple-element.18), channel_id=1, source_target_pairs={{0,1},{1,0},{2,3},{3,2},{4,5},{5,4},{6,7},{7,6},{8,9},{9,8},{10,11... | collective-permute-start | bytes 393224 | tf_op jit(solution)/shard_map/swap_features/ppermute | solution.py:162

commit v5 on v4

--- a/solution.py
+++ b/solution.py
@@ -12,6 +12,7 @@
 CAP = 2
 LANES = 128
 WIDTH = 896
+STEP = 512
 VMEM = 16 * 2**20
 F32 = jnp.float32
 BF16 = jnp.bfloat16
@@ -80,8 +81,8 @@
     rank = jnp.dot(member.astype(BF16), before, preferred_element_type=F32)
     select = jnp.where(rank == slot, member, 0.0).astype(BF16)
     copies = []
-    for i, lo in enumerate(range(0, feats, WIDTH)):
-        cols = (slice(None), pl.ds(lo, WIDTH))
+    for i, lo in enumerate(range(0, feats, STEP)):
+        cols = (slice(None), pl.ds(lo, STEP))
         out_ref[cols] = jnp.dot(select, held[cols], preferred_element_type=F32).astype(BF16)
         copies.append(pltpu.make_async_copy(out_ref.at[cols], out_hbm.at[cols], sems.at[i]))
         copies[-1].start()
@@ -107,16 +108,19 @@
 
 
 def project_body(routed_ref, *refs):
-    *pruned_refs, part_ref, low_ref = refs
-    part = None
-    for i, ref in enumerate(pruned_refs):
-        term = lax.dot_general(
+    *pruned_refs, last_hbm, part_ref, low_ref, last_ref, sem = refs
+    fetch = pltpu.make_async_copy(last_hbm, last_ref, sem)
+    fetch.start()
+    part = jnp.zeros(part_ref.shape, F32)
+    for i, ref in enumerate((*pruned_refs, last_ref)):
+        if ref is last_ref:
+            fetch.wait()
+        part = part + lax.dot_general(
             ref[...],
             routed_ref[:, i * WIDTH : (i + 1) * WIDTH],
             (((1,), (1,)), ((), ())),
             preferred_element_type=F32,
         )
-        part = term if part is None else part + term
     part_ref[...] = part
     low_ref[...] = part.astype(BF16)
 
@@ -139,14 +143,14 @@
     feats = kept_ref.shape[1]
     projected = [(p[...] + o[...].astype(F32)).astype(BF16) for p, o in zip(parts, others)]
     copies = []
-    for i, lo in enumerate(range(0, feats, WIDTH)):
-        cols = slice(lo, lo + WIDTH)
+    for i, lo in enumerate(range(0, feats, STEP)):
+        cols = slice(lo, lo + STEP)
         comp = jnp.dot(projected[0], routed_refs[0][:, cols], preferred_element_type=F32)
         for p, r in zip(projected[1:], routed_refs[1:]):
             comp = comp + jnp.dot(p, r[:, cols], preferred_element_type=F32)
         gain = keep_ref[:, cols].astype(F32) * (comp * scale_ref[:, cols])
         out_ref[:, cols] = (kept_ref[:, cols].astype(F32) + gain).astype(BF16)
-        cols = (slice(None), pl.ds(lo, WIDTH))
+        cols = (slice(None), pl.ds(lo, STEP))
         copies.append(pltpu.make_async_copy(out_ref.at[cols], out_hbm.at[cols], sems.at[i]))
         copies[-1].start()
     for copy in copies:
@@ -155,6 +159,10 @@
 
 def shape(*dims, dtype=BF16):
     return jax.ShapeDtypeStruct(dims, dtype)
+
+
+def in_hbm(x):
+    return pltpu.with_memory_space_constraint(x, pltpu.HBM)
 
 
 def shift(x, axis, step):
@@ -187,7 +195,7 @@
                 pltpu.SemaphoreType.DMA((2,)),
             ],
             compiler_params=params,
-        )(tokens, expert_ids.T)
+        )(in_hbm(tokens), in_hbm(expert_ids.T))
     with jax.named_scope("gather"):
         held = lax.all_gather(own, "zh", tiled=True)
     with jax.named_scope("pack"):
@@ -196,7 +204,10 @@
             out_shape=pltpu.HBM((rows, feats), BF16),
             in_specs=[pl.BlockSpec(memory_space=pltpu.SMEM), vmem],
             out_specs=hbm,
-            scratch_shapes=[pltpu.VMEM((rows, feats), BF16), pltpu.SemaphoreType.DMA((pieces,))],
+            scratch_shapes=[
+                pltpu.VMEM((rows, feats), BF16),
+                pltpu.SemaphoreType.DMA((feats // STEP,)),
+            ],
             compiler_params=params,
         )(first, held)
     with jax.named_scope("route"):
@@ -212,12 +223,17 @@
             1 << 22,
         )
     with jax.named_scope("project"):
-        part, low = call(
+        part, low = pl.pallas_call(
             project_body,
-            (shape(slab, rows, dtype=F32), shape(slab, rows)),
-            (routed, *pruned),
-            2 * rows * slab * feats,
-        )
+            out_shape=(shape(slab, rows, dtype=F32), shape(slab, rows)),
+            in_specs=[vmem] * pieces + [hbm],
+            out_specs=(vmem, vmem),
+            scratch_shapes=[pltpu.VMEM((slab, WIDTH), BF16), pltpu.SemaphoreType.DMA],
+            cost_estimate=pl.CostEstimate(
+                flops=2 * rows * slab * feats, bytes_accessed=1 << 22, transcendentals=0
+            ),
+            compiler_params=params,
+        )(routed, *pruned[:-1], in_hbm(pruned[-1]))
     with jax.named_scope("swap_features"):
         other = shift(low, "yl", 1)
     with jax.named_scope("scale"):
@@ -231,7 +247,10 @@
             out_shape=shape(slab, feats),
             in_specs=[vmem] * len(operands),
             out_specs=hbm,
-            scratch_shapes=[pltpu.VMEM((slab, feats), BF16), pltpu.SemaphoreType.DMA((pieces,))],
+            scratch_shapes=[
+                pltpu.VMEM((slab, feats), BF16),
+                pltpu.SemaphoreType.DMA((feats // STEP,)),
+            ],
             compiler_params=params,
         )(*operands)
     return out.reshape(1, slab, feats)

time: 67.3 us -> 66.1 us (0.982)
  local copies, waits for them, and re-layouts: 7.49 us -> 4.85 us
  Pallas kernels: 5.93 us -> 7.42 us
    unnamed x23 -> x17, local copies, waits for them, and re-layouts: 7.49 us -> 4.85 us
    pallas_call x0 -> x1, Pallas kernels: none -> 1.58 us  [local(): pl.pallas_call(project_body, out_shape=(shape(slab, rows, dtype=F32), sha...]
    pallas_call x3 -> x2, Pallas kernels: 2.19 us -> 1.48 us  [call(): pl.pallas_call(body, out_shape=out_shape, in_specs=[pl.BlockSpec(memory_s...]
    pallas_call x1, Pallas kernels: 0.24 us -> 0.93 us  [local(): pl.pallas_call(tag_body, out_shape=shape(tok_rows, feats + LANES), in_spe...]
where the time goes in v5:
time: 66.1 us; the launch traced here: 65.1 us
  waiting for transfers between devices  24.5 us (37%)
  blocking collectives  19.7 us (30%)
  starting transfers between devices  8.59 us (13%)
  Pallas kernels  7.42 us (11%)
  local copies, waits for them, and re-layouts  4.85 us (7%)
    all_to_all x1, waiting for transfers between devices, local(): lax.all_to_all(packed.reshape(dests, -1, feats), near, split_axis=0, conc...  20.8 us
    all_gather x1, blocking collectives, local(): held = lax.all_gather(own, 'zh', tiled=True)  19.7 us
    all_to_all x1, starting transfers between devices, local(): lax.all_to_all(packed.reshape(dests, -1, feats), near, split_axis=0, conc...  7.15 us
    unnamed x17, local copies, waits for them, and re-layouts  4.85 us
    ppermute x1, waiting for transfers between devices, shift(): return lax.ppermute(x, axis, [(i, (i + step) % n) for i in range(n)])  3.67 us
    pallas_call x1, Pallas kernels, local(): pl.pallas_call(functools.partial(pack_body, tok_rows, top), out_shape=plt...  1.78 us
    pallas_call x1, Pallas kernels, local(): pl.pallas_call(functools.partial(update_body, 1), out_shape=shape(slab, f...  1.65 us
    pallas_call x1, Pallas kernels, local(): pl.pallas_call(project_body, out_shape=(shape(slab, rows, dtype=F32), sha...  1.58 us
  transfers between devices with their start and end apart: 2, of which 2 were waited for; matrix products, arithmetic and copies ran while one was open for 0% of the time, Pallas kernels for 2%

profile of v5, /device:TPU:8, one launch (start us, length us, event | category | flops | bytes accessed | tf_op | source)
XLA Modules:
  0.0 65.1 jit_solution(2776270319852487360)
XLA Ops:
  0.0 0.9 %tag.1 = bf16[16,3712]{1,0:T(8,128)(2,1)S(1)} custom-call(bf16[16,3584]{1,0:T(8,128)(2,1)} %tokens_hbm.1, s32[8,16]{1,0:T(8,128)} %bitcast.11), custom_call_target="tpu_custom_call" | custom-call | tf_op jit(solution)/shard_map/tag/pallas_call | solution.py:188
  0.9 19.7 %all_gather.3.held = bf16[64,3712]{1,0:T(8,128)(2,1)S(1)} all-gather(bf16[16,3712]{1,0:T(8,128)(2,1)S(1)} %tag.1), channel_id=1, replica_groups=mesh['zh'=4,'zl'=2,'yh'=2,'x'=4,'core'=2,'yl'=2] {'zh'}, dimensions={0}, use_global_device_ids=true | all-gather | bytes 593920 | tf_op jit(solution)/shard_map/gather/all_gather | solution.py:200
  20.6 1.8 %pack.1 = bf16[256,3584]{1,0:T(8,128)(2,1)} custom-call(s32[1]{0:T(128)} %bitcast.first_ref, bf16[64,3712]{1,0:T(8,128)(2,1)S(1)} %all_gather.3.held), custom_call_target="tpu_custom_call" | custom-call | tf_op jit(solution)/shard_map/pack/pallas_call | solution.py:202
  22.4 0.0 copy-start.7
  22.4 7.2 %all-to-all-start = ((bf16[32,8,3584]{2,1,0:T(8,128)(2,1)}), bf16[32,8,3584]{2,1,0:T(8,128)(2,1)S(1)}, u32[]{:S(2)}, u32[]{:S(2)}) async-start(bf16[32,8,3584]{2,1,0:T(8,128)(2,1)} %bitcast.10), calls=%async_computation | async-start | bytes 3670016 | tf_op jit(solution)/shard_map/route/all_to_all | solution.py:214
  29.6 0.0 copy-done.7
  29.6 0.1 copy.6.bits_ref
  29.7 0.0 copy-start
  29.7 1.5 %copy-done = bf16[1,256,3584]{2,1,0:T(8,128)(2,1)S(1)} copy-done((bf16[1,256,3584]{2,1,0:T(8,128)(2,1)S(1)}, bf16[1,256,3584]{2,1,0:T(8,128)(2,1)}, u32[]{:S(2)}) %copy-start) | copy-done | bytes 1835032
  31.2 1.3 %prune.1 = (bf16[256,896]{1,0:T(8,128)(2,1)S(1)}, bf16[256,896]{1,0:T(8,128)(2,1)S(1)}, bf16[256,896]{1,0:T(8,128)(2,1)S(1)}, bf16[256,896]{1,0:T(8,128)(2,1)S(1...) custom-call(bf16[256,3584]{1,0:T(8,128)(2,1)S(1)} %bitcast.9, s32[256,112]{1,0:T(8,128)S(1)} %copy.6.bits_ref), custom_call_target="tpu_custom_call" | custom-call | flops 4194304 | bytes 7454720 | tf_op jit(solution)/shard_map/prune/pallas_call | solution.py:25
  32.5 0.0 copy-start.1
  32.5 1.2 %copy-done.1 = bf16[256,3584]{1,0:T(8,128)(2,1)} copy-done((bf16[256,3584]{1,0:T(8,128)(2,1)}, bf16[256,3584]{1,0:T(8,128)(2,1)S(1)}, u32[]{:S(2)}) %copy-start.1) | copy-done | bytes 1835032
  33.7 1.2 %copy-done.3 = bf16[256,3584]{1,0:T(8,128)(2,1)} copy-done((bf16[256,3584]{1,0:T(8,128)(2,1)}, bf16[256,3584]{1,0:T(8,128)(2,1)S(1)}, u32[]{:S(2)}) %copy-start.3) | copy-done | bytes 1835032
  35.0 0.8 %copy-done.5 = bf16[256,896]{1,0:T(8,128)(2,1)} copy-done((bf16[256,896]{1,0:T(8,128)(2,1)}, bf16[256,896]{1,0:T(8,128)(2,1)S(1)}, u32[]{:S(2)}) %copy-start.5) | copy-done | bytes 458776
  35.7 20.8 %all-to-all-done = bf16[32,8,3584]{2,1,0:T(8,128)(2,1)S(1)} async-done(((bf16[32,8,3584]{2,1,0:T(8,128)(2,1)}), bf16[32,8,3584]{2,1,0:T(8,128)(2,1)S(1)}, u32[]{:S(2)}, u32[]{:S(2)}) %all-to-all-start) | async-done | bytes 1835040 | tf_op jit(solution)/shard_map/route/all_to_all | solution.py:214
  56.5 1.6 %project.1 = (f32[256,256]{1,0:T(8,128)S(1)}, bf16[256,256]{1,0:T(8,128)(2,1)S(1)}) custom-call(bf16[256,3584]{1,0:T(8,128)(2,1)S(1)} %bitcast.6, bf16[256,896]{1,0:T(8,128)(2,1)S(1)} %get-tuple-element.13.refs_0_, bf16[256,896]{1,0:T(8,128)(2,1)S(1)} %get-tuple-element.14.refs_1_, bf16[256,896]{1,0:T(8,128)(2,1)S(1)} %get-tuple-element.15.refs_2_, ...), custom_call_target="tpu_custom_call" | custom-call | flops 469762048 | bytes 4194304 | tf_op jit(solution)/shard_map/project/pallas_call | solution.py:226
  58.1 0.0 copy-start.2
  58.1 1.4 %collective-permute-start = (bf16[256,256]{1,0:T(8,128)(2,1)S(1)}, bf16[256,256]{1,0:T(8,128)(2,1)S(1)}, u32[]{:S(2)}, u32[]{:S(2)}) collective-permute-start(bf16[256,256]{1,0:T(8,128)(2,1)S(1)} %get-tuple-element.18), channel_id=1, source_target_pairs={{0,1},{1,0},{2,3},{3,2},{4,5},{5,4},{6,7},{7,6},{8,9},{9,8},{10,11... | collective-permute-start | bytes 393224 | tf_op jit(solution)/shard_map/swap_features/ppermute | solution.py:170
  59.6 0.0 copy-done.6
  59.6 0.2 scale.1.refs_3_
  59.7 3.7 %collective-permute-done.refs_1_ = bf16[256,256]{1,0:T(8,128)(2,1)S(1)} collective-permute-done((bf16[256,256]{1,0:T(8,128)(2,1)S(1)}, bf16[256,256]{1,0:T(8,128)(2,1)S(1)}, u32[]{:S(2)}, u32[]{:S(2)}) %collective-permute-start) | collective-permute-done | bytes 131104 | tf_op jit(solution)/shard_map/swap_features/ppermute | solution.py:170
  63.4 0.0 copy-done.4
  63.4 0.0 copy-done.2
  63.4 1.6 %update.1 = bf16[256,3584]{1,0:T(8,128)(2,1)} custom-call(f32[256,256]{1,0:T(8,128)S(1)} %get-tuple-element.17.refs_0_, bf16[256,256]{1,0:T(8,128)(2,1)S(1)} %collective-permute-done.refs_1_, bf16[256,3584]{1,0:T(8,128)(2,1)S(1)} %bitcast.8, f32[1,3584]{1,0:T(1,128)S(1)} %scale.1.refs_3_, bf16[256,3584]{1,0:T(8,128)(2,1)S(1)} %copy-done.2, ...), custom_call_target="tpu_custom_call" | custom-call | tf_op jit(solution)/shard_map/update/pallas_call | solution.py:245
  (4 shorter events, 0.0 us)
Async XLA Ops:
  22.4 7.2 %copy-start.7 = (s32[256,112]{0,1:T(8,128)S(1)}, s32[256,112]{0,1:T(8,128)}, u32[]{:S(2)}) copy-start(s32[256,112]{0,1:T(8,128)} %param.8) | copy-start | bytes 344068
  22.4 34.1 %all-to-all-start = ((bf16[32,8,3584]{2,1,0:T(8,128)(2,1)}), bf16[32,8,3584]{2,1,0:T(8,128)(2,1)S(1)}, u32[]{:S(2)}, u32[]{:S(2)}) async-start(bf16[32,8,3584]{2,1,0:T(8,128)(2,1)} %bitcast.10), calls=%async_computation | async-start | bytes 3670016 | tf_op jit(solution)/shard_map/route/all_to_all | solution.py:214
  29.7 1.5 %copy-start = (bf16[1,256,3584]{2,1,0:T(8,128)(2,1)S(1)}, bf16[1,256,3584]{2,1,0:T(8,128)(2,1)}, u32[]{:S(2)}) copy-start(bf16[1,256,3584]{2,1,0:T(8,128)(2,1)} %param.7) | copy-start | bytes 5505028
  32.5 1.3 %copy-start.1 = (bf16[256,3584]{1,0:T(8,128)(2,1)}, bf16[256,3584]{1,0:T(8,128)(2,1)S(1)}, u32[]{:S(2)}) copy-start(bf16[256,3584]{1,0:T(8,128)(2,1)S(1)} %get-tuple-element.19.refs_4_) | copy-start | bytes 5505028
  33.7 1.2 %copy-start.3 = (bf16[256,3584]{1,0:T(8,128)(2,1)}, bf16[256,3584]{1,0:T(8,128)(2,1)S(1)}, u32[]{:S(2)}) copy-start(bf16[256,3584]{1,0:T(8,128)(2,1)S(1)} %get-tuple-element.20.refs_5_) | copy-start | bytes 5505028
  35.0 0.8 %copy-start.5 = (bf16[256,896]{1,0:T(8,128)(2,1)}, bf16[256,896]{1,0:T(8,128)(2,1)S(1)}, u32[]{:S(2)}) copy-start(bf16[256,896]{1,0:T(8,128)(2,1)S(1)} %get-tuple-element.16.refs_3_) | copy-start | bytes 1376260
  56.5 3.0 %copy-start.6 = (f32[1,3584]{1,0:T(1,128)S(1)}, f32[1,3584]{1,0:T(1,128)}, u32[]{:S(2)}) copy-start(f32[1,3584]{1,0:T(1,128)} %refs_1_.1) | copy-start | bytes 43012
  56.5 6.9 %copy-start.4 = (bf16[256,3584]{1,0:T(8,128)(2,1)S(1)}, bf16[256,3584]{1,0:T(8,128)(2,1)}, u32[]{:S(2)}) copy-start(bf16[256,3584]{1,0:T(8,128)(2,1)} %copy-done.3) | copy-start | bytes 5505028
  58.1 5.3 %copy-start.2 = (bf16[256,3584]{1,0:T(8,128)(2,1)S(1)}, bf16[256,3584]{1,0:T(8,128)(2,1)}, u32[]{:S(2)}) copy-start(bf16[256,3584]{1,0:T(8,128)(2,1)} %copy-done.1) | copy-start | bytes 5505028
  58.1 5.3 %collective-permute-start = (bf16[256,256]{1,0:T(8,128)(2,1)S(1)}, bf16[256,256]{1,0:T(8,128)(2,1)S(1)}, u32[]{:S(2)}, u32[]{:S(2)}) collective-permute-start(bf16[256,256]{1,0:T(8,128)(2,1)S(1)} %get-tuple-element.18), channel_id=1, source_target_pairs={{0,1},{1,0},{2,3},{3,2},{4,5},{5,4},{6,7},{7,6},{8,9},{9,8},{10,11... | collective-permute-start | bytes 393224 | tf_op jit(solution)/shard_map/swap_features/ppermute | solution.py:170

commit v6 on v5

--- a/solution.py
+++ b/solution.py
@@ -11,8 +11,8 @@
 ETA = 0.5
 CAP = 2
 LANES = 128
-WIDTH = 896
 STEP = 512
+PARTS = 2
 VMEM = 16 * 2**20
 F32 = jnp.float32
 BF16 = jnp.bfloat16
@@ -91,33 +91,46 @@
 
 
 def prune_body(weight_ref, bits_ref, *refs):
-    *pruned_refs, kept_ref, keep_ref = refs
+    *pruned_refs, rest_ref, kept_ref = refs
     rows, words = bits_ref.shape
-    feats = weight_ref.shape[1]
+    part = rows // len(pruned_refs)
+    wide = pruned_refs[-1].shape[1]
     lane = lax.broadcasted_iota(jnp.int32, (rows, LANES), 1)
     bits = jnp.concatenate([bits_ref[...], jnp.zeros((rows, LANES - words), jnp.int32)], axis=1)
-    for j in range(feats // LANES):
+    for j in range(weight_ref.shape[1] // LANES):
         word = jnp.take_along_axis(bits, lane // 32 + 4 * j, axis=1, mode="promise_in_bounds")
-        keep = jnp.bitwise_and(jnp.right_shift(word, lane % 32), 1).astype(F32)
-        cols = slice(j * LANES, (j + 1) * LANES)
+        keep = jnp.bitwise_and(jnp.right_shift(word, lane % 32), 1) == 1
+        lo = j * LANES
+        cols = slice(lo, lo + LANES)
         slab = weight_ref[:, cols].astype(F32)
-        piece, at = divmod(j * LANES, WIDTH)
-        pruned_refs[piece][:, at : at + LANES] = jnp.where(keep > 0.5, 0.0, slab).astype(BF16)
-        kept_ref[:, cols] = jnp.where(keep > 0.5, slab, 0.0).astype(BF16)
-        keep_ref[:, cols] = keep.astype(BF16)
-
-
-def project_body(routed_ref, *refs):
-    *pruned_refs, last_hbm, part_ref, low_ref, last_ref, sem = refs
-    fetch = pltpu.make_async_copy(last_hbm, last_ref, sem)
-    fetch.start()
-    part = jnp.zeros(part_ref.shape, F32)
-    for i, ref in enumerate((*pruned_refs, last_ref)):
-        if ref is last_ref:
-            fetch.wait()
+        pruned = jnp.where(keep, 0.0, slab).astype(BF16)
+        for i, ref in enumerate(pruned_refs):
+            mine = pruned[i * part : (i + 1) * part]
+            if lo < ref.shape[1]:
+                ref[:, cols] = mine
+            else:
+                rest_ref[:, lo - wide : lo - wide + LANES] = mine
+        kept_ref[:, cols] = jnp.where(keep, slab, jnp.inf).astype(BF16)
+
+
+def project_body(routed_ref, pruned_ref, *refs):
+    *rest, part_ref, low_ref = refs[:3] if len(refs) > 2 else refs
+    wide = pruned_ref.shape[1]
+    if rest:
+        rest_ref, sem = refs[3:]
+        fetch = pltpu.make_async_copy(rest[0], rest_ref, sem)
+        fetch.start()
+    part = lax.dot_general(
+        pruned_ref[...],
+        routed_ref[:, :wide],
+        (((1,), (1,)), ((), ())),
+        preferred_element_type=F32,
+    )
+    if rest:
+        fetch.wait()
         part = part + lax.dot_general(
-            ref[...],
-            routed_ref[:, i * WIDTH : (i + 1) * WIDTH],
+            rest_ref[...],
+            routed_ref[:, wide:],
             (((1,), (1,)), ((), ())),
             preferred_element_type=F32,
         )
@@ -128,8 +141,8 @@
 def scale_body(*refs):
     *routed_refs, damping_ref, scale_ref = refs
     feats = damping_ref.shape[1]
-    for lo in range(0, feats, WIDTH):
-        cols = slice(lo, lo + WIDTH)
+    for lo in range(0, feats, STEP):
+        cols = slice(lo, lo + STEP)
         diag = damping_ref[:, cols]
         for ref in routed_refs:
             rows = ref[:, cols].astype(F32)
@@ -137,21 +150,25 @@
         scale_ref[:, cols] = (ETA / ROWS_E) / diag
 
 
-def update_body(n, *refs):
-    parts, others, routed_refs = refs[:n], refs[n : 2 * n], refs[2 * n : 3 * n]
-    scale_ref, kept_ref, keep_ref, out_hbm, out_ref, sems = refs[3 * n :]
-    feats = kept_ref.shape[1]
-    projected = [(p[...] + o[...].astype(F32)).astype(BF16) for p, o in zip(parts, others)]
+def update_body(at, part_ref, other_ref, routed_ref, scale_ref, kept_ref, *refs):
+    out_hbm, out_ref, sems = refs[-3:]
+    rows, feats = out_ref.shape
+    mine = slice(at, at + rows)
+    projected = (part_ref[...] + other_ref[...].astype(F32)).astype(BF16)
     copies = []
     for i, lo in enumerate(range(0, feats, STEP)):
         cols = slice(lo, lo + STEP)
-        comp = jnp.dot(projected[0], routed_refs[0][:, cols], preferred_element_type=F32)
-        for p, r in zip(projected[1:], routed_refs[1:]):
-            comp = comp + jnp.dot(p, r[:, cols], preferred_element_type=F32)
-        gain = keep_ref[:, cols].astype(F32) * (comp * scale_ref[:, cols])
-        out_ref[:, cols] = (kept_ref[:, cols].astype(F32) + gain).astype(BF16)
-        cols = (slice(None), pl.ds(lo, STEP))
-        copies.append(pltpu.make_async_copy(out_ref.at[cols], out_hbm.at[cols], sems.at[i]))
+        comp = jnp.dot(projected, routed_ref[:, cols], preferred_element_type=F32)
+        kept = kept_ref[mine, cols].astype(F32)
+        updated = jnp.where(kept < jnp.inf, kept + comp * scale_ref[:, cols], 0.0)
+        out_ref[:, cols] = updated.astype(BF16)
+        copies.append(
+            pltpu.make_async_copy(
+                out_ref.at[:, pl.ds(lo, STEP)],
+                out_hbm.at[pl.ds(at, rows), pl.ds(lo, STEP)],
+                sems.at[i],
+            )
+        )
         copies[-1].start()
     for copy in copies:
         copy.wait()
@@ -179,7 +196,6 @@
     dests = lax.axis_size(near)
     n_tok = tok_rows * lax.axis_size("zh")
     rows = dests * lax.axis_size("zh") * CAP
-    pieces = feats // WIDTH
     first = (lax.axis_index("zh") * dests).astype(jnp.int32).reshape(1)
     hbm, vmem = pl.BlockSpec(memory_space=pltpu.HBM), pl.BlockSpec(memory_space=pltpu.VMEM)
     params = pltpu.CompilerParams(vmem_limit_bytes=VMEM)
@@ -215,44 +231,63 @@
             packed.reshape(dests, -1, feats), near, split_axis=0, concat_axis=0, tiled=True
         )
     routed = block.reshape(rows, feats)
+    part_rows = slab // PARTS
     with jax.named_scope("prune"):
-        *pruned, kept, keep = call(
+        *pruned, rest, kept = call(
             prune_body,
-            (shape(slab, WIDTH),) * pieces + (shape(slab, feats),) * 2,
+            (shape(part_rows, feats),) * (PARTS - 1)
+            + (shape(part_rows, feats - STEP), shape(part_rows, STEP), shape(slab, feats)),
             (weight, mask_bits),
             1 << 22,
         )
-    with jax.named_scope("project"):
-        part, low = pl.pallas_call(
-            project_body,
-            out_shape=(shape(slab, rows, dtype=F32), shape(slab, rows)),
-            in_specs=[vmem] * pieces + [hbm],
-            out_specs=(vmem, vmem),
-            scratch_shapes=[pltpu.VMEM((slab, WIDTH), BF16), pltpu.SemaphoreType.DMA],
-            cost_estimate=pl.CostEstimate(
-                flops=2 * rows * slab * feats, bytes_accessed=1 << 22, transcendentals=0
-            ),
-            compiler_params=params,
-        )(routed, *pruned[:-1], in_hbm(pruned[-1]))
+    parts = []
+    for i, p in enumerate(pruned):
+        last = i == PARTS - 1
+        if i:
+            p = lax.optimization_barrier((p, parts[-1][1]))[0]
+        with jax.named_scope("project"):
+            parts.append(
+                pl.pallas_call(
+                    project_body,
+                    out_shape=(shape(part_rows, rows, dtype=F32), shape(part_rows, rows)),
+                    in_specs=[vmem, vmem] + [hbm] * last,
+                    out_specs=(vmem, vmem),
+                    scratch_shapes=[pltpu.VMEM(rest.shape, BF16), pltpu.SemaphoreType.DMA] * last,
+                    cost_estimate=pl.CostEstimate(
+                        flops=2 * rows * part_rows * feats,
+                        bytes_accessed=1 << 21,
+                        transcendentals=0,
+                    ),
+                    compiler_params=params,
+                )(routed, p, *([in_hbm(rest)] if last else []))
+            )
     with jax.named_scope("swap_features"):
-        other = shift(low, "yl", 1)
+        others = [shift(low, "yl", 1) for _, low in parts]
     with jax.named_scope("scale"):
         scale = call(
             scale_body, shape(1, feats, dtype=F32), (routed, damping), 4 * slab * feats
         )
-    with jax.named_scope("update"):
-        operands = (part, other, routed, scale, kept, keep)
-        out = pl.pallas_call(
-            functools.partial(update_body, 1),
-            out_shape=shape(slab, feats),
-            in_specs=[vmem] * len(operands),
-            out_specs=hbm,
-            scratch_shapes=[
-                pltpu.VMEM((slab, feats), BF16),
-                pltpu.SemaphoreType.DMA((feats // STEP,)),
-            ],
-            compiler_params=params,
-        )(*operands)
+    out = None
+    for i, ((part, _), other) in enumerate(zip(parts, others)):
+        operands = (part, other, routed, scale, kept)
+        with jax.named_scope("update"):
+            out = pl.pallas_call(
+                functools.partial(update_body, i * part_rows),
+                out_shape=pltpu.HBM((slab, feats), BF16),
+                in_specs=[vmem] * len(operands) + [hbm] * (i > 0),
+                out_specs=hbm,
+                scratch_shapes=[
+                    pltpu.VMEM((part_rows, feats), BF16),
+                    pltpu.SemaphoreType.DMA((feats // STEP,)),
+                ],
+                input_output_aliases={len(operands): 0} if i else {},
+                cost_estimate=pl.CostEstimate(
+                    flops=2 * rows * part_rows * feats,
+                    bytes_accessed=1 << 22,
+                    transcendentals=0,
+                ),
+                compiler_params=params,
+            )(*operands, *([in_hbm(out)] if i else []))
     return out.reshape(1, slab, feats)
 
 

time: 66.1 us -> 66.4 us (level); the launches traced: 65.1 us -> 66.1 us
  Pallas kernels: 7.42 us -> 8.93 us
  waiting for transfers between devices: 24.5 us -> 23 us
  starting transfers between devices: 8.59 us -> 9.34 us
    pallas_call x2 -> x4, Pallas kernels: 3.23 us -> 4.98 us  [the longest x2 2.5 us: local(): pl.pallas_call(functools.partial(update_body, i * part_rows), out_shape=p...]
    ppermute x1 -> x2, waiting for transfers between devices: 3.67 us -> 2.21 us  [shift(): return lax.ppermute(x, axis, [(i, (i + step) % n) for i in range(n)])]
    ppermute x1 -> x2, starting transfers between devices: 1.44 us -> 2.19 us  [shift(): return lax.ppermute(x, axis, [(i, (i + step) % n) for i in range(n)])]
    unnamed x17 -> x15, local copies, waits for them, and re-layouts: 4.85 us -> 5.08 us
  transfers between devices with their start and end apart: 2 -> 3, of which waited for: 2 -> 3; matrix products, arithmetic and copies ran while one was open for 0% -> 1% of each run, Pallas kernels for 2% -> 6%
where the time goes in v6:
time: 66.4 us; the launch traced here: 66.1 us
  waiting for transfers between devices  23 us (35%)
  blocking collectives  19.7 us (30%)
  starting transfers between devices  9.34 us (14%)
  Pallas kernels  8.93 us (13%)
  local copies, waits for them, and re-layouts  5.08 us (8%)
    all_to_all x1, waiting for transfers between devices, local(): lax.all_to_all(packed.reshape(dests, -1, feats), near, split_axis=0, conc...  20.8 us
    all_gather x1, blocking collectives, local(): held = lax.all_gather(own, 'zh', tiled=True)  19.7 us
    all_to_all x1, starting transfers between devices, local(): lax.all_to_all(packed.reshape(dests, -1, feats), near, split_axis=0, conc...  7.15 us
    unnamed x15, local copies, waits for them, and re-layouts  5.08 us
    pallas_call x2, Pallas kernels, local(): pl.pallas_call(functools.partial(update_body, i * part_rows), out_shape=p...  2.5 us
    pallas_call x2, Pallas kernels, local(): pl.pallas_call(project_body, out_shape=(shape(part_rows, rows, dtype=F32)...  2.48 us
    ppermute x2, waiting for transfers between devices, shift(): return lax.ppermute(x, axis, [(i, (i + step) % n) for i in range(n)])  2.21 us
    ppermute x2, starting transfers between devices, shift(): return lax.ppermute(x, axis, [(i, (i + step) % n) for i in range(n)])  2.19 us
  transfers between devices with their start and end apart: 3, of which 3 were waited for; matrix products, arithmetic and copies ran while one was open for 1% of the time, Pallas kernels for 6%

profile of v6, /device:TPU:8, one launch (start us, length us, event | category | flops | bytes accessed | tf_op | source)
XLA Modules:
  0.0 66.1 jit_solution(5087228631135038812)
XLA Ops:
  0.0 0.9 %tag.1 = bf16[16,3712]{1,0:T(8,128)(2,1)S(1)} custom-call(bf16[16,3584]{1,0:T(8,128)(2,1)} %tokens_hbm.1, s32[8,16]{1,0:T(8,128)} %bitcast.13), custom_call_target="tpu_custom_call" | custom-call | tf_op jit(solution)/shard_map/tag/pallas_call | solution.py:204
  0.9 19.7 %all_gather.3.held = bf16[64,3712]{1,0:T(8,128)(2,1)S(1)} all-gather(bf16[16,3712]{1,0:T(8,128)(2,1)S(1)} %tag.1), channel_id=1, replica_groups=mesh['zh'=4,'zl'=2,'yh'=2,'x'=4,'core'=2,'yl'=2] {'zh'}, dimensions={0}, use_global_device_ids=true | all-gather | bytes 593920 | tf_op jit(solution)/shard_map/gather/all_gather | solution.py:216
  20.6 1.8 %pack.1 = bf16[256,3584]{1,0:T(8,128)(2,1)} custom-call(s32[1]{0:T(128)} %bitcast.first_ref, bf16[64,3712]{1,0:T(8,128)(2,1)S(1)} %all_gather.3.held), custom_call_target="tpu_custom_call" | custom-call | tf_op jit(solution)/shard_map/pack/pallas_call | solution.py:218
  22.4 0.0 copy-start.6
  22.4 7.2 %all-to-all-start = ((bf16[32,8,3584]{2,1,0:T(8,128)(2,1)}), bf16[32,8,3584]{2,1,0:T(8,128)(2,1)S(1)}, u32[]{:S(2)}, u32[]{:S(2)}) async-start(bf16[32,8,3584]{2,1,0:T(8,128)(2,1)} %bitcast.12), calls=%async_computation | async-start | bytes 3670016 | tf_op jit(solution)/shard_map/route/all_to_all | solution.py:230
  29.6 0.0 copy-done.6
  29.6 0.8 %copy.7.bits_ref = s32[256,112]{1,0:T(8,128)} copy(s32[256,112]{0,1:T(8,128)S(1)} %copy-done.6) | data formatting | bytes 229376 | tf_op args[3]
  30.3 1.5 %copy-done.2 = bf16[1,256,3584]{2,1,0:T(8,128)(2,1)S(1)} copy-done((bf16[1,256,3584]{2,1,0:T(8,128)(2,1)S(1)}, bf16[1,256,3584]{2,1,0:T(8,128)(2,1)}, u32[]{:S(2)}) %copy-start.2) | copy-done | bytes 1835032
  31.8 0.9 %copy-done.3 = s32[256,112]{1,0:T(8,128)S(1)} copy-done((s32[256,112]{1,0:T(8,128)S(1)}, s32[256,112]{1,0:T(8,128)}, u32[]{:S(2)}) %copy-start.3) | copy-done | bytes 114712
  32.7 1.1 %prune.1 = (bf16[128,3584]{1,0:T(8,128)(2,1)S(1)}, bf16[128,3072]{1,0:T(8,128)(2,1)S(1)}, bf16[128,512]{1,0:T(8,128)(2,1)S(1)}, bf16[256,3584]{1,0:T(8,128)(2,1)S(1)}) custom-call(bf16[256,3584]{1,0:T(8,128)(2,1)S(1)} %bitcast.11, s32[256,112]{1,0:T(8,128)S(1)} %copy-done.3), custom_call_target="tpu_custom_call" | custom-call | flops 4194304 | bytes 5619712 | tf_op jit(solution)/shard_map/prune/pallas_call | solution.py:25
  33.8 0.0 copy-start
  33.9 1.3 %copy-done = bf16[256,3584]{1,0:T(8,128)(2,1)} copy-done((bf16[256,3584]{1,0:T(8,128)(2,1)}, bf16[256,3584]{1,0:T(8,128)(2,1)S(1)}, u32[]{:S(2)}) %copy-start) | copy-done | bytes 1835032
  35.1 0.6 copy-done.4
  35.8 20.8 %all-to-all-done = bf16[32,8,3584]{2,1,0:T(8,128)(2,1)S(1)} async-done(((bf16[32,8,3584]{2,1,0:T(8,128)(2,1)}), bf16[32,8,3584]{2,1,0:T(8,128)(2,1)S(1)}, u32[]{:S(2)}, u32[]{:S(2)}) %all-to-all-start) | async-done | bytes 1835040 | tf_op jit(solution)/shard_map/route/all_to_all | solution.py:230
  56.5 0.7 %project.2 = (f32[128,256]{1,0:T(8,128)S(1)}, bf16[128,256]{1,0:T(8,128)(2,1)S(1)}) custom-call(bf16[256,3584]{1,0:T(8,128)(2,1)S(1)} %bitcast.6, bf16[128,3584]{1,0:T(8,128)(2,1)S(1)} %get-tuple-element.15.pruned_ref), custom_call_target="tpu_custom_call" | custom-call | flops 234881024 | bytes 2097152 | tf_op jit(solution)/shard_map/project/pallas_call | solution.py:250
  57.2 0.0 copy-start.5
  57.3 1.4 %collective-permute-start.1 = (bf16[128,256]{1,0:T(8,128)(2,1)S(1)}, bf16[128,256]{1,0:T(8,128)(2,1)S(1)}, u32[]{:S(2)}, u32[]{:S(2)}) collective-permute-start(bf16[128,256]{1,0:T(8,128)(2,1)S(1)} %get-tuple-element.16), channel_id=1, source_target_pairs={{0,1},{1,0},{2,3},{3,2},{4,5},{5,4},{6,7},{7,6},{8,9},{9,8},{10,11... | collective-permute-start | bytes 196616 | tf_op jit(solution)/shard_map/swap_features/ppermute | solution.py:187
  58.7 1.8 %project.3 = (f32[128,256]{1,0:T(8,128)S(1)}, bf16[128,256]{1,0:T(8,128)(2,1)S(1)}) custom-call(bf16[256,3584]{1,0:T(8,128)(2,1)S(1)} %bitcast.7, bf16[128,3072]{1,0:T(8,128)(2,1)S(1)} %get-tuple-element.17.pruned_ref, bf16[128,512]{1,0:T(8,128)(2,1)} %copy-done.4), custom_call_target="tpu_custom_call" | custom-call | flops 234881024 | bytes 2097152 | tf_op jit(solution)/shard_map/project/pallas_call | solution.py:250
  60.5 0.8 %collective-permute-start = (bf16[128,256]{1,0:T(8,128)(2,1)S(1)}, bf16[128,256]{1,0:T(8,128)(2,1)S(1)}, u32[]{:S(2)}, u32[]{:S(2)}) collective-permute-start(bf16[128,256]{1,0:T(8,128)(2,1)S(1)} %get-tuple-element.20), channel_id=1, source_target_pairs={{0,1},{1,0},{2,3},{3,2},{4,5},{5,4},{6,7},{7,6},{8,9},{9,8},{10,11... | collective-permute-start | bytes 196616 | tf_op jit(solution)/shard_map/swap_features/ppermute | solution.py:187
  61.2 0.1 scale.1.scale_ref
  61.4 0.3 collective-permute-done.1.other_ref
  61.6 1.2 %update.2.refs_0_ = bf16[256,3584]{1,0:T(8,128)(2,1)} custom-call(f32[128,256]{1,0:T(8,128)S(1)} %get-tuple-element.22.part_ref, bf16[128,256]{1,0:T(8,128)(2,1)S(1)} %collective-permute-done.1.other_ref, bf16[256,3584]{1,0:T(8,128)(2,1)S(1)} %bitcast.9, f32[1,3584]{1,0:T(1,128)S(1)} %scale.1.scale_ref, bf16[256,3584]{1,0:T(8,128)(2,1)S(1)} %copy-done.1), custom_call_target="tpu_custom_call" | custom-call | flops 234881024 | bytes 4194304 | tf_op jit(solution)/shard_map/update/pallas_call | solution.py:274
  62.9 2.0 %collective-permute-done.other_ref = bf16[128,256]{1,0:T(8,128)(2,1)S(1)} collective-permute-done((bf16[128,256]{1,0:T(8,128)(2,1)S(1)}, bf16[128,256]{1,0:T(8,128)(2,1)S(1)}, u32[]{:S(2)}, u32[]{:S(2)}) %collective-permute-start) | collective-permute-done | bytes 65568 | tf_op jit(solution)/shard_map/swap_features/ppermute | solution.py:187
  64.8 1.3 %update.3 = bf16[256,3584]{1,0:T(8,128)(2,1)} custom-call(f32[128,256]{1,0:T(8,128)S(1)} %get-tuple-element.19.part_ref, bf16[128,256]{1,0:T(8,128)(2,1)S(1)} %collective-permute-done.other_ref, bf16[256,3584]{1,0:T(8,128)(2,1)S(1)} %bitcast.10, f32[1,3584]{1,0:T(1,128)S(1)} %scale.1.scale_ref, ...), custom_call_target="tpu_custom_call", output_to_operand_aliasing={{}: (5, {})} | custom-call | flops 234881024 | bytes 4194304 | tf_op jit(solution)/shard_map/update/pallas_call | solution.py:274
  (6 shorter events, 0.0 us)
Async XLA Ops:
  22.4 7.2 %copy-start.6 = (s32[256,112]{0,1:T(8,128)S(1)}, s32[256,112]{0,1:T(8,128)}, u32[]{:S(2)}) copy-start(s32[256,112]{0,1:T(8,128)} %param.8) | copy-start | bytes 344068
  22.4 34.1 %all-to-all-start = ((bf16[32,8,3584]{2,1,0:T(8,128)(2,1)}), bf16[32,8,3584]{2,1,0:T(8,128)(2,1)S(1)}, u32[]{:S(2)}, u32[]{:S(2)}) async-start(bf16[32,8,3584]{2,1,0:T(8,128)(2,1)} %bitcast.12), calls=%async_computation | async-start | bytes 3670016 | tf_op jit(solution)/shard_map/route/all_to_all | solution.py:230
  30.3 1.5 %copy-start.2 = (bf16[1,256,3584]{2,1,0:T(8,128)(2,1)S(1)}, bf16[1,256,3584]{2,1,0:T(8,128)(2,1)}, u32[]{:S(2)}) copy-start(bf16[1,256,3584]{2,1,0:T(8,128)(2,1)} %param.7) | copy-start | bytes 5505028
  31.8 0.9 %copy-start.3 = (s32[256,112]{1,0:T(8,128)S(1)}, s32[256,112]{1,0:T(8,128)}, u32[]{:S(2)}) copy-start(s32[256,112]{1,0:T(8,128)} %copy.7.bits_ref) | copy-start | bytes 344068
  33.8 1.3 %copy-start = (bf16[256,3584]{1,0:T(8,128)(2,1)}, bf16[256,3584]{1,0:T(8,128)(2,1)S(1)}, u32[]{:S(2)}) copy-start(bf16[256,3584]{1,0:T(8,128)(2,1)S(1)} %get-tuple-element.21.kept_ref) | copy-start | bytes 5505028
  35.1 0.7 copy-start.4
  57.2 4.0 %copy-start.5 = (f32[1,3584]{1,0:T(1,128)S(1)}, f32[1,3584]{1,0:T(1,128)}, u32[]{:S(2)}) copy-start(f32[1,3584]{1,0:T(1,128)} %refs_1_.1) | copy-start | bytes 43012
  57.3 4.4 %collective-permute-start.1 = (bf16[128,256]{1,0:T(8,128)(2,1)S(1)}, bf16[128,256]{1,0:T(8,128)(2,1)S(1)}, u32[]{:S(2)}, u32[]{:S(2)}) collective-permute-start(bf16[128,256]{1,0:T(8,128)(2,1)S(1)} %get-tuple-element.16), channel_id=1, source_target_pairs={{0,1},{1,0},{2,3},{3,2},{4,5},{5,4},{6,7},{7,6},{8,9},{9,8},{10,11... | collective-permute-start | bytes 196616 | tf_op jit(solution)/shard_map/swap_features/ppermute | solution.py:187
  58.7 2.9 %copy-start.1 = (bf16[256,3584]{1,0:T(8,128)(2,1)S(1)}, bf16[256,3584]{1,0:T(8,128)(2,1)}, u32[]{:S(2)}) copy-start(bf16[256,3584]{1,0:T(8,128)(2,1)} %copy-done) | copy-start | bytes 5505028
  60.5 4.4 %collective-permute-start = (bf16[128,256]{1,0:T(8,128)(2,1)S(1)}, bf16[128,256]{1,0:T(8,128)(2,1)S(1)}, u32[]{:S(2)}, u32[]{:S(2)}) collective-permute-start(bf16[128,256]{1,0:T(8,128)(2,1)S(1)} %get-tuple-element.20), channel_id=1, source_target_pairs={{0,1},{1,0},{2,3},{3,2},{4,5},{5,4},{6,7},{7,6},{8,9},{9,8},{10,11... | collective-permute-start | bytes 196616 | tf_op jit(solution)/shard_map/swap_features/ppermute | solution.py:187

commit v7 on v6

--- a/solution.py
+++ b/solution.py
@@ -90,71 +90,60 @@
         copy.wait()
 
 
-def prune_body(weight_ref, bits_ref, *refs):
-    *pruned_refs, rest_ref, kept_ref = refs
+def prune_body(weight_ref, bits_ref, pruned_ref, rest_ref, kept_ref):
     rows, words = bits_ref.shape
-    part = rows // len(pruned_refs)
-    wide = pruned_refs[-1].shape[1]
+    wide = pruned_ref.shape[1]
     lane = lax.broadcasted_iota(jnp.int32, (rows, LANES), 1)
     bits = jnp.concatenate([bits_ref[...], jnp.zeros((rows, LANES - words), jnp.int32)], axis=1)
     for j in range(weight_ref.shape[1] // LANES):
         word = jnp.take_along_axis(bits, lane // 32 + 4 * j, axis=1, mode="promise_in_bounds")
         keep = jnp.bitwise_and(jnp.right_shift(word, lane % 32), 1) == 1
         lo = j * LANES
-        cols = slice(lo, lo + LANES)
-        slab = weight_ref[:, cols].astype(F32)
+        slab = weight_ref[:, lo : lo + LANES].astype(F32)
         pruned = jnp.where(keep, 0.0, slab).astype(BF16)
-        for i, ref in enumerate(pruned_refs):
-            mine = pruned[i * part : (i + 1) * part]
-            if lo < ref.shape[1]:
-                ref[:, cols] = mine
-            else:
-                rest_ref[:, lo - wide : lo - wide + LANES] = mine
-        kept_ref[:, cols] = jnp.where(keep, slab, jnp.inf).astype(BF16)
-
-
-def project_body(routed_ref, pruned_ref, *refs):
-    *rest, part_ref, low_ref = refs[:3] if len(refs) > 2 else refs
+        if lo < wide:
+            pruned_ref[:, lo : lo + LANES] = pruned
+        else:
+            rest_ref[:, lo - wide : lo - wide + LANES] = pruned
+        kept_ref[:, lo : lo + LANES] = jnp.where(keep, slab, jnp.inf).astype(BF16)
+
+
+def project_body(routed_ref, pruned_ref, rest_hbm, part_ref, *refs):
+    *low_refs, rest_ref, sem = refs
     wide = pruned_ref.shape[1]
-    if rest:
-        rest_ref, sem = refs[3:]
-        fetch = pltpu.make_async_copy(rest[0], rest_ref, sem)
-        fetch.start()
+    fetch = pltpu.make_async_copy(rest_hbm, rest_ref, sem)
+    fetch.start()
+    dims = (((1,), (1,)), ((), ()))
     part = lax.dot_general(
-        pruned_ref[...],
-        routed_ref[:, :wide],
-        (((1,), (1,)), ((), ())),
-        preferred_element_type=F32,
-    )
-    if rest:
-        fetch.wait()
-        part = part + lax.dot_general(
-            rest_ref[...],
-            routed_ref[:, wide:],
-            (((1,), (1,)), ((), ())),
-            preferred_element_type=F32,
-        )
+        pruned_ref[...], routed_ref[:, :wide], dims, preferred_element_type=F32
+    )
+    fetch.wait()
+    part = part + lax.dot_general(
+        rest_ref[...], routed_ref[:, wide:], dims, preferred_element_type=F32
+    )
     part_ref[...] = part
-    low_ref[...] = part.astype(BF16)
-
-
-def scale_body(*refs):
-    *routed_refs, damping_ref, scale_ref = refs
+    rows = low_refs[0].shape[0]
+    for i, ref in enumerate(low_refs):
+        ref[...] = part[i * rows : (i + 1) * rows].astype(BF16)
+
+
+def scale_body(routed_ref, damping_ref, kept_hbm, scale_ref, kept_ref, sem):
+    fetch = pltpu.make_async_copy(kept_hbm, kept_ref, sem)
+    fetch.start()
     feats = damping_ref.shape[1]
     for lo in range(0, feats, STEP):
         cols = slice(lo, lo + STEP)
-        diag = damping_ref[:, cols]
-        for ref in routed_refs:
-            rows = ref[:, cols].astype(F32)
-            diag = diag + jnp.sum(rows * rows, axis=0, keepdims=True) * (1.0 / ROWS_E)
+        rows = routed_ref[:, cols].astype(F32)
+        diag = jnp.sum(rows * rows, axis=0, keepdims=True) * (1.0 / ROWS_E) + damping_ref[:, cols]
         scale_ref[:, cols] = (ETA / ROWS_E) / diag
+    fetch.wait()
 
 
 def update_body(at, part_ref, other_ref, routed_ref, scale_ref, kept_ref, *refs):
     out_hbm, out_ref, sems = refs[-3:]
     rows, feats = out_ref.shape
     mine = slice(at, at + rows)
-    projected = (part_ref[...] + other_ref[...].astype(F32)).astype(BF16)
+    projected = (part_ref[mine, :] + other_ref[...].astype(F32)).astype(BF16)
     copies = []
     for i, lo in enumerate(range(0, feats, STEP)):
         cols = slice(lo, lo + STEP)
@@ -233,42 +222,37 @@
     routed = block.reshape(rows, feats)
     part_rows = slab // PARTS
     with jax.named_scope("prune"):
-        *pruned, rest, kept = call(
+        pruned, rest, kept = call(
             prune_body,
-            (shape(part_rows, feats),) * (PARTS - 1)
-            + (shape(part_rows, feats - STEP), shape(part_rows, STEP), shape(slab, feats)),
+            (shape(slab, feats - STEP), shape(slab, STEP), shape(slab, feats)),
             (weight, mask_bits),
             1 << 22,
         )
-    parts = []
-    for i, p in enumerate(pruned):
-        last = i == PARTS - 1
-        if i:
-            p = lax.optimization_barrier((p, parts[-1][1]))[0]
-        with jax.named_scope("project"):
-            parts.append(
-                pl.pallas_call(
-                    project_body,
-                    out_shape=(shape(part_rows, rows, dtype=F32), shape(part_rows, rows)),
-                    in_specs=[vmem, vmem] + [hbm] * last,
-                    out_specs=(vmem, vmem),
-                    scratch_shapes=[pltpu.VMEM(rest.shape, BF16), pltpu.SemaphoreType.DMA] * last,
-                    cost_estimate=pl.CostEstimate(
-                        flops=2 * rows * part_rows * feats,
-                        bytes_accessed=1 << 21,
-                        transcendentals=0,
-                    ),
-                    compiler_params=params,
-                )(routed, p, *([in_hbm(rest)] if last else []))
-            )
+    with jax.named_scope("project"):
+        part, *lows = pl.pallas_call(
+            project_body,
+            out_shape=(shape(slab, rows, dtype=F32),) + (shape(part_rows, rows),) * PARTS,
+            in_specs=[vmem, vmem, hbm],
+            out_specs=(vmem,) * (1 + PARTS),
+            scratch_shapes=[pltpu.VMEM((slab, STEP), BF16), pltpu.SemaphoreType.DMA],
+            cost_estimate=pl.CostEstimate(
+                flops=2 * rows * slab * feats, bytes_accessed=1 << 22, transcendentals=0
+            ),
+            compiler_params=params,
+        )(routed, pruned, in_hbm(rest))
     with jax.named_scope("swap_features"):
-        others = [shift(low, "yl", 1) for _, low in parts]
+        others = [shift(low, "yl", 1) for low in lows]
     with jax.named_scope("scale"):
-        scale = call(
-            scale_body, shape(1, feats, dtype=F32), (routed, damping), 4 * slab * feats
-        )
+        scale, kept = pl.pallas_call(
+            scale_body,
+            out_shape=(shape(1, feats, dtype=F32), shape(slab, feats)),
+            in_specs=[vmem, vmem, hbm],
+            out_specs=(vmem, vmem),
+            scratch_shapes=[pltpu.SemaphoreType.DMA],
+            compiler_params=params,
+        )(routed, damping, in_hbm(kept))
     out = None
-    for i, ((part, _), other) in enumerate(zip(parts, others)):
+    for i, other in enumerate(others):
         operands = (part, other, routed, scale, kept)
         with jax.named_scope("update"):
             out = pl.pallas_call(

time: 66.4 us -> 65.9 us (level)
  local copies, waits for them, and re-layouts: 5.08 us -> 3.56 us
    unnamed x15 -> x11, local copies, waits for them, and re-layouts: 5.08 us -> 3.56 us
    all_to_all x1, waiting for transfers between devices: 20.8 us -> 22.3 us  [local(): lax.all_to_all(packed.reshape(dests, -1, feats), near, split_axis=0, conc...]
    ppermute x2, waiting for transfers between devices: 2.21 us -> 1.31 us  [shift(): return lax.ppermute(x, axis, [(i, (i + step) % n) for i in range(n)])]
    pallas_call x2, Pallas kernels: 2.48 us -> 3.15 us  [the longest x1 1.64 us: local(): pl.pallas_call(project_body, out_shape=(shape(slab, rows, dtype=F32),) +...]
  transfers between devices with their start and end apart: 3 -> 3, of which waited for: 3 -> 2; matrix products, arithmetic and copies ran while one was open for 1% -> 0% of each run, Pallas kernels for 6% -> 6%
where the time goes in v7:
time: 65.9 us; the launch traced here: 65.6 us
  waiting for transfers between devices  23.6 us (36%)
  blocking collectives  19.7 us (30%)
  Pallas kernels  9.48 us (14%)
  starting transfers between devices  9.27 us (14%)
  local copies, waits for them, and re-layouts  3.56 us (5%)
    all_to_all x1, waiting for transfers between devices, local(): lax.all_to_all(packed.reshape(dests, -1, feats), near, split_axis=0, conc...  22.3 us
    all_gather x1, blocking collectives, local(): held = lax.all_gather(own, 'zh', tiled=True)  19.7 us
    all_to_all x1, starting transfers between devices, local(): lax.all_to_all(packed.reshape(dests, -1, feats), near, split_axis=0, conc...  7.15 us
    unnamed x11, local copies, waits for them, and re-layouts  3.56 us
    pallas_call x2, Pallas kernels, local(): pl.pallas_call(functools.partial(update_body, i * part_rows), out_shape=p...  2.5 us
    ppermute x2, starting transfers between devices, shift(): return lax.ppermute(x, axis, [(i, (i + step) % n) for i in range(n)])  2.11 us
    pallas_call x1, Pallas kernels, local(): pl.pallas_call(functools.partial(pack_body, tok_rows, top), out_shape=plt...  1.78 us
    pallas_call x1, Pallas kernels, local(): pl.pallas_call(project_body, out_shape=(shape(slab, rows, dtype=F32),) +...  1.64 us
  transfers between devices with their start and end apart: 3, of which 2 were waited for; matrix products, arithmetic and copies ran while one was open for 0% of the time, Pallas kernels for 6%

profile of v7, /device:TPU:8, one launch (start us, length us, event | category | flops | bytes accessed | tf_op | source)
XLA Modules:
  0.0 65.6 jit_solution(5446403584904039432)
XLA Ops:
  0.0 0.9 %tag.1 = bf16[16,3712]{1,0:T(8,128)(2,1)S(1)} custom-call(bf16[16,3584]{1,0:T(8,128)(2,1)} %tokens_hbm.1, s32[8,16]{1,0:T(8,128)} %bitcast.12), custom_call_target="tpu_custom_call" | custom-call | tf_op jit(solution)/shard_map/tag/pallas_call | solution.py:193
  0.9 19.7 %all_gather.3.held = bf16[64,3712]{1,0:T(8,128)(2,1)S(1)} all-gather(bf16[16,3712]{1,0:T(8,128)(2,1)S(1)} %tag.1), channel_id=1, replica_groups=mesh['zh'=4,'zl'=2,'yh'=2,'x'=4,'core'=2,'yl'=2] {'zh'}, dimensions={0}, use_global_device_ids=true | all-gather | bytes 593920 | tf_op jit(solution)/shard_map/gather/all_gather | solution.py:205
  20.6 1.8 %pack.1 = bf16[256,3584]{1,0:T(8,128)(2,1)} custom-call(s32[1]{0:T(128)} %bitcast.first_ref, bf16[64,3712]{1,0:T(8,128)(2,1)S(1)} %all_gather.3.held), custom_call_target="tpu_custom_call" | custom-call | tf_op jit(solution)/shard_map/pack/pallas_call | solution.py:207
  22.4 0.0 copy-start.4
  22.4 7.2 %all-to-all-start = ((bf16[32,8,3584]{2,1,0:T(8,128)(2,1)}), bf16[32,8,3584]{2,1,0:T(8,128)(2,1)S(1)}, u32[]{:S(2)}, u32[]{:S(2)}) async-start(bf16[32,8,3584]{2,1,0:T(8,128)(2,1)} %bitcast.11), calls=%async_computation | async-start | bytes 3670016 | tf_op jit(solution)/shard_map/route/all_to_all | solution.py:219
  29.6 0.0 copy-done.4
  29.6 0.1 copy.7.bits_ref
  29.7 0.0 copy-start
  29.7 1.5 %copy-done = bf16[1,256,3584]{2,1,0:T(8,128)(2,1)S(1)} copy-done((bf16[1,256,3584]{2,1,0:T(8,128)(2,1)S(1)}, bf16[1,256,3584]{2,1,0:T(8,128)(2,1)}, u32[]{:S(2)}) %copy-start) | copy-done | bytes 1835032
  31.2 1.1 %prune.1 = (bf16[256,3072]{1,0:T(8,128)(2,1)S(1)}, bf16[256,512]{1,0:T(8,128)(2,1)S(1)}, bf16[256,3584]{1,0:T(8,128)(2,1)S(1)}) custom-call(bf16[256,3584]{1,0:T(8,128)(2,1)S(1)} %bitcast.10, s32[256,112]{1,0:T(8,128)S(1)} %copy.7.bits_ref), custom_call_target="tpu_custom_call" | custom-call | flops 4194304 | bytes 5619712 | tf_op jit(solution)/shard_map/prune/pallas_call | solution.py:25
  32.3 0.0 copy-start.1
  32.3 1.2 %copy-done.1 = bf16[256,3584]{1,0:T(8,128)(2,1)} copy-done((bf16[256,3584]{1,0:T(8,128)(2,1)}, bf16[256,3584]{1,0:T(8,128)(2,1)S(1)}, u32[]{:S(2)}) %copy-start.1) | copy-done | bytes 1835032
  33.5 0.0 copy-start.2
  33.6 0.7 %copy-done.2 = bf16[256,512]{1,0:T(8,128)(2,1)} copy-done((bf16[256,512]{1,0:T(8,128)(2,1)}, bf16[256,512]{1,0:T(8,128)(2,1)S(1)}, u32[]{:S(2)}) %copy-start.2) | copy-done | bytes 262168
  34.3 22.3 %all-to-all-done = bf16[32,8,3584]{2,1,0:T(8,128)(2,1)S(1)} async-done(((bf16[32,8,3584]{2,1,0:T(8,128)(2,1)}), bf16[32,8,3584]{2,1,0:T(8,128)(2,1)S(1)}, u32[]{:S(2)}, u32[]{:S(2)}) %all-to-all-start) | async-done | bytes 1835040 | tf_op jit(solution)/shard_map/route/all_to_all | solution.py:219
  56.5 1.6 %project.1 = (f32[256,256]{1,0:T(8,128)S(1)}, bf16[128,256]{1,0:T(8,128)(2,1)S(1)}, bf16[128,256]{1,0:T(8,128)(2,1)S(1)}) custom-call(bf16[256,3584]{1,0:T(8,128)(2,1)S(1)} %bitcast.6, bf16[256,3072]{1,0:T(8,128)(2,1)S(1)} %get-tuple-element.13.pruned_ref, bf16[256,512]{1,0:T(8,128)(2,1)} %copy-done.2), custom_call_target="tpu_custom_call" | custom-call | flops 469762048 | bytes 4194304 | tf_op jit(solution)/shard_map/project/pallas_call | solution.py:232
  58.2 1.4 %collective-permute-start.1 = (bf16[128,256]{1,0:T(8,128)(2,1)S(1)}, bf16[128,256]{1,0:T(8,128)(2,1)S(1)}, u32[]{:S(2)}, u32[]{:S(2)}) collective-permute-start(bf16[128,256]{1,0:T(8,128)(2,1)S(1)} %get-tuple-element.20), channel_id=1, source_target_pairs={{0,1},{1,0},{2,3},{3,2},{4,5},{5,4},{6,7},{7,6},{8,9},{9,8},{10,11... | collective-permute-start | bytes 196616 | tf_op jit(solution)/shard_map/swap_features/ppermute | solution.py:176
  59.6 0.7 %collective-permute-start = (bf16[128,256]{1,0:T(8,128)(2,1)S(1)}, bf16[128,256]{1,0:T(8,128)(2,1)S(1)}, u32[]{:S(2)}, u32[]{:S(2)}) collective-permute-start(bf16[128,256]{1,0:T(8,128)(2,1)S(1)} %get-tuple-element.16), channel_id=1, source_target_pairs={{0,1},{1,0},{2,3},{3,2},{4,5},{5,4},{6,7},{7,6},{8,9},{9,8},{10,11... | collective-permute-start | bytes 196616 | tf_op jit(solution)/shard_map/swap_features/ppermute | solution.py:176
  60.3 0.0 copy-done.3
  60.3 1.5 %scale.1 = (f32[1,3584]{1,0:T(1,128)S(1)}, bf16[256,3584]{1,0:T(8,128)(2,1)S(1)}) custom-call(bf16[256,3584]{1,0:T(8,128)(2,1)S(1)} %bitcast.7, f32[1,3584]{1,0:T(1,128)S(1)} %copy-done.3, bf16[256,3584]{1,0:T(8,128)(2,1)} %copy-done.1), custom_call_target="tpu_custom_call" | custom-call | tf_op jit(solution)/shard_map/scale/pallas_call | solution.py:246
  61.8 1.3 %collective-permute-done.1.other_ref = bf16[128,256]{1,0:T(8,128)(2,1)S(1)} collective-permute-done((bf16[128,256]{1,0:T(8,128)(2,1)S(1)}, bf16[128,256]{1,0:T(8,128)(2,1)S(1)}, u32[]{:S(2)}, u32[]{:S(2)}) %collective-permute-start.1) | collective-permute-done | bytes 65568 | tf_op jit(solution)/shard_map/swap_features/ppermute | solution.py:176
  63.1 1.2 %update.2.refs_0_ = bf16[256,3584]{1,0:T(8,128)(2,1)} custom-call(f32[256,256]{1,0:T(8,128)S(1)} %get-tuple-element.15.part_ref, bf16[128,256]{1,0:T(8,128)(2,1)S(1)} %collective-permute-done.1.other_ref, bf16[256,3584]{1,0:T(8,128)(2,1)S(1)} %bitcast.8, f32[1,3584]{1,0:T(1,128)S(1)} %get-tuple-element.18.scale_ref, ...), custom_call_target="tpu_custom_call" | custom-call | flops 234881024 | bytes 4194304 | tf_op jit(solution)/shard_map/update/pallas_call | solution.py:258
  64.4 0.0 collective-permute-done.other_ref
  64.4 1.3 %update.3 = bf16[256,3584]{1,0:T(8,128)(2,1)} custom-call(f32[256,256]{1,0:T(8,128)S(1)} %get-tuple-element.15.part_ref, bf16[128,256]{1,0:T(8,128)(2,1)S(1)} %collective-permute-done.other_ref, bf16[256,3584]{1,0:T(8,128)(2,1)S(1)} %bitcast.9, f32[1,3584]{1,0:T(1,128)S(1)} %get-tuple-element.18.scale_ref, ...), custom_call_target="tpu_custom_call", output_to_operand_aliasing={{}: (5, {})} | custom-call | flops 234881024 | bytes 4194304 | tf_op jit(solution)/shard_map/update/pallas_call | solution.py:258
  (1 shorter events, 0.0 us)
Async XLA Ops:
  22.4 7.2 %copy-start.4 = (s32[256,112]{0,1:T(8,128)S(1)}, s32[256,112]{0,1:T(8,128)}, u32[]{:S(2)}) copy-start(s32[256,112]{0,1:T(8,128)} %param.8) | copy-start | bytes 344068
  22.4 34.1 %all-to-all-start = ((bf16[32,8,3584]{2,1,0:T(8,128)(2,1)}), bf16[32,8,3584]{2,1,0:T(8,128)(2,1)S(1)}, u32[]{:S(2)}, u32[]{:S(2)}) async-start(bf16[32,8,3584]{2,1,0:T(8,128)(2,1)} %bitcast.11), calls=%async_computation | async-start | bytes 3670016 | tf_op jit(solution)/shard_map/route/all_to_all | solution.py:219
  29.7 1.5 %copy-start = (bf16[1,256,3584]{2,1,0:T(8,128)(2,1)S(1)}, bf16[1,256,3584]{2,1,0:T(8,128)(2,1)}, u32[]{:S(2)}) copy-start(bf16[1,256,3584]{2,1,0:T(8,128)(2,1)} %param.7) | copy-start | bytes 5505028
  32.3 1.3 %copy-start.1 = (bf16[256,3584]{1,0:T(8,128)(2,1)}, bf16[256,3584]{1,0:T(8,128)(2,1)S(1)}, u32[]{:S(2)}) copy-start(bf16[256,3584]{1,0:T(8,128)(2,1)S(1)} %get-tuple-element.17.kept_hbm) | copy-start | bytes 5505028
  33.5 0.7 %copy-start.2 = (bf16[256,512]{1,0:T(8,128)(2,1)}, bf16[256,512]{1,0:T(8,128)(2,1)S(1)}, u32[]{:S(2)}) copy-start(bf16[256,512]{1,0:T(8,128)(2,1)S(1)} %get-tuple-element.14.rest_hbm) | copy-start | bytes 786436
  56.5 3.8 %copy-start.3 = (f32[1,3584]{1,0:T(1,128)S(1)}, f32[1,3584]{1,0:T(1,128)}, u32[]{:S(2)}) copy-start(f32[1,3584]{1,0:T(1,128)} %damping_ref.1) | copy-start | bytes 43012
  58.2 4.9 %collective-permute-start.1 = (bf16[128,256]{1,0:T(8,128)(2,1)S(1)}, bf16[128,256]{1,0:T(8,128)(2,1)S(1)}, u32[]{:S(2)}, u32[]{:S(2)}) collective-permute-start(bf16[128,256]{1,0:T(8,128)(2,1)S(1)} %get-tuple-element.20), channel_id=1, source_target_pairs={{0,1},{1,0},{2,3},{3,2},{4,5},{5,4},{6,7},{7,6},{8,9},{9,8},{10,11... | collective-permute-start | bytes 196616 | tf_op jit(solution)/shard_map/swap_features/ppermute | solution.py:176
  59.6 4.8 %collective-permute-start = (bf16[128,256]{1,0:T(8,128)(2,1)S(1)}, bf16[128,256]{1,0:T(8,128)(2,1)S(1)}, u32[]{:S(2)}, u32[]{:S(2)}) collective-permute-start(bf16[128,256]{1,0:T(8,128)(2,1)S(1)} %get-tuple-element.16), channel_id=1, source_target_pairs={{0,1},{1,0},{2,3},{3,2},{4,5},{5,4},{6,7},{7,6},{8,9},{9,8},{10,11... | collective-permute-start | bytes 196616 | tf_op jit(solution)/shard_map/swap_features/ppermute | solution.py:176

commit v8 on v7

--- a/solution.py
+++ b/solution.py
@@ -12,7 +12,6 @@
 CAP = 2
 LANES = 128
 STEP = 512
-PARTS = 2
 VMEM = 16 * 2**20
 F32 = jnp.float32
 BF16 = jnp.bfloat16
@@ -108,23 +107,24 @@
         kept_ref[:, lo : lo + LANES] = jnp.where(keep, slab, jnp.inf).astype(BF16)
 
 
-def project_body(routed_ref, pruned_ref, rest_hbm, part_ref, *refs):
-    *low_refs, rest_ref, sem = refs
-    wide = pruned_ref.shape[1]
-    fetch = pltpu.make_async_copy(rest_hbm, rest_ref, sem)
-    fetch.start()
-    dims = (((1,), (1,)), ((), ()))
-    part = lax.dot_general(
-        pruned_ref[...], routed_ref[:, :wide], dims, preferred_element_type=F32
-    )
-    fetch.wait()
-    part = part + lax.dot_general(
-        rest_ref[...], routed_ref[:, wide:], dims, preferred_element_type=F32
+def project_body(routed_ref, pruned_ref, part_ref):
+    part_ref[...] = lax.dot_general(
+        pruned_ref[...],
+        routed_ref[:, : pruned_ref.shape[1]],
+        (((1,), (1,)), ((), ())),
+        preferred_element_type=F32,
+    )
+
+
+def finish_body(routed_ref, rest_ref, first_ref, part_ref, low_ref):
+    part = first_ref[...] + lax.dot_general(
+        rest_ref[...],
+        routed_ref[:, routed_ref.shape[1] - rest_ref.shape[1] :],
+        (((1,), (1,)), ((), ())),
+        preferred_element_type=F32,
     )
     part_ref[...] = part
-    rows = low_refs[0].shape[0]
-    for i, ref in enumerate(low_refs):
-        ref[...] = part[i * rows : (i + 1) * rows].astype(BF16)
+    low_ref[...] = part.astype(BF16)
 
 
 def scale_body(routed_ref, damping_ref, kept_hbm, scale_ref, kept_ref, sem):
@@ -139,25 +139,17 @@
     fetch.wait()
 
 
-def update_body(at, part_ref, other_ref, routed_ref, scale_ref, kept_ref, *refs):
-    out_hbm, out_ref, sems = refs[-3:]
-    rows, feats = out_ref.shape
-    mine = slice(at, at + rows)
-    projected = (part_ref[mine, :] + other_ref[...].astype(F32)).astype(BF16)
+def update_body(part_ref, other_ref, routed_ref, scale_ref, kept_ref, out_hbm, out_ref, sems):
+    projected = (part_ref[...] + other_ref[...].astype(F32)).astype(BF16)
     copies = []
-    for i, lo in enumerate(range(0, feats, STEP)):
+    for i, lo in enumerate(range(0, out_ref.shape[1], STEP)):
         cols = slice(lo, lo + STEP)
         comp = jnp.dot(projected, routed_ref[:, cols], preferred_element_type=F32)
-        kept = kept_ref[mine, cols].astype(F32)
+        kept = kept_ref[:, cols].astype(F32)
         updated = jnp.where(kept < jnp.inf, kept + comp * scale_ref[:, cols], 0.0)
         out_ref[:, cols] = updated.astype(BF16)
-        copies.append(
-            pltpu.make_async_copy(
-                out_ref.at[:, pl.ds(lo, STEP)],
-                out_hbm.at[pl.ds(at, rows), pl.ds(lo, STEP)],
-                sems.at[i],
-            )
-        )
+        block = (slice(None), pl.ds(lo, STEP))
+        copies.append(pltpu.make_async_copy(out_ref.at[block], out_hbm.at[block], sems.at[i]))
         copies[-1].start()
     for copy in copies:
         copy.wait()
@@ -220,7 +212,6 @@
             packed.reshape(dests, -1, feats), near, split_axis=0, concat_axis=0, tiled=True
         )
     routed = block.reshape(rows, feats)
-    part_rows = slab // PARTS
     with jax.named_scope("prune"):
         pruned, rest, kept = call(
             prune_body,
@@ -229,19 +220,20 @@
             1 << 22,
         )
     with jax.named_scope("project"):
-        part, *lows = pl.pallas_call(
+        most = call(
             project_body,
-            out_shape=(shape(slab, rows, dtype=F32),) + (shape(part_rows, rows),) * PARTS,
-            in_specs=[vmem, vmem, hbm],
-            out_specs=(vmem,) * (1 + PARTS),
-            scratch_shapes=[pltpu.VMEM((slab, STEP), BF16), pltpu.SemaphoreType.DMA],
-            cost_estimate=pl.CostEstimate(
-                flops=2 * rows * slab * feats, bytes_accessed=1 << 22, transcendentals=0
-            ),
-            compiler_params=params,
-        )(routed, pruned, in_hbm(rest))
+            shape(slab, rows, dtype=F32),
+            (routed, pruned),
+            2 * rows * slab * pruned.shape[1],
+        )
+        part, low = call(
+            finish_body,
+            (shape(slab, rows, dtype=F32), shape(slab, rows)),
+            (routed, rest, most),
+            2 * rows * slab * rest.shape[1],
+        )
     with jax.named_scope("swap_features"):
-        others = [shift(low, "yl", 1) for low in lows]
+        other = shift(low, "yl", 1)
     with jax.named_scope("scale"):
         scale, kept = pl.pallas_call(
             scale_body,
@@ -251,27 +243,19 @@
             scratch_shapes=[pltpu.SemaphoreType.DMA],
             compiler_params=params,
         )(routed, damping, in_hbm(kept))
-    out = None
-    for i, other in enumerate(others):
+    with jax.named_scope("update"):
         operands = (part, other, routed, scale, kept)
-        with jax.named_scope("update"):
-            out = pl.pallas_call(
-                functools.partial(update_body, i * part_rows),
-                out_shape=pltpu.HBM((slab, feats), BF16),
-                in_specs=[vmem] * len(operands) + [hbm] * (i > 0),
-                out_specs=hbm,
-                scratch_shapes=[
-                    pltpu.VMEM((part_rows, feats), BF16),
-                    pltpu.SemaphoreType.DMA((feats // STEP,)),
-                ],
-                input_output_aliases={len(operands): 0} if i else {},
-                cost_estimate=pl.CostEstimate(
-                    flops=2 * rows * part_rows * feats,
-                    bytes_accessed=1 << 22,
-                    transcendentals=0,
-                ),
-                compiler_params=params,
-            )(*operands, *([in_hbm(out)] if i else []))
+        out = pl.pallas_call(
+            update_body,
+            out_shape=shape(slab, feats),
+            in_specs=[vmem] * len(operands),
+            out_specs=hbm,
+            scratch_shapes=[
+                pltpu.VMEM((slab, feats), BF16),
+                pltpu.SemaphoreType.DMA((feats // STEP,)),
+            ],
+            compiler_params=params,
+        )(*operands)
     return out.reshape(1, slab, feats)
 
 

time: 65.9 us -> 65.7 us (level); the launches traced: 65.6 us -> 64.7 us
  Pallas kernels: 9.48 us -> 7.83 us
  waiting for transfers between devices: 23.6 us -> 24.6 us
  starting transfers between devices: 9.27 us -> 8.59 us
    pallas_call x3 -> x1, Pallas kernels: 4.14 us -> 1.64 us  [local(): pl.pallas_call(update_body, out_shape=shape(slab, feats), in_specs=[vmem]...]
    ppermute x2 -> x1, waiting for transfers between devices: 1.31 us -> 2.31 us  [shift(): return lax.ppermute(x, axis, [(i, (i + step) % n) for i in range(n)])]
    pallas_call x1 -> x3, Pallas kernels: 1.11 us -> 1.98 us  [call(): pl.pallas_call(body, out_shape=out_shape, in_specs=[pl.BlockSpec(memory_s...]
    ppermute x2 -> x1, starting transfers between devices: 2.11 us -> 1.44 us  [shift(): return lax.ppermute(x, axis, [(i, (i + step) % n) for i in range(n)])]
    unnamed x11 -> x13, local copies, waits for them, and re-layouts: 3.56 us -> 3.89 us
  transfers between devices with their start and end apart: 3 -> 2, of which waited for: 2 -> 2; matrix products, arithmetic and copies ran while one was open for 0% -> 0% of each run, Pallas kernels for 6% -> 4%
where the time goes in v8:
time: 65.7 us; the launch traced here: 64.7 us
  waiting for transfers between devices  24.6 us (37%)
  blocking collectives  19.7 us (30%)
  starting transfers between devices  8.59 us (13%)
  Pallas kernels  7.83 us (12%)
  local copies, waits for them, and re-layouts  3.89 us (6%)
    all_to_all x1, waiting for transfers between devices, local(): lax.all_to_all(packed.reshape(dests, -1, feats), near, split_axis=0, conc...  22.3 us
    all_gather x1, blocking collectives, local(): held = lax.all_gather(own, 'zh', tiled=True)  19.7 us
    all_to_all x1, starting transfers between devices, local(): lax.all_to_all(packed.reshape(dests, -1, feats), near, split_axis=0, conc...  7.15 us
    unnamed x13, local copies, waits for them, and re-layouts  3.89 us
    ppermute x1, waiting for transfers between devices, shift(): return lax.ppermute(x, axis, [(i, (i + step) % n) for i in range(n)])  2.31 us
    pallas_call x3, Pallas kernels, call(): pl.pallas_call(body, out_shape=out_shape, in_specs=[pl.BlockSpec(memory_s...  1.98 us
    pallas_call x1, Pallas kernels, local(): pl.pallas_call(functools.partial(pack_body, tok_rows, top), out_shape=plt...  1.78 us
    pallas_call x1, Pallas kernels, local(): pl.pallas_call(update_body, out_shape=shape(slab, feats), in_specs=[vmem]...  1.64 us
  transfers between devices with their start and end apart: 2, of which 2 were waited for; matrix products, arithmetic and copies ran while one was open for 0% of the time, Pallas kernels for 4%

profile of v8, /device:TPU:8, one launch (start us, length us, event | category | flops | bytes accessed | tf_op | source)
XLA Modules:
  0.0 64.7 jit_solution(17275928289136368581)
XLA Ops:
  0.0 0.9 %tag.1 = bf16[16,3712]{1,0:T(8,128)(2,1)S(1)} custom-call(bf16[16,3584]{1,0:T(8,128)(2,1)} %tokens_hbm.1, s32[8,16]{1,0:T(8,128)} %bitcast.12), custom_call_target="tpu_custom_call" | custom-call | tf_op jit(solution)/shard_map/tag/pallas_call | solution.py:185
  0.9 19.7 %all_gather.3.held = bf16[64,3712]{1,0:T(8,128)(2,1)S(1)} all-gather(bf16[16,3712]{1,0:T(8,128)(2,1)S(1)} %tag.1), channel_id=1, replica_groups=mesh['zh'=4,'zl'=2,'yh'=2,'x'=4,'core'=2,'yl'=2] {'zh'}, dimensions={0}, use_global_device_ids=true | all-gather | bytes 593920 | tf_op jit(solution)/shard_map/gather/all_gather | solution.py:197
  20.6 1.8 %pack.1 = bf16[256,3584]{1,0:T(8,128)(2,1)} custom-call(s32[1]{0:T(128)} %bitcast.first_ref, bf16[64,3712]{1,0:T(8,128)(2,1)S(1)} %all_gather.3.held), custom_call_target="tpu_custom_call" | custom-call | tf_op jit(solution)/shard_map/pack/pallas_call | solution.py:199
  22.4 0.0 copy-start.5
  22.4 7.2 %all-to-all-start = ((bf16[32,8,3584]{2,1,0:T(8,128)(2,1)}), bf16[32,8,3584]{2,1,0:T(8,128)(2,1)S(1)}, u32[]{:S(2)}, u32[]{:S(2)}) async-start(bf16[32,8,3584]{2,1,0:T(8,128)(2,1)} %bitcast.11), calls=%async_computation | async-start | bytes 3670016 | tf_op jit(solution)/shard_map/route/all_to_all | solution.py:211
  29.6 0.0 copy-done.5
  29.6 0.1 copy.6.bits_ref
  29.7 0.0 copy-start
  29.7 1.5 %copy-done = bf16[1,256,3584]{2,1,0:T(8,128)(2,1)S(1)} copy-done((bf16[1,256,3584]{2,1,0:T(8,128)(2,1)S(1)}, bf16[1,256,3584]{2,1,0:T(8,128)(2,1)}, u32[]{:S(2)}) %copy-start) | copy-done | bytes 1835032
  31.2 1.1 %prune.1 = (bf16[256,3072]{1,0:T(8,128)(2,1)S(1)}, bf16[256,512]{1,0:T(8,128)(2,1)S(1)}, bf16[256,3584]{1,0:T(8,128)(2,1)S(1)}) custom-call(bf16[256,3584]{1,0:T(8,128)(2,1)S(1)} %bitcast.10, s32[256,112]{1,0:T(8,128)S(1)} %copy.6.bits_ref), custom_call_target="tpu_custom_call" | custom-call | flops 4194304 | bytes 5619712 | tf_op jit(solution)/shard_map/prune/pallas_call | solution.py:24
  32.3 0.0 copy-start.1
  32.3 1.2 %copy-done.1 = bf16[256,3584]{1,0:T(8,128)(2,1)} copy-done((bf16[256,3584]{1,0:T(8,128)(2,1)}, bf16[256,3584]{1,0:T(8,128)(2,1)S(1)}, u32[]{:S(2)}) %copy-start.1) | copy-done | bytes 1835032
  33.5 0.0 copy-start.2
  33.6 0.7 %copy-done.2 = bf16[256,512]{1,0:T(8,128)(2,1)} copy-done((bf16[256,512]{1,0:T(8,128)(2,1)}, bf16[256,512]{1,0:T(8,128)(2,1)S(1)}, u32[]{:S(2)}) %copy-start.2) | copy-done | bytes 262168
  34.3 22.3 %all-to-all-done = bf16[32,8,3584]{2,1,0:T(8,128)(2,1)S(1)} async-done(((bf16[32,8,3584]{2,1,0:T(8,128)(2,1)}), bf16[32,8,3584]{2,1,0:T(8,128)(2,1)S(1)}, u32[]{:S(2)}, u32[]{:S(2)}) %all-to-all-start) | async-done | bytes 1835040 | tf_op jit(solution)/shard_map/route/all_to_all | solution.py:211
  56.5 0.6 project.2.first_ref
  57.1 0.0 copy-start.4
  57.1 0.3 copy-done.3
  57.5 0.3 project.3
  57.7 1.4 %collective-permute-start = (bf16[256,256]{1,0:T(8,128)(2,1)S(1)}, bf16[256,256]{1,0:T(8,128)(2,1)S(1)}, u32[]{:S(2)}, u32[]{:S(2)}) collective-permute-start(bf16[256,256]{1,0:T(8,128)(2,1)S(1)} %get-tuple-element.15), channel_id=1, source_target_pairs={{0,1},{1,0},{2,3},{3,2},{4,5},{5,4},{6,7},{7,6},{8,9},{9,8},{10,11... | collective-permute-start | bytes 393224 | tf_op jit(solution)/shard_map/swap_features/ppermute | solution.py:168
  59.2 0.0 copy-done.4
  59.2 1.5 %scale.1 = (f32[1,3584]{1,0:T(1,128)S(1)}, bf16[256,3584]{1,0:T(8,128)(2,1)S(1)}) custom-call(bf16[256,3584]{1,0:T(8,128)(2,1)S(1)} %bitcast.8, f32[1,3584]{1,0:T(1,128)S(1)} %copy-done.4, bf16[256,3584]{1,0:T(8,128)(2,1)} %copy-done.1), custom_call_target="tpu_custom_call" | custom-call | tf_op jit(solution)/shard_map/scale/pallas_call | solution.py:238
  60.7 2.3 %collective-permute-done.other_ref = bf16[256,256]{1,0:T(8,128)(2,1)S(1)} collective-permute-done((bf16[256,256]{1,0:T(8,128)(2,1)S(1)}, bf16[256,256]{1,0:T(8,128)(2,1)S(1)}, u32[]{:S(2)}, u32[]{:S(2)}) %collective-permute-start) | collective-permute-done | bytes 131104 | tf_op jit(solution)/shard_map/swap_features/ppermute | solution.py:168
  63.0 1.6 %update.1 = bf16[256,3584]{1,0:T(8,128)(2,1)} custom-call(f32[256,256]{1,0:T(8,128)S(1)} %get-tuple-element.14.part_ref, bf16[256,256]{1,0:T(8,128)(2,1)S(1)} %collective-permute-done.other_ref, bf16[256,3584]{1,0:T(8,128)(2,1)S(1)} %bitcast.9, f32[1,3584]{1,0:T(1,128)S(1)} %get-tuple-element.17.scale_ref, bf16[256,3584]{1,0:T(8,128)(2,1)S(1)} %get-tuple-element.18.kept_ref), custom_call_target="tpu_custom_call" | custom-call | tf_op jit(solution)/shard_map/update/pallas_call | solution.py:248
  (1 shorter events, 0.0 us)
Async XLA Ops:
  22.4 7.2 %copy-start.5 = (s32[256,112]{0,1:T(8,128)S(1)}, s32[256,112]{0,1:T(8,128)}, u32[]{:S(2)}) copy-start(s32[256,112]{0,1:T(8,128)} %param.8) | copy-start | bytes 344068
  22.4 34.1 %all-to-all-start = ((bf16[32,8,3584]{2,1,0:T(8,128)(2,1)}), bf16[32,8,3584]{2,1,0:T(8,128)(2,1)S(1)}, u32[]{:S(2)}, u32[]{:S(2)}) async-start(bf16[32,8,3584]{2,1,0:T(8,128)(2,1)} %bitcast.11), calls=%async_computation | async-start | bytes 3670016 | tf_op jit(solution)/shard_map/route/all_to_all | solution.py:211
  29.7 1.5 %copy-start = (bf16[1,256,3584]{2,1,0:T(8,128)(2,1)S(1)}, bf16[1,256,3584]{2,1,0:T(8,128)(2,1)}, u32[]{:S(2)}) copy-start(bf16[1,256,3584]{2,1,0:T(8,128)(2,1)} %param.7) | copy-start | bytes 5505028
  32.3 1.3 %copy-start.1 = (bf16[256,3584]{1,0:T(8,128)(2,1)}, bf16[256,3584]{1,0:T(8,128)(2,1)S(1)}, u32[]{:S(2)}) copy-start(bf16[256,3584]{1,0:T(8,128)(2,1)S(1)} %get-tuple-element.16.kept_hbm) | copy-start | bytes 5505028
  33.5 0.7 %copy-start.2 = (bf16[256,512]{1,0:T(8,128)(2,1)}, bf16[256,512]{1,0:T(8,128)(2,1)S(1)}, u32[]{:S(2)}) copy-start(bf16[256,512]{1,0:T(8,128)(2,1)S(1)} %get-tuple-element.12.rest_ref) | copy-start | bytes 786436
  56.5 1.0 %copy-start.3 = (bf16[256,512]{1,0:T(8,128)(2,1)S(1)}, bf16[256,512]{1,0:T(8,128)(2,1)}, u32[]{:S(2)}) copy-start(bf16[256,512]{1,0:T(8,128)(2,1)} %copy-done.2) | copy-start | bytes 786436
  57.1 2.1 %copy-start.4 = (f32[1,3584]{1,0:T(1,128)S(1)}, f32[1,3584]{1,0:T(1,128)}, u32[]{:S(2)}) copy-start(f32[1,3584]{1,0:T(1,128)} %damping_ref.1) | copy-start | bytes 43012
  57.7 5.3 %collective-permute-start = (bf16[256,256]{1,0:T(8,128)(2,1)S(1)}, bf16[256,256]{1,0:T(8,128)(2,1)S(1)}, u32[]{:S(2)}, u32[]{:S(2)}) collective-permute-start(bf16[256,256]{1,0:T(8,128)(2,1)S(1)} %get-tuple-element.15), channel_id=1, source_target_pairs={{0,1},{1,0},{2,3},{3,2},{4,5},{5,4},{6,7},{7,6},{8,9},{9,8},{10,11... | collective-permute-start | bytes 393224 | tf_op jit(solution)/shard_map/swap_features/ppermute | solution.py:168

commit v9 on v8

--- a/solution.py
+++ b/solution.py
@@ -12,6 +12,7 @@
 CAP = 2
 LANES = 128
 STEP = 512
+REST = 256
 VMEM = 16 * 2**20
 F32 = jnp.float32
 BF16 = jnp.bfloat16
@@ -145,9 +146,9 @@
     for i, lo in enumerate(range(0, out_ref.shape[1], STEP)):
         cols = slice(lo, lo + STEP)
         comp = jnp.dot(projected, routed_ref[:, cols], preferred_element_type=F32)
-        kept = kept_ref[:, cols].astype(F32)
-        updated = jnp.where(kept < jnp.inf, kept + comp * scale_ref[:, cols], 0.0)
-        out_ref[:, cols] = updated.astype(BF16)
+        kept = kept_ref[:, cols]
+        updated = (kept.astype(F32) + comp * scale_ref[:, cols]).astype(BF16)
+        out_ref[:, cols] = jnp.where(kept < jnp.inf, updated, jnp.zeros_like(updated))
         block = (slice(None), pl.ds(lo, STEP))
         copies.append(pltpu.make_async_copy(out_ref.at[block], out_hbm.at[block], sems.at[i]))
         copies[-1].start()
@@ -215,7 +216,7 @@
     with jax.named_scope("prune"):
         pruned, rest, kept = call(
             prune_body,
-            (shape(slab, feats - STEP), shape(slab, STEP), shape(slab, feats)),
+            (shape(slab, feats - REST), shape(slab, REST), shape(slab, feats)),
             (weight, mask_bits),
             1 << 22,
         )

time: 65.7 us -> 65.6 us (level)
  waiting for transfers between devices: 24.6 us -> 23.1 us
  local copies, waits for them, and re-layouts: 3.89 us -> 5.32 us
    all_to_all x1, waiting for transfers between devices: 22.3 us -> 20.8 us  [local(): lax.all_to_all(packed.reshape(dests, -1, feats), near, split_axis=0, conc...]
    unnamed x13 -> x15, local copies, waits for them, and re-layouts: 3.89 us -> 5.32 us
  transfers between devices with their start and end apart: 2 -> 2, of which waited for: 2 -> 2; matrix products, arithmetic and copies ran while one was open for 0% -> 1% of each run, Pallas kernels for 4% -> 4%
where the time goes in v9:
time: 65.6 us; the launch traced here: 64.5 us
  waiting for transfers between devices  23.1 us (35%)
  blocking collectives  19.7 us (30%)
  starting transfers between devices  8.59 us (13%)
  Pallas kernels  7.71 us (12%)
  local copies, waits for them, and re-layouts  5.32 us (8%)
    all_to_all x1, waiting for transfers between devices, local(): lax.all_to_all(packed.reshape(dests, -1, feats), near, split_axis=0, conc...  20.8 us
    all_gather x1, blocking collectives, local(): held = lax.all_gather(own, 'zh', tiled=True)  19.7 us
    all_to_all x1, starting transfers between devices, local(): lax.all_to_all(packed.reshape(dests, -1, feats), near, split_axis=0, conc...  7.15 us
    unnamed x15, local copies, waits for them, and re-layouts  5.32 us
    ppermute x1, waiting for transfers between devices, shift(): return lax.ppermute(x, axis, [(i, (i + step) % n) for i in range(n)])  2.32 us
    pallas_call x3, Pallas kernels, call(): pl.pallas_call(body, out_shape=out_shape, in_specs=[pl.BlockSpec(memory_s...  1.97 us
    pallas_call x1, Pallas kernels, local(): pl.pallas_call(functools.partial(pack_body, tok_rows, top), out_shape=plt...  1.78 us
    pallas_call x1, Pallas kernels, local(): pl.pallas_call(update_body, out_shape=shape(slab, feats), in_specs=[vmem]...  1.52 us
  transfers between devices with their start and end apart: 2, of which 2 were waited for; matrix products, arithmetic and copies ran while one was open for 1% of the time, Pallas kernels for 4%

profile of v9, /device:TPU:8, one launch (start us, length us, event | category | flops | bytes accessed | tf_op | source)
XLA Modules:
  0.0 64.5 jit_solution(2601899987539964822)
XLA Ops:
  0.0 0.9 %tag.1 = bf16[16,3712]{1,0:T(8,128)(2,1)S(1)} custom-call(bf16[16,3584]{1,0:T(8,128)(2,1)} %tokens_hbm.1, s32[8,16]{1,0:T(8,128)} %bitcast.12), custom_call_target="tpu_custom_call" | custom-call | tf_op jit(solution)/shard_map/tag/pallas_call | solution.py:186
  0.9 19.7 %all_gather.3.held = bf16[64,3712]{1,0:T(8,128)(2,1)S(1)} all-gather(bf16[16,3712]{1,0:T(8,128)(2,1)S(1)} %tag.1), channel_id=1, replica_groups=mesh['zh'=4,'zl'=2,'yh'=2,'x'=4,'core'=2,'yl'=2] {'zh'}, dimensions={0}, use_global_device_ids=true | all-gather | bytes 593920 | tf_op jit(solution)/shard_map/gather/all_gather | solution.py:198
  20.6 1.8 %pack.1 = bf16[256,3584]{1,0:T(8,128)(2,1)} custom-call(s32[1]{0:T(128)} %bitcast.first_ref, bf16[64,3712]{1,0:T(8,128)(2,1)S(1)} %all_gather.3.held), custom_call_target="tpu_custom_call" | custom-call | tf_op jit(solution)/shard_map/pack/pallas_call | solution.py:200
  22.4 0.0 copy-start.6
  22.4 7.2 %all-to-all-start = ((bf16[32,8,3584]{2,1,0:T(8,128)(2,1)}), bf16[32,8,3584]{2,1,0:T(8,128)(2,1)S(1)}, u32[]{:S(2)}, u32[]{:S(2)}) async-start(bf16[32,8,3584]{2,1,0:T(8,128)(2,1)} %bitcast.11), calls=%async_computation | async-start | bytes 3670016 | tf_op jit(solution)/shard_map/route/all_to_all | solution.py:212
  29.6 0.0 copy-done.6
  29.6 0.8 %copy.6.bits_ref = s32[256,112]{1,0:T(8,128)} copy(s32[256,112]{0,1:T(8,128)S(1)} %copy-done.6) | data formatting | bytes 229376 | tf_op args[3]
  30.3 0.0 copy-start
  30.3 1.5 %copy-done = bf16[1,256,3584]{2,1,0:T(8,128)(2,1)S(1)} copy-done((bf16[1,256,3584]{2,1,0:T(8,128)(2,1)S(1)}, bf16[1,256,3584]{2,1,0:T(8,128)(2,1)}, u32[]{:S(2)}) %copy-start) | copy-done | bytes 1835032
  31.8 0.9 %copy-done.2 = s32[256,112]{1,0:T(8,128)S(1)} copy-done((s32[256,112]{1,0:T(8,128)S(1)}, s32[256,112]{1,0:T(8,128)}, u32[]{:S(2)}) %copy-start.2) | copy-done | bytes 114712
  32.7 1.1 %prune.1 = (bf16[256,3328]{1,0:T(8,128)(2,1)S(1)}, bf16[256,256]{1,0:T(8,128)(2,1)S(1)}, bf16[256,3584]{1,0:T(8,128)(2,1)S(1)}) custom-call(bf16[256,3584]{1,0:T(8,128)(2,1)S(1)} %bitcast.10, s32[256,112]{1,0:T(8,128)S(1)} %copy-done.2), custom_call_target="tpu_custom_call" | custom-call | flops 4194304 | bytes 5619712 | tf_op jit(solution)/shard_map/prune/pallas_call | solution.py:25
  33.8 0.0 copy-start.1
  33.9 1.2 %copy-done.1 = bf16[256,3584]{1,0:T(8,128)(2,1)} copy-done((bf16[256,3584]{1,0:T(8,128)(2,1)}, bf16[256,3584]{1,0:T(8,128)(2,1)S(1)}, u32[]{:S(2)}) %copy-start.1) | copy-done | bytes 1835032
  35.1 0.7 %copy-done.3 = bf16[256,256]{1,0:T(8,128)(2,1)} copy-done((bf16[256,256]{1,0:T(8,128)(2,1)}, bf16[256,256]{1,0:T(8,128)(2,1)S(1)}, u32[]{:S(2)}) %copy-start.3) | copy-done | bytes 131096
  35.8 20.8 %all-to-all-done = bf16[32,8,3584]{2,1,0:T(8,128)(2,1)S(1)} async-done(((bf16[32,8,3584]{2,1,0:T(8,128)(2,1)}), bf16[32,8,3584]{2,1,0:T(8,128)(2,1)S(1)}, u32[]{:S(2)}, u32[]{:S(2)}) %all-to-all-start) | async-done | bytes 1835040 | tf_op jit(solution)/shard_map/route/all_to_all | solution.py:212
  56.5 0.6 project.2.first_ref
  57.2 0.0 copy-start.5
  57.2 0.2 copy-done.4
  57.4 0.2 project.3
  57.7 1.4 %collective-permute-start = (bf16[256,256]{1,0:T(8,128)(2,1)S(1)}, bf16[256,256]{1,0:T(8,128)(2,1)S(1)}, u32[]{:S(2)}, u32[]{:S(2)}) collective-permute-start(bf16[256,256]{1,0:T(8,128)(2,1)S(1)} %get-tuple-element.15), channel_id=1, source_target_pairs={{0,1},{1,0},{2,3},{3,2},{4,5},{5,4},{6,7},{7,6},{8,9},{9,8},{10,11... | collective-permute-start | bytes 393224 | tf_op jit(solution)/shard_map/swap_features/ppermute | solution.py:169
  59.1 0.0 copy-done.5
  59.1 1.5 %scale.1 = (f32[1,3584]{1,0:T(1,128)S(1)}, bf16[256,3584]{1,0:T(8,128)(2,1)S(1)}) custom-call(bf16[256,3584]{1,0:T(8,128)(2,1)S(1)} %bitcast.8, f32[1,3584]{1,0:T(1,128)S(1)} %copy-done.5, bf16[256,3584]{1,0:T(8,128)(2,1)} %copy-done.1), custom_call_target="tpu_custom_call" | custom-call | tf_op jit(solution)/shard_map/scale/pallas_call | solution.py:239
  60.6 2.3 %collective-permute-done.other_ref = bf16[256,256]{1,0:T(8,128)(2,1)S(1)} collective-permute-done((bf16[256,256]{1,0:T(8,128)(2,1)S(1)}, bf16[256,256]{1,0:T(8,128)(2,1)S(1)}, u32[]{:S(2)}, u32[]{:S(2)}) %collective-permute-start) | collective-permute-done | bytes 131104 | tf_op jit(solution)/shard_map/swap_features/ppermute | solution.py:169
  62.9 1.5 %update.1 = bf16[256,3584]{1,0:T(8,128)(2,1)} custom-call(f32[256,256]{1,0:T(8,128)S(1)} %get-tuple-element.14.part_ref, bf16[256,256]{1,0:T(8,128)(2,1)S(1)} %collective-permute-done.other_ref, bf16[256,3584]{1,0:T(8,128)(2,1)S(1)} %bitcast.9, f32[1,3584]{1,0:T(1,128)S(1)} %get-tuple-element.17.scale_ref, bf16[256,3584]{1,0:T(8,128)(2,1)S(1)} %get-tuple-element.18.kept_ref), custom_call_target="tpu_custom_call" | custom-call | tf_op jit(solution)/shard_map/update/pallas_call | solution.py:249
  (3 shorter events, 0.0 us)
Async XLA Ops:
  22.4 7.2 %copy-start.6 = (s32[256,112]{0,1:T(8,128)S(1)}, s32[256,112]{0,1:T(8,128)}, u32[]{:S(2)}) copy-start(s32[256,112]{0,1:T(8,128)} %param.8) | copy-start | bytes 344068
  22.4 34.1 %all-to-all-start = ((bf16[32,8,3584]{2,1,0:T(8,128)(2,1)}), bf16[32,8,3584]{2,1,0:T(8,128)(2,1)S(1)}, u32[]{:S(2)}, u32[]{:S(2)}) async-start(bf16[32,8,3584]{2,1,0:T(8,128)(2,1)} %bitcast.11), calls=%async_computation | async-start | bytes 3670016 | tf_op jit(solution)/shard_map/route/all_to_all | solution.py:212
  30.3 1.5 %copy-start = (bf16[1,256,3584]{2,1,0:T(8,128)(2,1)S(1)}, bf16[1,256,3584]{2,1,0:T(8,128)(2,1)}, u32[]{:S(2)}) copy-start(bf16[1,256,3584]{2,1,0:T(8,128)(2,1)} %param.7) | copy-start | bytes 5505028
  31.8 0.9 %copy-start.2 = (s32[256,112]{1,0:T(8,128)S(1)}, s32[256,112]{1,0:T(8,128)}, u32[]{:S(2)}) copy-start(s32[256,112]{1,0:T(8,128)} %copy.6.bits_ref) | copy-start | bytes 344068
  33.8 1.3 %copy-start.1 = (bf16[256,3584]{1,0:T(8,128)(2,1)}, bf16[256,3584]{1,0:T(8,128)(2,1)S(1)}, u32[]{:S(2)}) copy-start(bf16[256,3584]{1,0:T(8,128)(2,1)S(1)} %get-tuple-element.16.kept_hbm) | copy-start | bytes 5505028
  35.1 0.7 %copy-start.3 = (bf16[256,256]{1,0:T(8,128)(2,1)}, bf16[256,256]{1,0:T(8,128)(2,1)S(1)}, u32[]{:S(2)}) copy-start(bf16[256,256]{1,0:T(8,128)(2,1)S(1)} %get-tuple-element.12.rest_ref) | copy-start | bytes 393220
  56.5 0.9 %copy-start.4 = (bf16[256,256]{1,0:T(8,128)(2,1)S(1)}, bf16[256,256]{1,0:T(8,128)(2,1)}, u32[]{:S(2)}) copy-start(bf16[256,256]{1,0:T(8,128)(2,1)} %copy-done.3) | copy-start | bytes 393220
  57.2 1.9 %copy-start.5 = (f32[1,3584]{1,0:T(1,128)S(1)}, f32[1,3584]{1,0:T(1,128)}, u32[]{:S(2)}) copy-start(f32[1,3584]{1,0:T(1,128)} %damping_ref.1) | copy-start | bytes 43012
  57.7 5.3 %collective-permute-start = (bf16[256,256]{1,0:T(8,128)(2,1)S(1)}, bf16[256,256]{1,0:T(8,128)(2,1)S(1)}, u32[]{:S(2)}, u32[]{:S(2)}) collective-permute-start(bf16[256,256]{1,0:T(8,128)(2,1)S(1)} %get-tuple-element.15), channel_id=1, source_target_pairs={{0,1},{1,0},{2,3},{3,2},{4,5},{5,4},{6,7},{7,6},{8,9},{9,8},{10,11... | collective-permute-start | bytes 393224 | tf_op jit(solution)/shard_map/swap_features/ppermute | solution.py:169

commit v10 on v9

--- a/solution.py
+++ b/solution.py
@@ -45,41 +45,43 @@
         lax.broadcasted_iota(jnp.int32, (top, LANES), 0)
         == lax.broadcasted_iota(jnp.int32, (top, LANES), 1)
     ).astype(BF16)
+    rows = out_ref.shape[0]
+    earlier = (
+        lax.broadcasted_iota(jnp.int32, (rows, rows), 1)
+        < lax.broadcasted_iota(jnp.int32, (rows, rows), 0)
+    ).astype(BF16)
+    expert = lax.broadcasted_iota(jnp.int32, (rows, LANES), 1).astype(F32)
     get_ids.wait()
-    ids = ids_ref[...].astype(F32).astype(BF16)
-    out_ref[:, feats:] = lax.dot_general(
-        ids, spread, (((0,), (0,)), ((), ())), preferred_element_type=F32
-    ).astype(BF16)
+    ids = lax.dot_general(
+        ids_ref[...].astype(F32).astype(BF16),
+        spread,
+        (((0,), (0,)), ((), ())),
+        preferred_element_type=F32,
+    )
+    named = ids[:, 0:1] == expert
+    for k in range(1, top):
+        named = named | (ids[:, k : k + 1] == expert)
+    member = jnp.where(named, 1.0, 0.0)
+    rank = jnp.dot(earlier, member.astype(BF16), preferred_element_type=F32)
+    out_ref[:, feats:] = (member * (1.0 + rank)).astype(BF16)
     get_tokens.wait()
 
 
-def pack_body(tok_rows, top, first_ref, held, out_hbm, out_ref, sems):
+def pack_body(tok_rows, first_ref, held, out_hbm, out_ref, sems):
     rows, feats = out_ref.shape
     tokens = held.shape[0]
     per_dest = tokens // tok_rows * CAP
-    pick = (
-        lax.broadcasted_iota(jnp.int32, (top, LANES), 0)
-        == lax.broadcasted_iota(jnp.int32, (top, LANES), 1)
-    ).astype(BF16)
-    ids = lax.dot_general(
+    row = lax.broadcasted_iota(jnp.int32, (rows, 1), 0)
+    expert = first_ref[0] + row // per_dest
+    pick = (lax.broadcasted_iota(jnp.int32, (rows, LANES), 1) == expert).astype(BF16)
+    taken = lax.dot_general(
         pick, held[:, feats:], (((1,), (1,)), ((), ())), preferred_element_type=F32
     )
-    row = lax.broadcasted_iota(jnp.int32, (rows, 1), 0)
-    expert = (first_ref[0] + row // per_dest).astype(F32)
     block = (row % per_dest) // CAP
     slot = (row % CAP).astype(F32)
     tok = lax.broadcasted_iota(jnp.int32, (1, tokens), 1)
-    named = ids[0:1, :] == expert
-    for k in range(1, top):
-        named = named | (ids[k : k + 1, :] == expert)
-    named = named & (tok // tok_rows == block)
-    member = jnp.where(named, 1.0, 0.0)
-    before = (
-        lax.broadcasted_iota(jnp.int32, (tokens, tokens), 0)
-        < lax.broadcasted_iota(jnp.int32, (tokens, tokens), 1)
-    ).astype(BF16)
-    rank = jnp.dot(member.astype(BF16), before, preferred_element_type=F32)
-    select = jnp.where(rank == slot, member, 0.0).astype(BF16)
+    mine = (tok // tok_rows == block) & (taken == slot + 1.0)
+    select = jnp.where(mine, 1.0, 0.0).astype(BF16)
     copies = []
     for i, lo in enumerate(range(0, feats, STEP)):
         cols = (slice(None), pl.ds(lo, STEP))
@@ -198,7 +200,7 @@
         held = lax.all_gather(own, "zh", tiled=True)
     with jax.named_scope("pack"):
         packed = pl.pallas_call(
-            functools.partial(pack_body, tok_rows, top),
+            functools.partial(pack_body, tok_rows),
             out_shape=pltpu.HBM((rows, feats), BF16),
             in_specs=[pl.BlockSpec(memory_space=pltpu.SMEM), vmem],
             out_specs=hbm,

time: 65.6 us -> 65.6 us (level)
  no operation moved by 1% of the time
where the time goes in v10:
time: 65.6 us; the launch traced here: 64.5 us
  waiting for transfers between devices  23.1 us (35%)
  blocking collectives  19.7 us (30%)
  starting transfers between devices  8.59 us (13%)
  Pallas kernels  7.73 us (12%)
  local copies, waits for them, and re-layouts  5.32 us (8%)
    all_to_all x1, waiting for transfers between devices, local(): lax.all_to_all(packed.reshape(dests, -1, feats), near, split_axis=0, conc...  20.8 us
    all_gather x1, blocking collectives, local(): held = lax.all_gather(own, 'zh', tiled=True)  19.7 us
    all_to_all x1, starting transfers between devices, local(): lax.all_to_all(packed.reshape(dests, -1, feats), near, split_axis=0, conc...  7.16 us
    unnamed x15, local copies, waits for them, and re-layouts  5.32 us
    ppermute x1, waiting for transfers between devices, shift(): return lax.ppermute(x, axis, [(i, (i + step) % n) for i in range(n)])  2.32 us
    pallas_call x3, Pallas kernels, call(): pl.pallas_call(body, out_shape=out_shape, in_specs=[pl.BlockSpec(memory_s...  1.97 us
    pallas_call x1, Pallas kernels, local(): pl.pallas_call(functools.partial(pack_body, tok_rows), out_shape=pltpu.HB...  1.64 us
    pallas_call x1, Pallas kernels, local(): pl.pallas_call(update_body, out_shape=shape(slab, feats), in_specs=[vmem]...  1.52 us
  transfers between devices with their start and end apart: 2, of which 2 were waited for; matrix products, arithmetic and copies ran while one was open for 1% of the time, Pallas kernels for 4%

profile of v10, /device:TPU:8, one launch (start us, length us, event | category | flops | bytes accessed | tf_op | source)
XLA Modules:
  0.0 64.5 jit_solution(5656246073336514302)
XLA Ops:
  0.0 1.1 %tag.1 = bf16[16,3712]{1,0:T(8,128)(2,1)S(1)} custom-call(bf16[16,3584]{1,0:T(8,128)(2,1)} %tokens_hbm.1, s32[8,16]{1,0:T(8,128)} %bitcast.12), custom_call_target="tpu_custom_call" | custom-call | tf_op jit(solution)/shard_map/tag/pallas_call | solution.py:188
  1.1 19.7 %all_gather.3.held = bf16[64,3712]{1,0:T(8,128)(2,1)S(1)} all-gather(bf16[16,3712]{1,0:T(8,128)(2,1)S(1)} %tag.1), channel_id=1, replica_groups=mesh['zh'=4,'zl'=2,'yh'=2,'x'=4,'core'=2,'yl'=2] {'zh'}, dimensions={0}, use_global_device_ids=true | all-gather | bytes 593920 | tf_op jit(solution)/shard_map/gather/all_gather | solution.py:200
  20.8 1.6 %pack.1 = bf16[256,3584]{1,0:T(8,128)(2,1)} custom-call(s32[1]{0:T(128)} %bitcast.first_ref, bf16[64,3712]{1,0:T(8,128)(2,1)S(1)} %all_gather.3.held), custom_call_target="tpu_custom_call" | custom-call | tf_op jit(solution)/shard_map/pack/pallas_call | solution.py:202
  22.4 0.0 copy-start.6
  22.4 7.2 %all-to-all-start = ((bf16[32,8,3584]{2,1,0:T(8,128)(2,1)}), bf16[32,8,3584]{2,1,0:T(8,128)(2,1)S(1)}, u32[]{:S(2)}, u32[]{:S(2)}) async-start(bf16[32,8,3584]{2,1,0:T(8,128)(2,1)} %bitcast.11), calls=%async_computation | async-start | bytes 3670016 | tf_op jit(solution)/shard_map/route/all_to_all | solution.py:214
  29.6 0.0 copy-done.6
  29.6 0.8 %copy.6.bits_ref = s32[256,112]{1,0:T(8,128)} copy(s32[256,112]{0,1:T(8,128)S(1)} %copy-done.6) | data formatting | bytes 229376 | tf_op args[3]
  30.3 0.0 copy-start
  30.3 1.5 %copy-done = bf16[1,256,3584]{2,1,0:T(8,128)(2,1)S(1)} copy-done((bf16[1,256,3584]{2,1,0:T(8,128)(2,1)S(1)}, bf16[1,256,3584]{2,1,0:T(8,128)(2,1)}, u32[]{:S(2)}) %copy-start) | copy-done | bytes 1835032
  31.8 0.9 %copy-done.2 = s32[256,112]{1,0:T(8,128)S(1)} copy-done((s32[256,112]{1,0:T(8,128)S(1)}, s32[256,112]{1,0:T(8,128)}, u32[]{:S(2)}) %copy-start.2) | copy-done | bytes 114712
  32.8 1.1 %prune.1 = (bf16[256,3328]{1,0:T(8,128)(2,1)S(1)}, bf16[256,256]{1,0:T(8,128)(2,1)S(1)}, bf16[256,3584]{1,0:T(8,128)(2,1)S(1)}) custom-call(bf16[256,3584]{1,0:T(8,128)(2,1)S(1)} %bitcast.10, s32[256,112]{1,0:T(8,128)S(1)} %copy-done.2), custom_call_target="tpu_custom_call" | custom-call | flops 4194304 | bytes 5619712 | tf_op jit(solution)/shard_map/prune/pallas_call | solution.py:25
  33.9 0.0 copy-start.1
  33.9 1.2 %copy-done.1 = bf16[256,3584]{1,0:T(8,128)(2,1)} copy-done((bf16[256,3584]{1,0:T(8,128)(2,1)}, bf16[256,3584]{1,0:T(8,128)(2,1)S(1)}, u32[]{:S(2)}) %copy-start.1) | copy-done | bytes 1835032
  35.1 0.7 %copy-done.3 = bf16[256,256]{1,0:T(8,128)(2,1)} copy-done((bf16[256,256]{1,0:T(8,128)(2,1)}, bf16[256,256]{1,0:T(8,128)(2,1)S(1)}, u32[]{:S(2)}) %copy-start.3) | copy-done | bytes 131096
  35.8 20.8 %all-to-all-done = bf16[32,8,3584]{2,1,0:T(8,128)(2,1)S(1)} async-done(((bf16[32,8,3584]{2,1,0:T(8,128)(2,1)}), bf16[32,8,3584]{2,1,0:T(8,128)(2,1)S(1)}, u32[]{:S(2)}, u32[]{:S(2)}) %all-to-all-start) | async-done | bytes 1835040 | tf_op jit(solution)/shard_map/route/all_to_all | solution.py:214
  56.6 0.6 project.2.first_ref
  57.2 0.0 copy-start.5
  57.2 0.2 copy-done.4
  57.5 0.2 project.3
  57.7 1.4 %collective-permute-start = (bf16[256,256]{1,0:T(8,128)(2,1)S(1)}, bf16[256,256]{1,0:T(8,128)(2,1)S(1)}, u32[]{:S(2)}, u32[]{:S(2)}) collective-permute-start(bf16[256,256]{1,0:T(8,128)(2,1)S(1)} %get-tuple-element.15), channel_id=1, source_target_pairs={{0,1},{1,0},{2,3},{3,2},{4,5},{5,4},{6,7},{7,6},{8,9},{9,8},{10,11... | collective-permute-start | bytes 393224 | tf_op jit(solution)/shard_map/swap_features/ppermute | solution.py:171
  59.1 0.0 copy-done.5
  59.1 1.5 %scale.1 = (f32[1,3584]{1,0:T(1,128)S(1)}, bf16[256,3584]{1,0:T(8,128)(2,1)S(1)}) custom-call(bf16[256,3584]{1,0:T(8,128)(2,1)S(1)} %bitcast.8, f32[1,3584]{1,0:T(1,128)S(1)} %copy-done.5, bf16[256,3584]{1,0:T(8,128)(2,1)} %copy-done.1), custom_call_target="tpu_custom_call" | custom-call | tf_op jit(solution)/shard_map/scale/pallas_call | solution.py:241
  60.6 2.3 %collective-permute-done.other_ref = bf16[256,256]{1,0:T(8,128)(2,1)S(1)} collective-permute-done((bf16[256,256]{1,0:T(8,128)(2,1)S(1)}, bf16[256,256]{1,0:T(8,128)(2,1)S(1)}, u32[]{:S(2)}, u32[]{:S(2)}) %collective-permute-start) | collective-permute-done | bytes 131104 | tf_op jit(solution)/shard_map/swap_features/ppermute | solution.py:171
  63.0 1.5 %update.1 = bf16[256,3584]{1,0:T(8,128)(2,1)} custom-call(f32[256,256]{1,0:T(8,128)S(1)} %get-tuple-element.14.part_ref, bf16[256,256]{1,0:T(8,128)(2,1)S(1)} %collective-permute-done.other_ref, bf16[256,3584]{1,0:T(8,128)(2,1)S(1)} %bitcast.9, f32[1,3584]{1,0:T(1,128)S(1)} %get-tuple-element.17.scale_ref, bf16[256,3584]{1,0:T(8,128)(2,1)S(1)} %get-tuple-element.18.kept_ref), custom_call_target="tpu_custom_call" | custom-call | tf_op jit(solution)/shard_map/update/pallas_call | solution.py:251
  (3 shorter events, 0.0 us)
Async XLA Ops:
  22.4 7.2 %copy-start.6 = (s32[256,112]{0,1:T(8,128)S(1)}, s32[256,112]{0,1:T(8,128)}, u32[]{:S(2)}) copy-start(s32[256,112]{0,1:T(8,128)} %param.8) | copy-start | bytes 344068
  22.4 34.1 %all-to-all-start = ((bf16[32,8,3584]{2,1,0:T(8,128)(2,1)}), bf16[32,8,3584]{2,1,0:T(8,128)(2,1)S(1)}, u32[]{:S(2)}, u32[]{:S(2)}) async-start(bf16[32,8,3584]{2,1,0:T(8,128)(2,1)} %bitcast.11), calls=%async_computation | async-start | bytes 3670016 | tf_op jit(solution)/shard_map/route/all_to_all | solution.py:214
  30.3 1.5 %copy-start = (bf16[1,256,3584]{2,1,0:T(8,128)(2,1)S(1)}, bf16[1,256,3584]{2,1,0:T(8,128)(2,1)}, u32[]{:S(2)}) copy-start(bf16[1,256,3584]{2,1,0:T(8,128)(2,1)} %param.7) | copy-start | bytes 5505028
  31.8 0.9 %copy-start.2 = (s32[256,112]{1,0:T(8,128)S(1)}, s32[256,112]{1,0:T(8,128)}, u32[]{:S(2)}) copy-start(s32[256,112]{1,0:T(8,128)} %copy.6.bits_ref) | copy-start | bytes 344068
  33.9 1.3 %copy-start.1 = (bf16[256,3584]{1,0:T(8,128)(2,1)}, bf16[256,3584]{1,0:T(8,128)(2,1)S(1)}, u32[]{:S(2)}) copy-start(bf16[256,3584]{1,0:T(8,128)(2,1)S(1)} %get-tuple-element.16.kept_hbm) | copy-start | bytes 5505028
  35.1 0.7 %copy-start.3 = (bf16[256,256]{1,0:T(8,128)(2,1)}, bf16[256,256]{1,0:T(8,128)(2,1)S(1)}, u32[]{:S(2)}) copy-start(bf16[256,256]{1,0:T(8,128)(2,1)S(1)} %get-tuple-element.12.rest_ref) | copy-start | bytes 393220
  56.6 0.9 %copy-start.4 = (bf16[256,256]{1,0:T(8,128)(2,1)S(1)}, bf16[256,256]{1,0:T(8,128)(2,1)}, u32[]{:S(2)}) copy-start(bf16[256,256]{1,0:T(8,128)(2,1)} %copy-done.3) | copy-start | bytes 393220
  57.2 1.9 %copy-start.5 = (f32[1,3584]{1,0:T(1,128)S(1)}, f32[1,3584]{1,0:T(1,128)}, u32[]{:S(2)}) copy-start(f32[1,3584]{1,0:T(1,128)} %damping_ref.1) | copy-start | bytes 43012
  57.7 5.3 %collective-permute-start = (bf16[256,256]{1,0:T(8,128)(2,1)S(1)}, bf16[256,256]{1,0:T(8,128)(2,1)S(1)}, u32[]{:S(2)}, u32[]{:S(2)}) collective-permute-start(bf16[256,256]{1,0:T(8,128)(2,1)S(1)} %get-tuple-element.15), channel_id=1, source_target_pairs={{0,1},{1,0},{2,3},{3,2},{4,5},{5,4},{6,7},{7,6},{8,9},{9,8},{10,11... | collective-permute-start | bytes 393224 | tf_op jit(solution)/shard_map/swap_features/ppermute | solution.py:171

commit v11 on v10

--- a/solution.py
+++ b/solution.py
@@ -12,6 +12,7 @@
 CAP = 2
 LANES = 128
 STEP = 512
+FINE = 256
 REST = 256
 VMEM = 16 * 2**20
 F32 = jnp.float32
@@ -145,13 +146,13 @@
 def update_body(part_ref, other_ref, routed_ref, scale_ref, kept_ref, out_hbm, out_ref, sems):
     projected = (part_ref[...] + other_ref[...].astype(F32)).astype(BF16)
     copies = []
-    for i, lo in enumerate(range(0, out_ref.shape[1], STEP)):
-        cols = slice(lo, lo + STEP)
+    for i, lo in enumerate(range(0, out_ref.shape[1], FINE)):
+        cols = slice(lo, lo + FINE)
         comp = jnp.dot(projected, routed_ref[:, cols], preferred_element_type=F32)
         kept = kept_ref[:, cols]
         updated = (kept.astype(F32) + comp * scale_ref[:, cols]).astype(BF16)
         out_ref[:, cols] = jnp.where(kept < jnp.inf, updated, jnp.zeros_like(updated))
-        block = (slice(None), pl.ds(lo, STEP))
+        block = (slice(None), pl.ds(lo, FINE))
         copies.append(pltpu.make_async_copy(out_ref.at[block], out_hbm.at[block], sems.at[i]))
         copies[-1].start()
     for copy in copies:
@@ -255,7 +256,7 @@
             out_specs=hbm,
             scratch_shapes=[
                 pltpu.VMEM((slab, feats), BF16),
-                pltpu.SemaphoreType.DMA((feats // STEP,)),
+                pltpu.SemaphoreType.DMA((feats // FINE,)),
             ],
             compiler_params=params,
         )(*operands)

time: 65.6 us -> 65.7 us (level)
  no operation moved by 1% of the time
where the time goes in v11:
time: 65.7 us; the launch traced here: 64.6 us
  waiting for transfers between devices  23.1 us (35%)
  blocking collectives  19.7 us (30%)
  starting transfers between devices  8.59 us (13%)
  Pallas kernels  7.82 us (12%)
  local copies, waits for them, and re-layouts  5.32 us (8%)
    all_to_all x1, waiting for transfers between devices, local(): lax.all_to_all(packed.reshape(dests, -1, feats), near, split_axis=0, conc...  20.8 us
    all_gather x1, blocking collectives, local(): held = lax.all_gather(own, 'zh', tiled=True)  19.7 us
    all_to_all x1, starting transfers between devices, local(): lax.all_to_all(packed.reshape(dests, -1, feats), near, split_axis=0, conc...  7.16 us
    unnamed x15, local copies, waits for them, and re-layouts  5.32 us
    ppermute x1, waiting for transfers between devices, shift(): return lax.ppermute(x, axis, [(i, (i + step) % n) for i in range(n)])  2.32 us
    pallas_call x3, Pallas kernels, call(): pl.pallas_call(body, out_shape=out_shape, in_specs=[pl.BlockSpec(memory_s...  1.97 us
    pallas_call x1, Pallas kernels, local(): pl.pallas_call(functools.partial(pack_body, tok_rows), out_shape=pltpu.HB...  1.64 us
    pallas_call x1, Pallas kernels, local(): pl.pallas_call(update_body, out_shape=shape(slab, feats), in_specs=[vmem]...  1.61 us
  transfers between devices with their start and end apart: 2, of which 2 were waited for; matrix products, arithmetic and copies ran while one was open for 1% of the time, Pallas kernels for 4%

profile of v11, /device:TPU:8, one launch (start us, length us, event | category | flops | bytes accessed | tf_op | source)
XLA Modules:
  0.0 64.6 jit_solution(5512874197628355666)
XLA Ops:
  0.0 1.1 %tag.1 = bf16[16,3712]{1,0:T(8,128)(2,1)S(1)} custom-call(bf16[16,3584]{1,0:T(8,128)(2,1)} %tokens_hbm.1, s32[8,16]{1,0:T(8,128)} %bitcast.12), custom_call_target="tpu_custom_call" | custom-call | tf_op jit(solution)/shard_map/tag/pallas_call | solution.py:189
  1.1 19.7 %all_gather.3.held = bf16[64,3712]{1,0:T(8,128)(2,1)S(1)} all-gather(bf16[16,3712]{1,0:T(8,128)(2,1)S(1)} %tag.1), channel_id=1, replica_groups=mesh['zh'=4,'zl'=2,'yh'=2,'x'=4,'core'=2,'yl'=2] {'zh'}, dimensions={0}, use_global_device_ids=true | all-gather | bytes 593920 | tf_op jit(solution)/shard_map/gather/all_gather | solution.py:201
  20.8 1.6 %pack.1 = bf16[256,3584]{1,0:T(8,128)(2,1)} custom-call(s32[1]{0:T(128)} %bitcast.first_ref, bf16[64,3712]{1,0:T(8,128)(2,1)S(1)} %all_gather.3.held), custom_call_target="tpu_custom_call" | custom-call | tf_op jit(solution)/shard_map/pack/pallas_call | solution.py:203
  22.4 0.0 copy-start.6
  22.4 7.2 %all-to-all-start = ((bf16[32,8,3584]{2,1,0:T(8,128)(2,1)}), bf16[32,8,3584]{2,1,0:T(8,128)(2,1)S(1)}, u32[]{:S(2)}, u32[]{:S(2)}) async-start(bf16[32,8,3584]{2,1,0:T(8,128)(2,1)} %bitcast.11), calls=%async_computation | async-start | bytes 3670016 | tf_op jit(solution)/shard_map/route/all_to_all | solution.py:215
  29.6 0.0 copy-done.6
  29.6 0.8 %copy.6.bits_ref = s32[256,112]{1,0:T(8,128)} copy(s32[256,112]{0,1:T(8,128)S(1)} %copy-done.6) | data formatting | bytes 229376 | tf_op args[3]
  30.3 0.0 copy-start
  30.3 1.5 %copy-done = bf16[1,256,3584]{2,1,0:T(8,128)(2,1)S(1)} copy-done((bf16[1,256,3584]{2,1,0:T(8,128)(2,1)S(1)}, bf16[1,256,3584]{2,1,0:T(8,128)(2,1)}, u32[]{:S(2)}) %copy-start) | copy-done | bytes 1835032
  31.8 0.9 %copy-done.2 = s32[256,112]{1,0:T(8,128)S(1)} copy-done((s32[256,112]{1,0:T(8,128)S(1)}, s32[256,112]{1,0:T(8,128)}, u32[]{:S(2)}) %copy-start.2) | copy-done | bytes 114712
  32.8 1.1 %prune.1 = (bf16[256,3328]{1,0:T(8,128)(2,1)S(1)}, bf16[256,256]{1,0:T(8,128)(2,1)S(1)}, bf16[256,3584]{1,0:T(8,128)(2,1)S(1)}) custom-call(bf16[256,3584]{1,0:T(8,128)(2,1)S(1)} %bitcast.10, s32[256,112]{1,0:T(8,128)S(1)} %copy-done.2), custom_call_target="tpu_custom_call" | custom-call | flops 4194304 | bytes 5619712 | tf_op jit(solution)/shard_map/prune/pallas_call | solution.py:26
  33.9 0.0 copy-start.1
  33.9 1.2 %copy-done.1 = bf16[256,3584]{1,0:T(8,128)(2,1)} copy-done((bf16[256,3584]{1,0:T(8,128)(2,1)}, bf16[256,3584]{1,0:T(8,128)(2,1)S(1)}, u32[]{:S(2)}) %copy-start.1) | copy-done | bytes 1835032
  35.1 0.7 %copy-done.3 = bf16[256,256]{1,0:T(8,128)(2,1)} copy-done((bf16[256,256]{1,0:T(8,128)(2,1)}, bf16[256,256]{1,0:T(8,128)(2,1)S(1)}, u32[]{:S(2)}) %copy-start.3) | copy-done | bytes 131096
  35.8 20.8 %all-to-all-done = bf16[32,8,3584]{2,1,0:T(8,128)(2,1)S(1)} async-done(((bf16[32,8,3584]{2,1,0:T(8,128)(2,1)}), bf16[32,8,3584]{2,1,0:T(8,128)(2,1)S(1)}, u32[]{:S(2)}, u32[]{:S(2)}) %all-to-all-start) | async-done | bytes 1835040 | tf_op jit(solution)/shard_map/route/all_to_all | solution.py:215
  56.6 0.6 project.2.first_ref
  57.2 0.0 copy-start.5
  57.2 0.2 copy-done.4
  57.5 0.2 project.3
  57.7 1.4 %collective-permute-start = (bf16[256,256]{1,0:T(8,128)(2,1)S(1)}, bf16[256,256]{1,0:T(8,128)(2,1)S(1)}, u32[]{:S(2)}, u32[]{:S(2)}) collective-permute-start(bf16[256,256]{1,0:T(8,128)(2,1)S(1)} %get-tuple-element.15), channel_id=1, source_target_pairs={{0,1},{1,0},{2,3},{3,2},{4,5},{5,4},{6,7},{7,6},{8,9},{9,8},{10,11... | collective-permute-start | bytes 393224 | tf_op jit(solution)/shard_map/swap_features/ppermute | solution.py:172
  59.1 0.0 copy-done.5
  59.1 1.5 %scale.1 = (f32[1,3584]{1,0:T(1,128)S(1)}, bf16[256,3584]{1,0:T(8,128)(2,1)S(1)}) custom-call(bf16[256,3584]{1,0:T(8,128)(2,1)S(1)} %bitcast.8, f32[1,3584]{1,0:T(1,128)S(1)} %copy-done.5, bf16[256,3584]{1,0:T(8,128)(2,1)} %copy-done.1), custom_call_target="tpu_custom_call" | custom-call | tf_op jit(solution)/shard_map/scale/pallas_call | solution.py:242
  60.6 2.3 %collective-permute-done.other_ref = bf16[256,256]{1,0:T(8,128)(2,1)S(1)} collective-permute-done((bf16[256,256]{1,0:T(8,128)(2,1)S(1)}, bf16[256,256]{1,0:T(8,128)(2,1)S(1)}, u32[]{:S(2)}, u32[]{:S(2)}) %collective-permute-start) | collective-permute-done | bytes 131104 | tf_op jit(solution)/shard_map/swap_features/ppermute | solution.py:172
  63.0 1.6 %update.1 = bf16[256,3584]{1,0:T(8,128)(2,1)} custom-call(f32[256,256]{1,0:T(8,128)S(1)} %get-tuple-element.14.part_ref, bf16[256,256]{1,0:T(8,128)(2,1)S(1)} %collective-permute-done.other_ref, bf16[256,3584]{1,0:T(8,128)(2,1)S(1)} %bitcast.9, f32[1,3584]{1,0:T(1,128)S(1)} %get-tuple-element.17.scale_ref, bf16[256,3584]{1,0:T(8,128)(2,1)S(1)} %get-tuple-element.18.kept_ref), custom_call_target="tpu_custom_call" | custom-call | tf_op jit(solution)/shard_map/update/pallas_call | solution.py:252
  (3 shorter events, 0.0 us)
Async XLA Ops:
  22.4 7.2 %copy-start.6 = (s32[256,112]{0,1:T(8,128)S(1)}, s32[256,112]{0,1:T(8,128)}, u32[]{:S(2)}) copy-start(s32[256,112]{0,1:T(8,128)} %param.8) | copy-start | bytes 344068
  22.4 34.1 %all-to-all-start = ((bf16[32,8,3584]{2,1,0:T(8,128)(2,1)}), bf16[32,8,3584]{2,1,0:T(8,128)(2,1)S(1)}, u32[]{:S(2)}, u32[]{:S(2)}) async-start(bf16[32,8,3584]{2,1,0:T(8,128)(2,1)} %bitcast.11), calls=%async_computation | async-start | bytes 3670016 | tf_op jit(solution)/shard_map/route/all_to_all | solution.py:215
  30.3 1.5 %copy-start = (bf16[1,256,3584]{2,1,0:T(8,128)(2,1)S(1)}, bf16[1,256,3584]{2,1,0:T(8,128)(2,1)}, u32[]{:S(2)}) copy-start(bf16[1,256,3584]{2,1,0:T(8,128)(2,1)} %param.7) | copy-start | bytes 5505028
  31.8 0.9 %copy-start.2 = (s32[256,112]{1,0:T(8,128)S(1)}, s32[256,112]{1,0:T(8,128)}, u32[]{:S(2)}) copy-start(s32[256,112]{1,0:T(8,128)} %copy.6.bits_ref) | copy-start | bytes 344068
  33.9 1.3 %copy-start.1 = (bf16[256,3584]{1,0:T(8,128)(2,1)}, bf16[256,3584]{1,0:T(8,128)(2,1)S(1)}, u32[]{:S(2)}) copy-start(bf16[256,3584]{1,0:T(8,128)(2,1)S(1)} %get-tuple-element.16.kept_hbm) | copy-start | bytes 5505028
  35.1 0.7 %copy-start.3 = (bf16[256,256]{1,0:T(8,128)(2,1)}, bf16[256,256]{1,0:T(8,128)(2,1)S(1)}, u32[]{:S(2)}) copy-start(bf16[256,256]{1,0:T(8,128)(2,1)S(1)} %get-tuple-element.12.rest_ref) | copy-start | bytes 393220
  56.6 0.9 %copy-start.4 = (bf16[256,256]{1,0:T(8,128)(2,1)S(1)}, bf16[256,256]{1,0:T(8,128)(2,1)}, u32[]{:S(2)}) copy-start(bf16[256,256]{1,0:T(8,128)(2,1)} %copy-done.3) | copy-start | bytes 393220
  57.2 1.9 %copy-start.5 = (f32[1,3584]{1,0:T(1,128)S(1)}, f32[1,3584]{1,0:T(1,128)}, u32[]{:S(2)}) copy-start(f32[1,3584]{1,0:T(1,128)} %damping_ref.1) | copy-start | bytes 43012
  57.7 5.3 %collective-permute-start = (bf16[256,256]{1,0:T(8,128)(2,1)S(1)}, bf16[256,256]{1,0:T(8,128)(2,1)S(1)}, u32[]{:S(2)}, u32[]{:S(2)}) collective-permute-start(bf16[256,256]{1,0:T(8,128)(2,1)S(1)} %get-tuple-element.15), channel_id=1, source_target_pairs={{0,1},{1,0},{2,3},{3,2},{4,5},{5,4},{6,7},{7,6},{8,9},{9,8},{10,11... | collective-permute-start | bytes 393224 | tf_op jit(solution)/shard_map/swap_features/ppermute | solution.py:172
